TPU v7x, 128 devices: a whole 4x4x4 slice. The times are simulated.
128 devices in a mesh: pipe: 2 (over core), dp: 16 (over y, x), tensor: 4 (over z).
Axes of the slice: x: 4, y: 4, z: 4, core: 2. Of those that a mesh axis runs over, the one named last changes fastest.
Arguments:
- saved_inputs: bfloat16 [2, 2, 2, 6144, 896], P('pipe', None, None, 'dp')
- early_cotangents: bfloat16 [2, 2, 6144, 896], P('pipe', None, 'dp'), may hold values from -30 to 30
- final_cotangent: bfloat16 [6144, 896], P('dp'), may hold values from -6 to 6
- valid_counts: int32 [16, 2], P('dp'), may hold values from 96 to 384, as said below
- master: float32 [2, 896, 2, 3, 2560], P('pipe', 'dp', None, None, 'tensor'), may hold values from -0.1875 to 0.1875
- first_moment: bfloat16 [2, 896, 2, 3, 2560], P('pipe', 'dp', None, None, 'tensor'), may hold values from -6 to 6
- second_moment: bfloat16 [2, 896, 2, 3, 2560], P('pipe', 'dp', None, None, 'tensor'), may hold values from 0.049804688 to 5
Outputs:
- new_master: float32 [2, 896, 2, 3, 2560], P('pipe', 'dp', None, None, 'tensor')
- new_first: bfloat16 [2, 896, 2, 3, 2560], P('pipe', 'dp', None, None, 'tensor')
- new_second: bfloat16 [2, 896, 2, 3, 2560], P('pipe', 'dp', None, None, 'tensor')
Inputs may be any that keep to these rules, and one draw needn't show every extreme that they name: `valid_counts`: every draw has an entry equal to 384.
All inputs are finite; a program needn't handle non-finite values.
Results may differ from a plain program's by a relative error of at most 0.025.
Values may be sent and summed in bfloat16 or wider, within the bound.
No kernel may reach another device: no remote copies, remote signals or barrier semaphores. Data moves between devices by JAX's collectives and lax.ppermute only.
A program may use at most 448 MiB of HBM per device.

v0:
```python
import functools
import math

import jax
import jax.numpy as jnp
from jax import lax
from jax.experimental import pallas as pl
from jax.experimental.pallas import tpu as pltpu
from jax.sharding import PartitionSpec as P

STEP = 20
SIDE = 4
F32 = jnp.float32
BF16 = jnp.bfloat16
ORDER = (1, 3, 2)
VMEM_LIMIT = 20 * 1024 * 1024


def peers(fetch):
    got = {by: fetch(by) for by in ORDER}
    return [got[by] for by in (1, 2, 3)]


def from_plane(value, by, first):
    pairs = []
    for core in range(2):
        for y in range(SIDE):
            for x in range(SIDE):
                if (core == 0) == first:
                    source = (y, (x + by) % SIDE)
                else:
                    source = ((y + by) % SIDE, x)
                base = core * SIDE * SIDE
                pairs.append((base + source[0] * SIDE + source[1], base + y * SIDE + x))
    return lax.ppermute(value, ("pipe", "dp"), pairs)


def from_z(value, by):
    pairs = [((z + by) % SIDE, z) for z in range(SIDE)]
    return lax.ppermute(value, "tensor", pairs)


def across(value, by, source):
    pairs = [(source * SIDE + (z + by) % SIDE, (1 - source) * SIDE + z) for z in range(SIDE)]
    pairs += [((1 - source) * SIDE + z, source * SIDE + z) for z in range(SIDE)]
    return lax.ppermute(value, ("pipe", "tensor"), pairs)


def from_other_core(value):
    return lax.ppermute(value, "pipe", [(0, 1), (1, 0)])


def total_of(parts):
    total = parts[0].astype(F32)
    for part in parts[1:]:
        total = total + part.astype(F32)
    return total


def run(kernel, ins, outs, scratch=(), flops=0, name=None):
    arrays, specs = [], []
    for item in ins:
        array, space = item if isinstance(item, tuple) else (item, pltpu.VMEM)
        arrays.append(array)
        specs.append(pl.BlockSpec(memory_space=space))
    moved = sum(a.size * a.dtype.itemsize for a in arrays)
    moved += sum(math.prod(o[0]) * jnp.dtype(o[1]).itemsize for o in outs)
    return pl.pallas_call(
        kernel,
        out_shape=[jax.ShapeDtypeStruct(o[0], o[1]) for o in outs],
        in_specs=specs,
        out_specs=[pl.BlockSpec(memory_space=o[2] if o[2:] else pltpu.VMEM) for o in outs],
        scratch_shapes=list(scratch),
        compiler_params=pltpu.CompilerParams(vmem_limit_bytes=VMEM_LIMIT),
        cost_estimate=pl.CostEstimate(flops=flops, bytes_accessed=moved, transcendentals=0),
        name=name,
    )(*arrays)


def after(value, *others):
    return lax.optimization_barrier((value, others))[0]


def normalized(inputs):
    values = inputs.astype(F32)
    root_mean = jnp.sqrt(jnp.mean(values * values, axis=-1, keepdims=True) + 1e-06)
    return values / root_mean, root_mean


def dot(left, right):
    return jnp.dot(left, right, preferred_element_type=F32)


def gate_parts(normed, weights, units):
    both = dot(normed, weights[:, : 2 * units])
    gate, up_rows = both[:, :units], both[:, units:]
    sigmoid_gate = jax.nn.sigmoid(gate)
    activated = gate * sigmoid_gate
    hidden = (activated * up_rows).astype(BF16)
    slope = up_rows * sigmoid_gate * (1.0 + gate * (1.0 - sigmoid_gate))
    return hidden, slope, activated


def both_grads(cotangent, slope, activated, weights, units):
    hidden_grad = dot(cotangent, weights[:, 2 * units :])
    return jnp.concatenate(
        [(hidden_grad * slope).astype(BF16), (hidden_grad * activated).astype(BF16)], 1
    )


def store_branch(grads, inputs, weights, units, outs):
    branch = lax.dot_general(
        grads, weights[:, : 2 * units], (((1,), (1,)), ((), ())), preferred_element_type=F32
    )
    unit_rows, root_mean = normalized(inputs)
    centered = branch - unit_rows * jnp.mean(branch * unit_rows, axis=-1, keepdims=True)
    rows = (centered / root_mean).astype(BF16)
    group = rows.shape[0] // SIDE
    for i, out in enumerate(outs):
        out[...] = rows[i * group : (i + 1) * group]


def started(copies):
    for copy in copies:
        copy.start()
    return copies


def waited(copies):
    for copy in copies:
        copy.wait()


def weight_copies(pieces, weights, sems):
    rows, columns = pieces[0].shape[0], weights.shape[1]
    first = pieces[0].shape[1] - columns
    return started(
        [
            pltpu.make_async_copy(
                piece.at[:, pl.ds(first, columns)], weights.at[pl.ds(i * rows, rows)], sems.at[i]
            )
            for i, piece in enumerate(pieces)
        ]
    )


def order_kernel(mover, whole, out, matrix, weights, sems):
    rows, columns = out.shape[0] // SIDE, out.shape[1] // 3
    copies = [pltpu.make_async_copy(mover, matrix, sems.at[0])]
    for i in range(3):
        part = pl.ds(i * columns, columns)
        copies.append(
            pltpu.make_async_copy(whole.at[:, part], weights.at[:, part], sems.at[i + 1])
        )
    started(copies)
    copies[0].wait()
    for i in range(3):
        copies[i + 1].wait()
        part = slice(i * columns, (i + 1) * columns)
        out[:, part] = dot(matrix[...], weights[:, part]).astype(BF16)


def gate_kernel(units, x, weights, *outs):
    normed = normalized(x[...])[0].astype(BF16)
    outs[0][...] = normed.T
    outs[1][...], outs[2][...], outs[3][...] = gate_parts(normed, weights, units)


def first_kernel(units, x, d, *refs):
    pieces, halves, outs = refs[:4], refs[4:8], refs[8:12]
    weights, sems, stages, out_sems = refs[12], refs[13], refs[14:18], refs[18]
    copies = weight_copies(pieces, weights, sems)
    sends = [
        pltpu.make_async_copy(stage, half, out_sems.at[i])
        for i, (stage, half) in enumerate(zip(stages, halves))
    ]
    normed = normalized(x[...])[0].astype(BF16)
    stages[0][...] = normed.T
    sends[0].start()
    waited(copies)
    hidden, slope, activated = gate_parts(normed, weights, units)
    stages[1][...], stages[2][...], stages[3][...] = hidden, slope, activated
    started(sends[1:])
    grads = both_grads(d[...], slope, activated, weights, units)
    store_branch(grads, x[...], weights, units, outs)
    waited(sends)


def chain_kernel(units, active, x, slope, activated, weights, *refs):
    groups, outs = refs[:4], refs[4:]

    @pl.when(active[0] != 0)
    def _():
        cotangent = jnp.concatenate([g[...] for g in groups], 0)
        grads = both_grads(cotangent, slope[...], activated[...], weights, units)
        store_branch(grads, x[...], weights, units, outs)

    @pl.when(active[0] == 0)
    def _():
        for out in outs:
            out[...] = jnp.zeros(out.shape, out.dtype)


def far_chain_kernel(units, active, x, slope, activated, *refs):
    pieces, groups, outs = refs[:4], refs[4:8], refs[8:12]
    weights, sems, slope_here, activated_here = refs[12:]

    @pl.when(active[0] != 0)
    def _():
        copies = weight_copies(pieces, weights, sems)
        copies += started(
            [
                pltpu.make_async_copy(slope, slope_here, sems.at[4]),
                pltpu.make_async_copy(activated, activated_here, sems.at[5]),
            ]
        )
        cotangent = jnp.concatenate([g[...] for g in groups], 0)
        waited(copies)
        grads = both_grads(cotangent, slope_here[...], activated_here[...], weights, units)
        store_branch(grads, x[...], weights, units, outs)

    @pl.when(active[0] == 0)
    def _():
        for out in outs:
            out[...] = jnp.zeros(out.shape, out.dtype)


def early_kernel(units, x, d, *refs):
    if len(refs) > 5:
        pieces, outs, weights, sems = refs[:4], refs[4:8], refs[8], refs[9]
        copies = weight_copies(pieces, weights, sems)
    else:
        weights, outs, copies = refs[0], refs[1:], []
    normed = normalized(x[...])[0].astype(BF16)
    outs[0][...] = normed.T
    outs[1][...] = d[...].T
    waited(copies)
    hidden, slope, activated = gate_parts(normed, weights, units)
    outs[2][...] = hidden
    outs[3][...] = both_grads(d[...], slope, activated, weights, units)


def terms_kernel(units, use_first, *refs):
    first, second = refs[:4], refs[4:8]
    normed_early, cot_early, hidden_early, grads_early = refs[8:12]
    normed_last, hidden_last, slope, activated = refs[12:16]
    lefts, grads, hiddens = refs[-3:]
    if len(refs) > 24:
        pieces, outs, weights, sems = refs[16:20], refs[20:24], refs[24], refs[25]
        copies = weight_copies(pieces, weights, sems)
    else:
        weights, outs, copies = refs[16], refs[17:21], []
    down = slice(weights.shape[1] - units, weights.shape[1])
    tokens = normed_early.shape[1]
    cotangent = jnp.concatenate(
        [jnp.where(use_first[0] != 0, a[...], b[...]) for a, b in zip(first, second)], 0
    )
    lefts[0, :, :tokens] = normed_early[...]
    lefts[0, :, tokens:] = normed_last[...]
    lefts[1, :, :tokens] = cot_early[...]
    lefts[1, :, tokens:] = cotangent.T
    grads[:tokens] = grads_early[...]
    hiddens[:tokens] = hidden_early[...]
    hiddens[tokens:] = hidden_last[...]
    waited(copies)
    hidden_grad = dot(cotangent, weights[:, down])
    grads[tokens:, :units] = (hidden_grad * slope[...]).astype(BF16)
    grads[tokens:, units:] = (hidden_grad * activated[...]).astype(BF16)
    for i, out in enumerate(outs):
        rows = slice(i * out.shape[0], (i + 1) * out.shape[0])
        out[:, : 2 * units] = dot(lefts[0, rows], grads[...]).astype(BF16)
        out[:, 2 * units :] = dot(lefts[1, rows], hiddens[...]).astype(BF16)


def mix_kernel(crossing, d, *refs):
    total = d[...].astype(F32) + total_of([r[...] for r in refs[:4]])
    rows = total.astype(BF16)
    if crossing:
        rows = dot(rows, refs[4][...]).astype(BF16)
    refs[-1][...] = rows


def add_kernel(*refs):
    total = total_of([r[...] for r in refs[:4]])
    outs = refs[4:]
    rows = total.shape[0] // len(outs)
    for i, out in enumerate(outs):
        out[...] = total[i * rows : (i + 1) * rows].astype(out.dtype)


def finish_kernel(*refs):
    total = total_of([r[...] for r in refs[:4]])
    refs[4][...] = total
    squares = jnp.sum(total * total, axis=0, keepdims=True)
    refs[5][...] = jnp.broadcast_to(jnp.sum(squares, axis=1, keepdims=True), refs[5].shape)


def near_pieces(pieces):
    return {by: from_plane(pieces[by], -by, False) for by in (1, 3)}


def far_piece(piece):
    return {2: from_plane(piece, -2, False)}


def add_pieces(own, got):
    share, wide = own.shape[0] // SIDE, own.shape[1]
    outs = [((share, wide), F32)] + [((share, wide), BF16)] * 3
    return run(add_kernel, [own, got[1], got[2], got[3]], outs, name="add")


def own_rows(sums):
    parts = [sums[0]] + peers(lambda by: from_plane(sums[by], -by, True))
    return run(finish_kernel, parts, [(sums[0].shape, F32), ((8, 128), F32)], name="finish")


def reduced_group(first_group, got, matrix):
    return run(
        functools.partial(mix_kernel, matrix is not None),
        [first_group] + got + ([] if matrix is None else [matrix]),
        [(first_group.shape, BF16)],
        name="mix",
    )[0]


def scattered(parts):
    return [parts[0]] + peers(lambda by: from_z(parts[by], -by))


def shared_groups(mine):
    return [mine] + peers(lambda by: from_z(mine, by))


def summed_everywhere(value):
    value = value + from_other_core(value)
    value = total_of([value] + peers(lambda by: from_plane(value, by, True)))
    value = total_of([value] + peers(lambda by: from_plane(value, by, False)))
    return total_of([value] + peers(lambda by: from_z(value, by)))[0, 0]


def per_device(
    saved_inputs,
    early_cotangents,
    final_cotangent,
    valid_counts,
    master,
    first_moment,
    second_moment,
):
    tokens, width = saved_inputs.shape[3:]
    units = master.shape[4]
    share = width // lax.axis_size("dp")
    section = lax.axis_index("pipe")
    place = lax.axis_index("dp")
    place_y, place_x = place // SIDE, place % SIDE
    place_z = lax.axis_index("tensor")
    group = tokens // SIDE
    wide = 3 * units
    on_first = (section == 0).astype(jnp.int32).reshape(1)
    on_second = 1 - on_first

    def as_stored(array):
        return array[0].transpose(0, 2, 1, 3)

    masters = as_stored(master)

    def shard_of(leg):
        return masters[:, :, leg, :].astype(BF16).reshape(share, wide)

    shard = shard_of(1)
    block = jnp.concatenate([shard] + peers(lambda by: from_plane(shard, by, True)), 0)
    lower_whole = lax.all_gather(shard_of(0), "dp", axis=0, tiled=True)
    upper = [block] + peers(lambda by: from_plane(block, by, False))
    saved_inputs, early_cotangents, final_cotangent = after(
        (saved_inputs, early_cotangents, final_cotangent), block
    )

    block = jnp.arange(width) // share
    outer, inner = block // SIDE, block % SIDE
    by_y = jnp.where(section == 0, outer, inner)
    by_x = jnp.where(section == 0, inner, outer)
    source_block = ((place_y + by_y) % SIDE) * SIDE + (place_x + by_x) % SIDE
    source_column = source_block * share + jnp.arange(width) % share
    mover = (jnp.arange(width)[:, None] == source_column[None, :]).astype(BF16)
    swapped_column = (inner * SIDE + outer) * share + jnp.arange(width) % share
    swap = (jnp.arange(width)[:, None] == swapped_column[None, :]).astype(BF16)
    turns = [(place_z + j) % SIDE for j in range(SIDE)]

    def turned(rows):
        return jnp.concatenate(
            [lax.dynamic_slice_in_dim(rows, turn * group, group, rows.ndim - 2) for turn in turns],
            rows.ndim - 2,
        )

    def moved(rows):
        return jnp.dot(turned(rows), mover, preferred_element_type=F32).astype(BF16)

    inputs = moved(saved_inputs[0])
    position = turned(lax.broadcasted_iota(jnp.int32, (tokens, 1), 0))
    early = jnp.where(position < valid_counts[0, 0], moved(early_cotangents[0]), 0)
    final = jnp.where(position < valid_counts[0, 1], moved(final_cotangent), 0)
    final_groups = [final[i * group : (i + 1) * group] for i in range(SIDE)]

    flop = 2 * tokens * width * units
    whole = [((width, wide), BF16)]
    half_outs = [
        ((width, tokens), BF16),
        ((tokens, units), BF16),
        ((tokens, units), F32),
        ((tokens, units), F32),
    ]
    group_outs = [((group, width), BF16)] * SIDE

    def far(arrays):
        return [(array, pltpu.HBM) for array in arrays]

    def fetched(columns):
        return [pltpu.VMEM((width, columns), BF16), pltpu.SemaphoreType.DMA((6,))]

    def early_parts(leg, leg_inputs, weights):
        one = len(weights) == 1
        return run(
            functools.partial(early_kernel, units),
            [leg_inputs, early[leg], *(weights if one else far(weights))],
            [
                ((width, tokens), BF16),
                ((width, tokens), BF16),
                ((tokens, units), BF16),
                ((tokens, 2 * units), BF16),
            ],
            [] if one else fetched(wide),
            5 * flop,
            "early",
        )

    def terms(use_first, first, second, early_half, half, weights):
        one = len(weights) == 1
        return run(
            functools.partial(terms_kernel, units),
            [
                (use_first, pltpu.SMEM),
                *first,
                *second,
                *early_half,
                *half,
                *(weights if one else far(weights)),
            ],
            [((width // SIDE, wide), BF16)] * SIDE,
            ([] if one else fetched(units))
            + [
                pltpu.VMEM((2, width, 2 * tokens), BF16),
                pltpu.VMEM((2 * tokens, 2 * units), BF16),
                pltpu.VMEM((2 * tokens, units), BF16),
            ],
            7 * flop,
            "terms",
        )

    upper = after(upper, (inputs, early, final, mover))
    outs = run(
        functools.partial(first_kernel, units),
        [inputs[1, 1], final, *far(upper)],
        [(*out, pltpu.HBM) for out in half_outs] + group_outs,
        fetched(wide)
        + [pltpu.VMEM(*out) for out in half_outs]
        + [pltpu.SemaphoreType.DMA((SIDE,))],
        5 * flop,
        "first",
    )
    upper_half, part3 = outs[:4], outs[4:]
    got = scattered(part3)
    early_one = early_parts(1, after(inputs[1, 0], part3[0]), upper)
    mine2 = reduced_group(after(final_groups[0], early_one), got, swap)
    cot2 = [across(mine2, by, 0) for by in range(SIDE)]
    part2 = run(
        functools.partial(far_chain_kernel, units),
        [
            (on_second, pltpu.SMEM),
            inputs[1, 1],
            *far(upper_half[2:]),
            *far(upper),
            *cot2,
        ],
        group_outs,
        fetched(wide) + [pltpu.VMEM(*out) for out in half_outs[2:]],
        3 * flop,
        "chain",
    )

    got = [across(part2[by], -by, 1) for by in range(SIDE)]
    lower_whole = after(lower_whole, part2[0])
    (lower_weights,) = run(
        order_kernel,
        far([mover.T, lower_whole]),
        whole,
        [pltpu.VMEM((width, width), BF16), *fetched(wide)],
        2 * width * width * wide,
        "order",
    )
    mine1 = reduced_group(after(mine2, lower_weights), got, None)
    cot1 = [across(mine1, by, 0) for by in range(SIDE)]
    lower_half = run(
        functools.partial(gate_kernel, units),
        [after(inputs[0, 1], mine1), lower_weights],
        half_outs,
        flops=2 * flop,
        name="gate",
    )
    part1 = run(
        functools.partial(chain_kernel, units),
        [
            (on_second, pltpu.SMEM),
            inputs[0, 1],
            lower_half[2],
            lower_half[3],
            lower_weights,
            *cot1,
        ],
        group_outs,
        flops=3 * flop,
        name="chain",
    )
    got = [across(part1[by], -by, 1) for by in range(SIDE)]
    early_one = after(early_one, part1[0])
    upper_terms = terms(on_first, final_groups, cot2, early_one, upper_half, upper)
    mine0 = reduced_group(after(mine1, upper_terms[0]), got, swap)
    cot0 = shared_groups(mine0)
    upper_got = near_pieces(after(upper_terms, mine0))
    early_zero = early_parts(0, after(inputs[0, 0], mine0), [lower_weights])
    upper_got |= far_piece(after(upper_terms[2], cot0))
    lower_terms = terms(on_second, cot1, cot0, early_zero, lower_half, [lower_weights])

    lower_got = near_pieces(lower_terms) | far_piece(lower_terms[2])
    upper_sums = add_pieces(after(upper_terms[0], lower_terms[0]), upper_got)
    upper_gradient, upper_squares = own_rows(upper_sums)
    lower_gradient, lower_squares = own_rows(add_pieces(lower_terms[0], lower_got))
    gradient = jnp.stack(
        [rows.reshape(share, 3, units) for rows in (lower_gradient, upper_gradient)], 2
    )

    total = summed_everywhere(lower_squares + upper_squares)
    param_count = lax.axis_size("pipe") * 6 * width * units * lax.axis_size("tensor")
    clip_factor = jnp.minimum(1.0, math.sqrt(param_count) / (jnp.sqrt(total) + 1e-06))
    scaled = gradient * clip_factor
    moment_one = 0.9 * as_stored(first_moment).astype(F32) + 0.1 * scaled
    moment_two = 0.95 * as_stored(second_moment).astype(F32) + 0.05 * scaled * scaled
    update = (
        moment_one / (1.0 - 0.9**STEP) / (jnp.sqrt(moment_two / (1.0 - 0.95**STEP)) + 1e-08)
        + 0.1 * masters
    )
    results = (masters - 0.001 * update, moment_one.astype(BF16), moment_two.astype(BF16))
    return tuple(result.transpose(0, 2, 1, 3)[None] for result in results)


def solution(mesh):
    in_specs = (
        P("pipe", None, None, "dp", None),
        P("pipe", None, "dp", None),
        P("dp", None),
        P("dp", None),
        P("pipe", "dp", None, None, "tensor"),
        P("pipe", "dp", None, None, "tensor"),
        P("pipe", "dp", None, None, "tensor"),
    )
    out_specs = (
        P("pipe", "dp", None, None, "tensor"),
        P("pipe", "dp", None, None, "tensor"),
        P("pipe", "dp", None, None, "tensor"),
    )
    return jax.shard_map(
        per_device, mesh=mesh, in_specs=in_specs, out_specs=out_specs, check_vma=False
    )
```

profile of v0, /device:TPU:0, one launch (start us, length us, event | category | flops | bytes accessed | tf_op | source)
XLA Modules:
  0.0 212.9 jit_solution(6809043254669051677)
XLA Ops:
  7.2 1.2 copy.43
  9.5 1.6 collective-permute-start.2
  11.1 2.7 %collective-permute-start.1 = (bf16[56,1920]{1,0:T(8,128)(2,1)S(1)}, bf16[56,1920]{1,0:T(8,128)(2,1)}, u32[]{:S(2)}, u32[]{:S(2)}) collective-permute-start(bf16[56,1920]{1,0:T(8,128)(2,1)S(1)} %bitcast.110), channel_id=1, source_target_pairs={{8,0},{12,4},{0,8},{4,12},{24,16},{28,20},{16,24},{20,28},{40,32},... | collective-permute-start | bytes 645128 | tf_op jit(solution)/shard_map/ppermute | solution.py:35
  13.9 1.4 collective-permute-start
  15.9 1.4 broadcast_compare_fusion
  18.0 2.0 collective-permute-done
  22.8 1.7 collective-permute-start.5
  24.6 2.9 %collective-permute-start.4 = (bf16[224,1920]{1,0:T(8,128)(2,1)S(1)}, bf16[224,1920]{1,0:T(8,128)(2,1)S(1)}, u32[]{:S(2)}, u32[]{:S(2)}) collective-permute-start(bf16[224,1920]{1,0:T(8,128)(2,1)S(1)} %constant_dynamic-update-slice_fusion.refs_0_.refs_16_), channel_id=1, source_target_pairs={{32,0},{36,4},{40,8},{44,12},{48,16},{52,20},{56,24},{60,28},{0,32... | collective-permute-start | bytes 2580488 | tf_op jit(solution)/shard_map/ppermute | solution.py:35
  27.5 1.9 collective-permute-start.3
  29.4 1.4 dynamic-slice_bitcast_fusion.7
  32.9 1.8 broadcast_select_fusion
  35.7 4.9 %fusion.16 = bf16[2,2,384,896]{3,2,1,0:T(8,128)(2,1)S(1)} fusion(bf16[2,2,96,896]{3,2,1,0:T(8,128)(2,1)S(1)} %get-tuple-element.154, bf16[2,2,96,896]{3,2,1,0:T(8,128)(2,1)S(1)} %get-tuple-element.155, bf16[2,2,96,896]{3,2,1,0:T(8,128)(2,1)S(1)} %get-tuple-element.156, bf16[2,2,96,896]{3,2,1,0:T(8,128)(2,1)S(1)} %get-tuple-element.153, s32[896]{0:T(1024)S(1)} %fusion.61), kind=kOutput, calls=%fused_computation.17 | convolution fusion | flops 2479439872 | bytes 5508608 | tf_op jit(solution)/shard_map/dot_general | solution.py:396
  41.7 8.0 %collective-permute-done.4.refs_2_.refs_18_ = bf16[224,1920]{1,0:T(8,128)(2,1)S(1)} collective-permute-done((bf16[224,1920]{1,0:T(8,128)(2,1)S(1)}, bf16[224,1920]{1,0:T(8,128)(2,1)S(1)}, u32[]{:S(2)}, u32[]{:S(2)}) %collective-permute-start.4) | collective-permute-done | bytes 860192 | tf_op jit(solution)/shard_map/ppermute | solution.py:35
  49.7 6.0 %first.1 = (bf16[896,384]{1,0:T(8,128)(2,1)S(1)}, bf16[384,640]{1,0:T(8,128)(2,1)S(1)}, f32[384,640]{1,0:T(8,128)S(1)}, f32[384,640]{1,0:T(8,128)S(1)}, bf16[96,...) custom-call(bf16[384,896]{1,0:T(8,128)(2,1)S(1)} %get-tuple-element., ...), custom_call_target="tpu_custom_call" | custom-call | flops 2202009600 | bytes 8650752 | tf_op jit(solution)/shard_map/first/pallas_call | solution.py:68
  57.4 1.9 collective-permute-start.6
  59.4 3.6 %collective-permute-start.7 = (bf16[96,896]{1,0:T(8,128)(2,1)S(1)}, bf16[96,896]{1,0:T(8,128)(2,1)S(1)}, u32[]{:S(2)}, u32[]{:S(2)}) collective-permute-start(bf16[96,896]{1,0:T(8,128)(2,1)S(1)} %get-tuple-element.88), channel_id=1, source_target_pairs={{2,0},{3,1},{0,2},{1,3},{6,4},{7,5},{4,6},{5,7},{10,8},{11,9},{8,1... | collective-permute-start | bytes 516104 | tf_op jit(solution)/shard_map/ppermute | solution.py:40
  62.9 1.2 collective-permute-start.8
  64.1 3.2 %early.2 = (bf16[896,384]{1,0:T(8,128)(2,1)S(1)}, bf16[896,384]{1,0:T(8,128)(2,1)S(1)}, bf16[384,640]{1,0:T(8,128)(2,1)S(1)}, bf16[384,1280]{1,0:T(8,128)(2,1)S(1)}) custom-call(bf16[384,896]{1,0:T(8,128)(2,1)S(1)} %get-tuple-element.81.x, bf16[384,896]{1,0:T(8,128)(2,1)S(1)} %get-tuple-element.158.d, ...), custom_call_target="tpu_custom_call" | custom-call | flops 2202009600 | bytes 7667712 | tf_op jit(solution)/shard_map/early/pallas_call | solution.py:68
  68.2 1.2 collective-permute-done.7.refs_2_
  70.0 2.5 %collective-permute-start.11 = (bf16[96,896]{1,0:T(8,128)(2,1)S(1)}, bf16[96,896]{1,0:T(8,128)(2,1)S(1)}, u32[]{:S(2)}, u32[]{:S(2)}) collective-permute-start(bf16[96,896]{1,0:T(8,128)(2,1)S(1)} %mix.3.d), channel_id=1, source_target_pairs={{2,64},{3,65},{0,66},{1,67},{64,0},{65,1},{66,2},{67,3},{6,68},{7,... | collective-permute-start | bytes 516104 | tf_op jit(solution)/shard_map/ppermute | solution.py:46
  73.0 1.6 fusion.8.mover
  75.4 1.8 collective-permute-done.10.refs_5_
  78.4 4.1 %collective-permute-start.14 = (bf16[96,896]{1,0:T(8,128)(2,1)}, bf16[96,896]{1,0:T(8,128)(2,1)}, u32[]{:S(2)}, u32[]{:S(2)}) collective-permute-start(bf16[96,896]{1,0:T(8,128)(2,1)} %get-tuple-element.95), channel_id=1, source_target_pairs={{67,0},{64,1},{65,2},{66,3},{0,64},{1,65},{2,66},{3,67},{71,4},{68... | collective-permute-start | bytes 516104 | tf_op jit(solution)/shard_map/ppermute | solution.py:46
  82.6 2.3 %collective-permute-start.16 = (bf16[96,896]{1,0:T(8,128)(2,1)}, bf16[96,896]{1,0:T(8,128)(2,1)}, u32[]{:S(2)}, u32[]{:S(2)}) collective-permute-start(bf16[96,896]{1,0:T(8,128)(2,1)} %get-tuple-element.97), channel_id=1, source_target_pairs={{65,0},{66,1},{67,2},{64,3},{0,64},{1,65},{2,66},{3,67},{69,4},{70... | collective-permute-start | bytes 516104 | tf_op jit(solution)/shard_map/ppermute | solution.py:46
  85.3 1.4 copy-done
  86.7 2.0 copy-done.24
  88.7 5.7 %order.1.weights.refs_0_.refs_16_ = bf16[896,1920]{1,0:T(8,128)(2,1)S(1)} custom-call(bf16[896,896]{1,0:T(8,128)(2,1)S(1)} %copy-done, bf16[896,1920]{1,0:T(8,128)(2,1)S(1)} %copy-done.24), custom_call_target="tpu_custom_call" | custom-call | flops 3082813440 | bytes 8486912 | tf_op jit(solution)/shard_map/order/pallas_call | solution.py:68
  94.4 1.3 mix.4.d
  96.9 2.0 collective-permute-start.18
  99.1 1.4 gate.1
  102.0 4.1 %collective-permute-start.21 = (bf16[96,896]{1,0:T(8,128)(2,1)S(1)}, bf16[96,896]{1,0:T(8,128)(2,1)S(1)}, u32[]{:S(2)}, u32[]{:S(2)}) collective-permute-start(bf16[96,896]{1,0:T(8,128)(2,1)S(1)} %get-tuple-element.101), channel_id=1, source_target_pairs={{64,0},{65,1},{66,2},{67,3},{0,64},{1,65},{2,66},{3,67},{68,4},{69... | collective-permute-start | bytes 516104 | tf_op jit(solution)/shard_map/ppermute | solution.py:46
  106.8 1.6 collective-permute-start.24
  108.5 4.4 %terms.2 = (bf16[224,1920]{1,0:T(8,128)(2,1)S(1)}, bf16[224,1920]{1,0:T(8,128)(2,1)S(1)}, bf16[224,1920]{1,0:T(8,128)(2,1)S(1)}, bf16[224,1920]{1,0:T(8,128)(2,1)S(1)}) custom-call(s32[1]{0:T(128)} %bitcast.4.use_first, bf16[96,896]{1,0:T(8,128)(2,1)S(1)} %get-tuple-element.86.d.refs_0_, bf16[96,896]{1,0:T(8,128)(2,1)S(1)} %copy-done.23, ...), custom_call_target="tpu_custom_call" | custom-call | flops 3082813440 | bytes 14254084 | tf_op jit(solution)/shard_map/terms/pallas_call | solution.py:68
  114.3 1.4 collective-permute-start.34
  116.6 2.3 %collective-permute-start.26 = (bf16[96,896]{1,0:T(8,128)(2,1)S(1)}, bf16[96,896]{1,0:T(8,128)(2,1)S(1)}, u32[]{:S(2)}, u32[]{:S(2)}) collective-permute-start(bf16[96,896]{1,0:T(8,128)(2,1)S(1)} %mix.5.refs_4_), channel_id=1, source_target_pairs={{2,0},{3,1},{0,2},{1,3},{6,4},{7,5},{4,6},{5,7},{10,8},{11,9},{8,1... | collective-permute-start | bytes 516104 | tf_op jit(solution)/shard_map/ppermute | solution.py:40
  119.9 2.0 collective-permute-start.36
  121.8 2.0 early.3
  123.9 2.7 %collective-permute-done.27.refs_7_ = bf16[96,896]{1,0:T(8,128)(2,1)S(1)} collective-permute-done((bf16[96,896]{1,0:T(8,128)(2,1)S(1)}, bf16[96,896]{1,0:T(8,128)(2,1)S(1)}, u32[]{:S(2)}, u32[]{:S(2)}) %collective-permute-start.27) | collective-permute-done | bytes 172064 | tf_op jit(solution)/shard_map/ppermute | solution.py:40
  127.2 3.5 %collective-permute-start.35 = (bf16[224,1920]{1,0:T(8,128)(2,1)S(1)}, bf16[224,1920]{1,0:T(8,128)(2,1)S(1)}, u32[]{:S(2)}, u32[]{:S(2)}) collective-permute-start(bf16[224,1920]{1,0:T(8,128)(2,1)S(1)} %get-tuple-element.134), channel_id=1, source_target_pairs={{32,0},{36,4},{40,8},{44,12},{48,16},{52,20},{56,24},{60,28},{0,32... | collective-permute-start | bytes 2580488 | tf_op jit(solution)/shard_map/ppermute | solution.py:35
  130.7 3.8 %terms.3 = (bf16[224,1920]{1,0:T(8,128)(2,1)S(1)}, bf16[224,1920]{1,0:T(8,128)(2,1)S(1)}, bf16[224,1920]{1,0:T(8,128)(2,1)S(1)}, bf16[224,1920]{1,0:T(8,128)(2,1)S(1)}) custom-call(s32[1]{0:T(128)S(6)} %sub.36.active.use_first, bf16[96,896]{1,0:T(8,128)(2,1)S(1)} %collective-permute-done.17.refs_0_, bf16[96,896]{1,0:T(8,128)(2,1)S(1)} %collective-permute-done.18.refs_1_, ...), custom_call_target="tpu_custom_call" | custom-call | flops 3082813440 | bytes 14254084 | tf_op jit(solution)/shard_map/terms/pallas_call | solution.py:68
  135.0 2.3 %collective-permute-start.29 = (bf16[224,1920]{1,0:T(8,128)(2,1)S(1)}, bf16[224,1920]{1,0:T(8,128)(2,1)S(1)}, u32[]{:S(2)}, u32[]{:S(2)}) collective-permute-start(bf16[224,1920]{1,0:T(8,128)(2,1)S(1)} %get-tuple-element.122), channel_id=1, source_target_pairs={{32,0},{36,4},{40,8},{44,12},{48,16},{52,20},{56,24},{60,28},{0,32... | collective-permute-start | bytes 2580488 | tf_op jit(solution)/shard_map/ppermute | solution.py:35
  137.8 12.8 %collective-permute-done.36.refs_3_ = bf16[224,1920]{1,0:T(8,128)(2,1)S(1)} collective-permute-done((bf16[224,1920]{1,0:T(8,128)(2,1)S(1)}, bf16[224,1920]{1,0:T(8,128)(2,1)S(1)}, u32[]{:S(2)}, u32[]{:S(2)}) %collective-permute-start.36) | collective-permute-done | bytes 860192 | tf_op jit(solution)/shard_map/ppermute | solution.py:35
  151.2 3.1 %collective-permute-start.39 = (bf16[56,1920]{1,0:T(8,128)(2,1)S(1)}, bf16[56,1920]{1,0:T(8,128)(2,1)S(1)}, u32[]{:S(2)}, u32[]{:S(2)}) collective-permute-start(bf16[56,1920]{1,0:T(8,128)(2,1)S(1)} %get-tuple-element.139), channel_id=1, source_target_pairs={{4,0},{8,4},{12,8},{0,12},{20,16},{24,20},{28,24},{16,28},{36,32},... | collective-permute-start | bytes 645128 | tf_op jit(solution)/shard_map/ppermute | solution.py:35
  154.3 10.7 %collective-permute-done.29.refs_2_ = bf16[224,1920]{1,0:T(8,128)(2,1)S(1)} collective-permute-done((bf16[224,1920]{1,0:T(8,128)(2,1)S(1)}, bf16[224,1920]{1,0:T(8,128)(2,1)S(1)}, u32[]{:S(2)}, u32[]{:S(2)}) %collective-permute-start.29) | collective-permute-done | bytes 860192 | tf_op jit(solution)/shard_map/ppermute | solution.py:35
  165.5 1.4 collective-permute-start.31
  166.9 2.2 %collective-permute-start.32 = (bf16[56,1920]{1,0:T(8,128)(2,1)S(1)}, bf16[56,1920]{1,0:T(8,128)(2,1)S(1)}, u32[]{:S(2)}, u32[]{:S(2)}) collective-permute-start(bf16[56,1920]{1,0:T(8,128)(2,1)S(1)} %get-tuple-element.126), channel_id=1, source_target_pairs={{8,0},{12,4},{0,8},{4,12},{24,16},{28,20},{16,24},{20,28},{40,32},... | collective-permute-start | bytes 645128 | tf_op jit(solution)/shard_map/ppermute | solution.py:35
  170.4 2.3 %collective-permute-done.31.refs_1_ = bf16[56,1920]{1,0:T(8,128)(2,1)S(1)} collective-permute-done((bf16[56,1920]{1,0:T(8,128)(2,1)S(1)}, bf16[56,1920]{1,0:T(8,128)(2,1)S(1)}, u32[]{:S(2)}, u32[]{:S(2)}) %collective-permute-start.31) | collective-permute-done | bytes 215072 | tf_op jit(solution)/shard_map/ppermute | solution.py:35
  172.6 2.6 %collective-permute-done.32.refs_2_ = bf16[56,1920]{1,0:T(8,128)(2,1)S(1)} collective-permute-done((bf16[56,1920]{1,0:T(8,128)(2,1)S(1)}, bf16[56,1920]{1,0:T(8,128)(2,1)S(1)}, u32[]{:S(2)}, u32[]{:S(2)}) %collective-permute-start.32) | collective-permute-done | bytes 215072 | tf_op jit(solution)/shard_map/ppermute | solution.py:35
  176.1 1.2 collective-permute-done.40
  177.3 1.3 collective-permute-start.43
  178.5 2.9 %collective-permute-start.42 = (f32[8,128]{1,0:T(8,128)S(1)}, f32[8,128]{1,0:T(8,128)S(1)}, u32[]{:S(2)}, u32[]{:S(2)}) collective-permute-start(f32[8,128]{1,0:T(8,128)S(1)} %add.249), channel_id=1, source_target_pairs={{8,0},{12,4},{0,8},{4,12},{24,16},{28,20},{16,24},{20,28},{40,32},... | collective-permute-start | bytes 12296 | tf_op jit(solution)/shard_map/ppermute | solution.py:35
  182.1 1.6 collective-permute-done.42
  183.7 1.4 collective-permute-done.41
  185.0 1.9 collective-permute-start.46
  186.9 2.6 %collective-permute-start.45 = (f32[8,128]{1,0:T(8,128)S(1)}, f32[8,128]{1,0:T(8,128)S(1)}, u32[]{:S(2)}, u32[]{:S(2)}) collective-permute-start(f32[8,128]{1,0:T(8,128)S(1)} %add_add_fusion.2), channel_id=1, source_target_pairs={{32,0},{36,4},{40,8},{44,12},{48,16},{52,20},{56,24},{60,28},{0,32... | collective-permute-start | bytes 12296 | tf_op jit(solution)/shard_map/ppermute | solution.py:35
  189.5 1.1 collective-permute-start.44
  190.6 1.4 collective-permute-done.45
  192.0 1.1 collective-permute-done.44
  193.1 1.1 collective-permute-start.49
  194.2 2.3 %collective-permute-start.48 = (f32[8,128]{1,0:T(8,128)S(1)}, f32[8,128]{1,0:T(8,128)S(1)}, u32[]{:S(2)}, u32[]{:S(2)}) collective-permute-start(f32[8,128]{1,0:T(8,128)S(1)} %add_add_fusion.1), channel_id=1, source_target_pairs={{2,0},{3,1},{0,2},{1,3},{6,4},{7,5},{4,6},{5,7},{10,8},{11,9},{8,1... | collective-permute-start | bytes 12296 | tf_op jit(solution)/shard_map/ppermute | solution.py:40
  196.5 1.4 collective-permute-start.47
  202.4 1.1 copy.27
  203.4 1.1 copy.26
  204.5 1.3 copy.25
  (182 shorter events, 31.3 us)
Async XLA Ops:
  7.2 78.1 %all-gather.2.cloned.1.call-start = ((), (), s32[]{:S(2)}) async-start(), calls=%async_computation | async-start | bytes 3655680 | tf_op jit(solution)/shard_map/all_gather | solution.py:372
  8.6 20.7 %copy-start.39 = (bf16[384,896]{1,0:T(8,128)(2,1)S(1)}, bf16[384,896]{1,0:T(8,128)(2,1)}, u32[]{:S(2)}) copy-start(bf16[384,896]{1,0:T(8,128)(2,1)} %param.9) | copy-start | bytes 2064388
  9.5 12.3 %collective-permute-start.2 = (bf16[56,1920]{1,0:T(8,128)(2,1)S(1)}, bf16[56,1920]{1,0:T(8,128)(2,1)}, u32[]{:S(2)}, u32[]{:S(2)}) collective-permute-start(bf16[56,1920]{1,0:T(8,128)(2,1)S(1)} %bitcast.109), channel_id=1, source_target_pairs={{12,0},{0,4},{4,8},{8,12},{28,16},{16,20},{20,24},{24,28},{44,32},... | collective-permute-start | bytes 645128 | tf_op jit(solution)/shard_map/ppermute | solution.py:35
  11.1 9.7 %collective-permute-start.1 = (bf16[56,1920]{1,0:T(8,128)(2,1)S(1)}, bf16[56,1920]{1,0:T(8,128)(2,1)}, u32[]{:S(2)}, u32[]{:S(2)}) collective-permute-start(bf16[56,1920]{1,0:T(8,128)(2,1)S(1)} %bitcast.110), channel_id=1, source_target_pairs={{8,0},{12,4},{0,8},{4,12},{24,16},{28,20},{16,24},{20,28},{40,32},... | collective-permute-start | bytes 645128 | tf_op jit(solution)/shard_map/ppermute | solution.py:35
  13.9 6.0 %collective-permute-start = (bf16[56,1920]{1,0:T(8,128)(2,1)S(1)}, bf16[56,1920]{1,0:T(8,128)(2,1)}, u32[]{:S(2)}, u32[]{:S(2)}) collective-permute-start(bf16[56,1920]{1,0:T(8,128)(2,1)S(1)} %bitcast.111), channel_id=1, source_target_pairs={{4,0},{8,4},{12,8},{0,12},{20,16},{24,20},{28,24},{16,28},{36,32},... | collective-permute-start | bytes 645128 | tf_op jit(solution)/shard_map/ppermute | solution.py:35
  17.9 12.8 %copy-start.38 = (bf16[1,2,2,384,896]{4,3,2,1,0:T(8,128)(2,1)S(1)}, bf16[1,2,2,384,896]{4,3,2,1,0:T(8,128)(2,1)}, u32[]{:S(2)}) copy-start(bf16[1,2,2,384,896]{4,3,2,1,0:T(8,128)(2,1)} %param.7) | copy-start | bytes 8257540
  22.8 18.9 %collective-permute-start.5 = (bf16[224,1920]{1,0:T(8,128)(2,1)S(1)}, bf16[224,1920]{1,0:T(8,128)(2,1)S(1)}, u32[]{:S(2)}, u32[]{:S(2)}) collective-permute-start(bf16[224,1920]{1,0:T(8,128)(2,1)S(1)} %constant_dynamic-update-slice_fusion.refs_0_.refs_16_), channel_id=1, source_target_pairs={{48,0},{52,4},{56,8},{60,12},{0,16},{4,20},{8,24},{12,28},{16,32},... | collective-permute-start | bytes 2580488 | tf_op jit(solution)/shard_map/ppermute | solution.py:35
  24.6 25.2 %collective-permute-start.4 = (bf16[224,1920]{1,0:T(8,128)(2,1)S(1)}, bf16[224,1920]{1,0:T(8,128)(2,1)S(1)}, u32[]{:S(2)}, u32[]{:S(2)}) collective-permute-start(bf16[224,1920]{1,0:T(8,128)(2,1)S(1)} %constant_dynamic-update-slice_fusion.refs_0_.refs_16_), channel_id=1, source_target_pairs={{32,0},{36,4},{40,8},{44,12},{48,16},{52,20},{56,24},{60,28},{0,32... | collective-permute-start | bytes 2580488 | tf_op jit(solution)/shard_map/ppermute | solution.py:35
  27.5 22.3 %collective-permute-start.3 = (bf16[224,1920]{1,0:T(8,128)(2,1)S(1)}, bf16[224,1920]{1,0:T(8,128)(2,1)S(1)}, u32[]{:S(2)}, u32[]{:S(2)}) collective-permute-start(bf16[224,1920]{1,0:T(8,128)(2,1)S(1)} %constant_dynamic-update-slice_fusion.refs_0_.refs_16_), channel_id=1, source_target_pairs={{16,0},{20,4},{24,8},{28,12},{32,16},{36,20},{40,24},{44,28},{48,3... | collective-permute-start | bytes 2580488 | tf_op jit(solution)/shard_map/ppermute | solution.py:35
  41.7 35.6 %copy-start.5 = (bf16[224,1920]{1,0:T(8,128)(2,1)}, bf16[224,1920]{1,0:T(8,128)(2,1)S(1)}, u32[]{:S(2)}) copy-start(bf16[224,1920]{1,0:T(8,128)(2,1)S(1)} %collective-permute-done.5.refs_3_.refs_19_) | copy-start | bytes 2580484
  49.7 27.6 %copy-start.7 = (bf16[224,1920]{1,0:T(8,128)(2,1)}, bf16[224,1920]{1,0:T(8,128)(2,1)S(1)}, u32[]{:S(2)}) copy-start(bf16[224,1920]{1,0:T(8,128)(2,1)S(1)} %collective-permute-done.4.refs_2_.refs_18_) | copy-start | bytes 2580484
  49.7 27.6 %copy-start.9 = (bf16[224,1920]{1,0:T(8,128)(2,1)}, bf16[224,1920]{1,0:T(8,128)(2,1)S(1)}, u32[]{:S(2)}) copy-start(bf16[224,1920]{1,0:T(8,128)(2,1)S(1)} %collective-permute-done.3.refs_1_.refs_17_) | copy-start | bytes 2580484
  57.4 19.9 %copy-start.1 = (f32[384,640]{1,0:T(8,128)}, f32[384,640]{1,0:T(8,128)S(1)}, u32[]{:S(2)}) copy-start(f32[384,640]{1,0:T(8,128)S(1)} %get-tuple-element.90.slope.refs_14_) | copy-start | bytes 2949124
  57.4 19.9 %copy-start.3 = (f32[384,640]{1,0:T(8,128)}, f32[384,640]{1,0:T(8,128)S(1)}, u32[]{:S(2)}) copy-start(f32[384,640]{1,0:T(8,128)S(1)} %get-tuple-element.91.activated.refs_15_) | copy-start | bytes 2949124
  57.4 10.8 %collective-permute-start.6 = (bf16[96,896]{1,0:T(8,128)(2,1)S(1)}, bf16[96,896]{1,0:T(8,128)(2,1)S(1)}, u32[]{:S(2)}, u32[]{:S(2)}) collective-permute-start(bf16[96,896]{1,0:T(8,128)(2,1)S(1)} %get-tuple-element.87), channel_id=1, source_target_pairs={{3,0},{0,1},{1,2},{2,3},{7,4},{4,5},{5,6},{6,7},{11,8},{8,9},{9,10... | collective-permute-start | bytes 516104 | tf_op jit(solution)/shard_map/ppermute | solution.py:40
  59.4 10.0 %collective-permute-start.7 = (bf16[96,896]{1,0:T(8,128)(2,1)S(1)}, bf16[96,896]{1,0:T(8,128)(2,1)S(1)}, u32[]{:S(2)}, u32[]{:S(2)}) collective-permute-start(bf16[96,896]{1,0:T(8,128)(2,1)S(1)} %get-tuple-element.88), channel_id=1, source_target_pairs={{2,0},{3,1},{0,2},{1,3},{6,4},{7,5},{4,6},{5,7},{10,8},{11,9},{8,1... | collective-permute-start | bytes 516104 | tf_op jit(solution)/shard_map/ppermute | solution.py:40
  62.9 6.5 %collective-permute-start.8 = (bf16[96,896]{1,0:T(8,128)(2,1)S(1)}, bf16[96,896]{1,0:T(8,128)(2,1)S(1)}, u32[]{:S(2)}, u32[]{:S(2)}) collective-permute-start(bf16[96,896]{1,0:T(8,128)(2,1)S(1)} %get-tuple-element.89), channel_id=1, source_target_pairs={{1,0},{2,1},{3,2},{0,3},{5,4},{6,5},{7,6},{4,7},{9,8},{10,9},{11,1... | collective-permute-start | bytes 516104 | tf_op jit(solution)/shard_map/ppermute | solution.py:40
  68.2 10.1 %copy-start.35 = (bf16[384,640]{1,0:T(8,128)(2,1)}, bf16[384,640]{1,0:T(8,128)(2,1)S(1)}, u32[]{:S(2)}) copy-start(bf16[384,640]{1,0:T(8,128)(2,1)S(1)} %get-tuple-element.104.refs_10_) | copy-start | bytes 1474564
  69.8 4.8 %collective-permute-start.12 = (bf16[96,896]{1,0:T(8,128)(2,1)S(1)}, bf16[96,896]{1,0:T(8,128)(2,1)S(1)}, u32[]{:S(2)}, u32[]{:S(2)}) collective-permute-start(bf16[96,896]{1,0:T(8,128)(2,1)S(1)} %mix.3.d), channel_id=1, source_target_pairs={{3,64},{0,65},{1,66},{2,67},{64,0},{65,1},{66,2},{67,3},{7,68},{4,... | collective-permute-start | bytes 516104 | tf_op jit(solution)/shard_map/ppermute | solution.py:46
  70.0 5.4 %collective-permute-start.11 = (bf16[96,896]{1,0:T(8,128)(2,1)S(1)}, bf16[96,896]{1,0:T(8,128)(2,1)S(1)}, u32[]{:S(2)}, u32[]{:S(2)}) collective-permute-start(bf16[96,896]{1,0:T(8,128)(2,1)S(1)} %mix.3.d), channel_id=1, source_target_pairs={{2,64},{3,65},{0,66},{1,67},{64,0},{65,1},{66,2},{67,3},{6,68},{7,... | collective-permute-start | bytes 516104 | tf_op jit(solution)/shard_map/ppermute | solution.py:46
  72.5 4.8 %collective-permute-start.10 = (bf16[96,896]{1,0:T(8,128)(2,1)S(1)}, bf16[96,896]{1,0:T(8,128)(2,1)S(1)}, u32[]{:S(2)}, u32[]{:S(2)}) collective-permute-start(bf16[96,896]{1,0:T(8,128)(2,1)S(1)} %mix.3.d), channel_id=1, source_target_pairs={{1,64},{2,65},{3,66},{0,67},{64,0},{65,1},{66,2},{67,3},{5,68},{6,... | collective-permute-start | bytes 516104 | tf_op jit(solution)/shard_map/ppermute | solution.py:46
  72.5 4.8 %collective-permute-start.9 = (bf16[96,896]{1,0:T(8,128)(2,1)S(1)}, bf16[96,896]{1,0:T(8,128)(2,1)S(1)}, u32[]{:S(2)}, u32[]{:S(2)}) collective-permute-start(bf16[96,896]{1,0:T(8,128)(2,1)S(1)} %mix.3.d), channel_id=1, source_target_pairs={{0,64},{1,65},{2,66},{3,67},{64,0},{65,1},{66,2},{67,3},{4,68},{5,... | collective-permute-start | bytes 516104 | tf_op jit(solution)/shard_map/ppermute | solution.py:46
  78.4 16.0 %collective-permute-start.14 = (bf16[96,896]{1,0:T(8,128)(2,1)}, bf16[96,896]{1,0:T(8,128)(2,1)}, u32[]{:S(2)}, u32[]{:S(2)}) collective-permute-start(bf16[96,896]{1,0:T(8,128)(2,1)} %get-tuple-element.95), channel_id=1, source_target_pairs={{67,0},{64,1},{65,2},{66,3},{0,64},{1,65},{2,66},{3,67},{71,4},{68... | collective-permute-start | bytes 516104 | tf_op jit(solution)/shard_map/ppermute | solution.py:46
  82.5 11.9 %collective-permute-start.15 = (bf16[96,896]{1,0:T(8,128)(2,1)}, bf16[96,896]{1,0:T(8,128)(2,1)}, u32[]{:S(2)}, u32[]{:S(2)}) collective-permute-start(bf16[96,896]{1,0:T(8,128)(2,1)} %get-tuple-element.96), channel_id=1, source_target_pairs={{66,0},{67,1},{64,2},{65,3},{0,64},{1,65},{2,66},{3,67},{70,4},{71... | collective-permute-start | bytes 516104 | tf_op jit(solution)/shard_map/ppermute | solution.py:46
  82.6 11.8 %collective-permute-start.16 = (bf16[96,896]{1,0:T(8,128)(2,1)}, bf16[96,896]{1,0:T(8,128)(2,1)}, u32[]{:S(2)}, u32[]{:S(2)}) collective-permute-start(bf16[96,896]{1,0:T(8,128)(2,1)} %get-tuple-element.97), channel_id=1, source_target_pairs={{65,0},{66,1},{67,2},{64,3},{0,64},{1,65},{2,66},{3,67},{69,4},{70... | collective-permute-start | bytes 516104 | tf_op jit(solution)/shard_map/ppermute | solution.py:46
  84.9 9.5 %collective-permute-start.13 = (bf16[96,896]{1,0:T(8,128)(2,1)}, bf16[96,896]{1,0:T(8,128)(2,1)}, u32[]{:S(2)}, u32[]{:S(2)}) collective-permute-start(bf16[96,896]{1,0:T(8,128)(2,1)} %get-tuple-element.92), channel_id=1, source_target_pairs={{64,0},{65,1},{66,2},{67,3},{0,64},{1,65},{2,66},{3,67},{68,4},{69... | collective-permute-start | bytes 516104 | tf_op jit(solution)/shard_map/ppermute | solution.py:46
  95.7 4.8 %collective-permute-start.20 = (bf16[96,896]{1,0:T(8,128)(2,1)S(1)}, bf16[96,896]{1,0:T(8,128)(2,1)S(1)}, u32[]{:S(2)}, u32[]{:S(2)}) collective-permute-start(bf16[96,896]{1,0:T(8,128)(2,1)S(1)} %mix.4.d), channel_id=1, source_target_pairs={{3,64},{0,65},{1,66},{2,67},{64,0},{65,1},{66,2},{67,3},{7,68},{4,... | collective-permute-start | bytes 516104 | tf_op jit(solution)/shard_map/ppermute | solution.py:46
  96.7 4.8 %collective-permute-start.19 = (bf16[96,896]{1,0:T(8,128)(2,1)S(1)}, bf16[96,896]{1,0:T(8,128)(2,1)S(1)}, u32[]{:S(2)}, u32[]{:S(2)}) collective-permute-start(bf16[96,896]{1,0:T(8,128)(2,1)S(1)} %mix.4.d), channel_id=1, source_target_pairs={{2,64},{3,65},{0,66},{1,67},{64,0},{65,1},{66,2},{67,3},{6,68},{7,... | collective-permute-start | bytes 516104 | tf_op jit(solution)/shard_map/ppermute | solution.py:46
  96.9 4.9 %collective-permute-start.18 = (bf16[96,896]{1,0:T(8,128)(2,1)S(1)}, bf16[96,896]{1,0:T(8,128)(2,1)S(1)}, u32[]{:S(2)}, u32[]{:S(2)}) collective-permute-start(bf16[96,896]{1,0:T(8,128)(2,1)S(1)} %mix.4.d), channel_id=1, source_target_pairs={{1,64},{2,65},{3,66},{0,67},{64,0},{65,1},{66,2},{67,3},{5,68},{6,... | collective-permute-start | bytes 516104 | tf_op jit(solution)/shard_map/ppermute | solution.py:46
  98.9 2.9 %collective-permute-start.17 = (bf16[96,896]{1,0:T(8,128)(2,1)S(1)}, bf16[96,896]{1,0:T(8,128)(2,1)S(1)}, u32[]{:S(2)}, u32[]{:S(2)}) collective-permute-start(bf16[96,896]{1,0:T(8,128)(2,1)S(1)} %mix.4.d), channel_id=1, source_target_pairs={{0,64},{1,65},{2,66},{3,67},{64,0},{65,1},{66,2},{67,3},{4,68},{5,... | collective-permute-start | bytes 516104 | tf_op jit(solution)/shard_map/ppermute | solution.py:46
  102.0 12.0 %collective-permute-start.21 = (bf16[96,896]{1,0:T(8,128)(2,1)S(1)}, bf16[96,896]{1,0:T(8,128)(2,1)S(1)}, u32[]{:S(2)}, u32[]{:S(2)}) collective-permute-start(bf16[96,896]{1,0:T(8,128)(2,1)S(1)} %get-tuple-element.101), channel_id=1, source_target_pairs={{64,0},{65,1},{66,2},{67,3},{0,64},{1,65},{2,66},{3,67},{68,4},{69... | collective-permute-start | bytes 516104 | tf_op jit(solution)/shard_map/ppermute | solution.py:46
  106.0 7.9 %collective-permute-start.22 = (bf16[96,896]{1,0:T(8,128)(2,1)S(1)}, bf16[96,896]{1,0:T(8,128)(2,1)S(1)}, u32[]{:S(2)}, u32[]{:S(2)}) collective-permute-start(bf16[96,896]{1,0:T(8,128)(2,1)S(1)} %get-tuple-element.110), channel_id=1, source_target_pairs={{67,0},{64,1},{65,2},{66,3},{0,64},{1,65},{2,66},{3,67},{71,4},{68... | collective-permute-start | bytes 516104 | tf_op jit(solution)/shard_map/ppermute | solution.py:46
  106.1 7.9 %collective-permute-start.23 = (bf16[96,896]{1,0:T(8,128)(2,1)S(1)}, bf16[96,896]{1,0:T(8,128)(2,1)S(1)}, u32[]{:S(2)}, u32[]{:S(2)}) collective-permute-start(bf16[96,896]{1,0:T(8,128)(2,1)S(1)} %get-tuple-element.111), channel_id=1, source_target_pairs={{66,0},{67,1},{64,2},{65,3},{0,64},{1,65},{2,66},{3,67},{70,4},{71... | collective-permute-start | bytes 516104 | tf_op jit(solution)/shard_map/ppermute | solution.py:46
  106.8 7.2 %collective-permute-start.24 = (bf16[96,896]{1,0:T(8,128)(2,1)S(1)}, bf16[96,896]{1,0:T(8,128)(2,1)S(1)}, u32[]{:S(2)}, u32[]{:S(2)}) collective-permute-start(bf16[96,896]{1,0:T(8,128)(2,1)S(1)} %get-tuple-element.112), channel_id=1, source_target_pairs={{65,0},{66,1},{67,2},{64,3},{0,64},{1,65},{2,66},{3,67},{69,4},{70... | collective-permute-start | bytes 516104 | tf_op jit(solution)/shard_map/ppermute | solution.py:46
  108.5 13.3 %copy-start.11 = (bf16[384,896]{1,0:T(8,128)(2,1)S(1)}, bf16[384,896]{1,0:T(8,128)(2,1)}, u32[]{:S(2)}) copy-start(bf16[384,896]{1,0:T(8,128)(2,1)} %get-tuple-element.157.d) | copy-start | bytes 2064388
  108.5 13.3 %copy-start.12 = (bf16[384,896]{1,0:T(8,128)(2,1)S(1)}, bf16[384,896]{1,0:T(8,128)(2,1)}, u32[]{:S(2)}) copy-start(bf16[384,896]{1,0:T(8,128)(2,1)} %get-tuple-element.113.x) | copy-start | bytes 2064388
  114.3 23.0 %collective-permute-start.34 = (bf16[224,1920]{1,0:T(8,128)(2,1)S(1)}, bf16[224,1920]{1,0:T(8,128)(2,1)S(1)}, u32[]{:S(2)}, u32[]{:S(2)}) collective-permute-start(bf16[224,1920]{1,0:T(8,128)(2,1)S(1)} %get-tuple-element.133), channel_id=1, source_target_pairs={{48,0},{52,4},{56,8},{60,12},{0,16},{4,20},{8,24},{12,28},{16,32},... | collective-permute-start | bytes 2580488 | tf_op jit(solution)/shard_map/ppermute | solution.py:35
  115.7 10.9 %collective-permute-start.27 = (bf16[96,896]{1,0:T(8,128)(2,1)S(1)}, bf16[96,896]{1,0:T(8,128)(2,1)S(1)}, u32[]{:S(2)}, u32[]{:S(2)}) collective-permute-start(bf16[96,896]{1,0:T(8,128)(2,1)S(1)} %mix.5.refs_4_), channel_id=1, source_target_pairs={{3,0},{0,1},{1,2},{2,3},{7,4},{4,5},{5,6},{6,7},{11,8},{8,9},{9,10... | collective-permute-start | bytes 516104 | tf_op jit(solution)/shard_map/ppermute | solution.py:40
  116.6 10.0 %collective-permute-start.26 = (bf16[96,896]{1,0:T(8,128)(2,1)S(1)}, bf16[96,896]{1,0:T(8,128)(2,1)S(1)}, u32[]{:S(2)}, u32[]{:S(2)}) collective-permute-start(bf16[96,896]{1,0:T(8,128)(2,1)S(1)} %mix.5.refs_4_), channel_id=1, source_target_pairs={{2,0},{3,1},{0,2},{1,3},{6,4},{7,5},{4,6},{5,7},{10,8},{11,9},{8,1... | collective-permute-start | bytes 516104 | tf_op jit(solution)/shard_map/ppermute | solution.py:40
  119.0 8.2 %collective-permute-start.25 = (bf16[96,896]{1,0:T(8,128)(2,1)S(1)}, bf16[96,896]{1,0:T(8,128)(2,1)S(1)}, u32[]{:S(2)}, u32[]{:S(2)}) collective-permute-start(bf16[96,896]{1,0:T(8,128)(2,1)S(1)} %mix.5.refs_4_), channel_id=1, source_target_pairs={{1,0},{2,1},{3,2},{0,3},{5,4},{6,5},{7,6},{4,7},{9,8},{10,9},{11,1... | collective-permute-start | bytes 516104 | tf_op jit(solution)/shard_map/ppermute | solution.py:40
  119.9 30.7 %collective-permute-start.36 = (bf16[224,1920]{1,0:T(8,128)(2,1)S(1)}, bf16[224,1920]{1,0:T(8,128)(2,1)S(1)}, u32[]{:S(2)}, u32[]{:S(2)}) collective-permute-start(bf16[224,1920]{1,0:T(8,128)(2,1)S(1)} %get-tuple-element.135), channel_id=1, source_target_pairs={{16,0},{20,4},{24,8},{28,12},{32,16},{36,20},{40,24},{44,28},{48,3... | collective-permute-start | bytes 2580488 | tf_op jit(solution)/shard_map/ppermute | solution.py:35
  127.2 23.4 %collective-permute-start.35 = (bf16[224,1920]{1,0:T(8,128)(2,1)S(1)}, bf16[224,1920]{1,0:T(8,128)(2,1)S(1)}, u32[]{:S(2)}, u32[]{:S(2)}) collective-permute-start(bf16[224,1920]{1,0:T(8,128)(2,1)S(1)} %get-tuple-element.134), channel_id=1, source_target_pairs={{32,0},{36,4},{40,8},{44,12},{48,16},{52,20},{56,24},{60,28},{0,32... | collective-permute-start | bytes 2580488 | tf_op jit(solution)/shard_map/ppermute | solution.py:35
  134.4 16.8 %collective-permute-start.28 = (bf16[224,1920]{1,0:T(8,128)(2,1)S(1)}, bf16[224,1920]{1,0:T(8,128)(2,1)S(1)}, u32[]{:S(2)}, u32[]{:S(2)}) collective-permute-start(bf16[224,1920]{1,0:T(8,128)(2,1)S(1)} %get-tuple-element.121), channel_id=1, source_target_pairs={{48,0},{52,4},{56,8},{60,12},{0,16},{4,20},{8,24},{12,28},{16,32},... | collective-permute-start | bytes 2580488 | tf_op jit(solution)/shard_map/ppermute | solution.py:35
  135.0 30.1 %collective-permute-start.29 = (bf16[224,1920]{1,0:T(8,128)(2,1)S(1)}, bf16[224,1920]{1,0:T(8,128)(2,1)S(1)}, u32[]{:S(2)}, u32[]{:S(2)}) collective-permute-start(bf16[224,1920]{1,0:T(8,128)(2,1)S(1)} %get-tuple-element.122), channel_id=1, source_target_pairs={{32,0},{36,4},{40,8},{44,12},{48,16},{52,20},{56,24},{60,28},{0,32... | collective-permute-start | bytes 2580488 | tf_op jit(solution)/shard_map/ppermute | solution.py:35
  137.3 27.8 %collective-permute-start.30 = (bf16[224,1920]{1,0:T(8,128)(2,1)S(1)}, bf16[224,1920]{1,0:T(8,128)(2,1)S(1)}, u32[]{:S(2)}, u32[]{:S(2)}) collective-permute-start(bf16[224,1920]{1,0:T(8,128)(2,1)S(1)} %get-tuple-element.123), channel_id=1, source_target_pairs={{16,0},{20,4},{24,8},{28,12},{32,16},{36,20},{40,24},{44,28},{48,3... | collective-permute-start | bytes 2580488 | tf_op jit(solution)/shard_map/ppermute | solution.py:35
  151.0 18.1 %collective-permute-start.37 = (bf16[56,1920]{1,0:T(8,128)(2,1)S(1)}, bf16[56,1920]{1,0:T(8,128)(2,1)S(1)}, u32[]{:S(2)}, u32[]{:S(2)}) collective-permute-start(bf16[56,1920]{1,0:T(8,128)(2,1)S(1)} %get-tuple-element.137), channel_id=1, source_target_pairs={{12,0},{0,4},{4,8},{8,12},{28,16},{16,20},{20,24},{24,28},{44,32},... | collective-permute-start | bytes 645128 | tf_op jit(solution)/shard_map/ppermute | solution.py:35
  151.1 19.0 %collective-permute-start.38 = (bf16[56,1920]{1,0:T(8,128)(2,1)S(1)}, bf16[56,1920]{1,0:T(8,128)(2,1)S(1)}, u32[]{:S(2)}, u32[]{:S(2)}) collective-permute-start(bf16[56,1920]{1,0:T(8,128)(2,1)S(1)} %get-tuple-element.138), channel_id=1, source_target_pairs={{8,0},{12,4},{0,8},{4,12},{24,16},{28,20},{16,24},{20,28},{40,32},... | collective-permute-start | bytes 645128 | tf_op jit(solution)/shard_map/ppermute | solution.py:35
  151.2 18.9 %collective-permute-start.39 = (bf16[56,1920]{1,0:T(8,128)(2,1)S(1)}, bf16[56,1920]{1,0:T(8,128)(2,1)S(1)}, u32[]{:S(2)}, u32[]{:S(2)}) collective-permute-start(bf16[56,1920]{1,0:T(8,128)(2,1)S(1)} %get-tuple-element.139), channel_id=1, source_target_pairs={{4,0},{8,4},{12,8},{0,12},{20,16},{24,20},{28,24},{16,28},{36,32},... | collective-permute-start | bytes 645128 | tf_op jit(solution)/shard_map/ppermute | solution.py:35
  165.5 7.1 %collective-permute-start.31 = (bf16[56,1920]{1,0:T(8,128)(2,1)S(1)}, bf16[56,1920]{1,0:T(8,128)(2,1)S(1)}, u32[]{:S(2)}, u32[]{:S(2)}) collective-permute-start(bf16[56,1920]{1,0:T(8,128)(2,1)S(1)} %get-tuple-element.125), channel_id=1, source_target_pairs={{12,0},{0,4},{4,8},{8,12},{28,16},{16,20},{20,24},{24,28},{44,32},... | collective-permute-start | bytes 645128 | tf_op jit(solution)/shard_map/ppermute | solution.py:35
  166.9 8.3 %collective-permute-start.32 = (bf16[56,1920]{1,0:T(8,128)(2,1)S(1)}, bf16[56,1920]{1,0:T(8,128)(2,1)S(1)}, u32[]{:S(2)}, u32[]{:S(2)}) collective-permute-start(bf16[56,1920]{1,0:T(8,128)(2,1)S(1)} %get-tuple-element.126), channel_id=1, source_target_pairs={{8,0},{12,4},{0,8},{4,12},{24,16},{28,20},{16,24},{20,28},{40,32},... | collective-permute-start | bytes 645128 | tf_op jit(solution)/shard_map/ppermute | solution.py:35
  169.1 6.7 %collective-permute-start.33 = (bf16[56,1920]{1,0:T(8,128)(2,1)S(1)}, bf16[56,1920]{1,0:T(8,128)(2,1)S(1)}, u32[]{:S(2)}, u32[]{:S(2)}) collective-permute-start(bf16[56,1920]{1,0:T(8,128)(2,1)S(1)} %get-tuple-element.127), channel_id=1, source_target_pairs={{4,0},{8,4},{12,8},{0,12},{20,16},{24,20},{28,24},{16,28},{36,32},... | collective-permute-start | bytes 645128 | tf_op jit(solution)/shard_map/ppermute | solution.py:35
  170.4 31.1 %copy-start.37 = (f32[1,56,2,3,640]{4,2,3,1,0:T(2,128)S(1)}, f32[1,56,2,3,640]{4,2,3,1,0:T(2,128)}, u32[]{:S(2)}) copy-start(f32[1,56,2,3,640]{4,2,3,1,0:T(2,128)} %param.11) | copy-start | bytes 2580484
  170.4 31.1 %copy-start.40 = (bf16[1,56,2,3,640]{4,2,3,1,0:T(2,128)(2,1)S(1)}, bf16[1,56,2,3,640]{4,2,3,1,0:T(2,128)(2,1)}, u32[]{:S(2)}) copy-start(bf16[1,56,2,3,640]{4,2,3,1,0:T(2,128)(2,1)} %param.13) | copy-start | bytes 1290244
  170.4 31.1 %copy-start.41 = (bf16[1,56,2,3,640]{4,2,3,1,0:T(2,128)(2,1)S(1)}, bf16[1,56,2,3,640]{4,2,3,1,0:T(2,128)(2,1)}, u32[]{:S(2)}) copy-start(bf16[1,56,2,3,640]{4,2,3,1,0:T(2,128)(2,1)} %param.12) | copy-start | bytes 1290244
  176.1 1.2 collective-permute-start.40
  177.3 4.8 %collective-permute-start.43 = (f32[8,128]{1,0:T(8,128)S(1)}, f32[8,128]{1,0:T(8,128)S(1)}, u32[]{:S(2)}, u32[]{:S(2)}) collective-permute-start(f32[8,128]{1,0:T(8,128)S(1)} %add.249), channel_id=1, source_target_pairs={{12,0},{0,4},{4,8},{8,12},{28,16},{16,20},{20,24},{24,28},{44,32},... | collective-permute-start | bytes 12296 | tf_op jit(solution)/shard_map/ppermute | solution.py:35
  178.5 5.1 %collective-permute-start.42 = (f32[8,128]{1,0:T(8,128)S(1)}, f32[8,128]{1,0:T(8,128)S(1)}, u32[]{:S(2)}, u32[]{:S(2)}) collective-permute-start(f32[8,128]{1,0:T(8,128)S(1)} %add.249), channel_id=1, source_target_pairs={{8,0},{12,4},{0,8},{4,12},{24,16},{28,20},{16,24},{20,28},{40,32},... | collective-permute-start | bytes 12296 | tf_op jit(solution)/shard_map/ppermute | solution.py:35
  181.4 3.6 %collective-permute-start.41 = (f32[8,128]{1,0:T(8,128)S(1)}, f32[8,128]{1,0:T(8,128)S(1)}, u32[]{:S(2)}, u32[]{:S(2)}) collective-permute-start(f32[8,128]{1,0:T(8,128)S(1)} %add.249), channel_id=1, source_target_pairs={{4,0},{8,4},{12,8},{0,12},{20,16},{24,20},{28,24},{16,28},{36,32},... | collective-permute-start | bytes 12296 | tf_op jit(solution)/shard_map/ppermute | solution.py:35
  185.0 5.6 %collective-permute-start.46 = (f32[8,128]{1,0:T(8,128)S(1)}, f32[8,128]{1,0:T(8,128)S(1)}, u32[]{:S(2)}, u32[]{:S(2)}) collective-permute-start(f32[8,128]{1,0:T(8,128)S(1)} %add_add_fusion.2), channel_id=1, source_target_pairs={{48,0},{52,4},{56,8},{60,12},{0,16},{4,20},{8,24},{12,28},{16,32},... | collective-permute-start | bytes 12296 | tf_op jit(solution)/shard_map/ppermute | solution.py:35
  186.9 5.1 %collective-permute-start.45 = (f32[8,128]{1,0:T(8,128)S(1)}, f32[8,128]{1,0:T(8,128)S(1)}, u32[]{:S(2)}, u32[]{:S(2)}) collective-permute-start(f32[8,128]{1,0:T(8,128)S(1)} %add_add_fusion.2), channel_id=1, source_target_pairs={{32,0},{36,4},{40,8},{44,12},{48,16},{52,20},{56,24},{60,28},{0,32... | collective-permute-start | bytes 12296 | tf_op jit(solution)/shard_map/ppermute | solution.py:35
  189.5 3.6 %collective-permute-start.44 = (f32[8,128]{1,0:T(8,128)S(1)}, f32[8,128]{1,0:T(8,128)S(1)}, u32[]{:S(2)}, u32[]{:S(2)}) collective-permute-start(f32[8,128]{1,0:T(8,128)S(1)} %add_add_fusion.2), channel_id=1, source_target_pairs={{16,0},{20,4},{24,8},{28,12},{32,16},{36,20},{40,24},{44,28},{48,3... | collective-permute-start | bytes 12296 | tf_op jit(solution)/shard_map/ppermute | solution.py:35
  193.1 5.2 %collective-permute-start.49 = (f32[8,128]{1,0:T(8,128)S(1)}, f32[8,128]{1,0:T(8,128)S(1)}, u32[]{:S(2)}, u32[]{:S(2)}) collective-permute-start(f32[8,128]{1,0:T(8,128)S(1)} %add_add_fusion.1), channel_id=1, source_target_pairs={{3,0},{0,1},{1,2},{2,3},{7,4},{4,5},{5,6},{6,7},{11,8},{8,9},{9,10... | collective-permute-start | bytes 12296 | tf_op jit(solution)/shard_map/ppermute | solution.py:40
  194.2 5.1 %collective-permute-start.48 = (f32[8,128]{1,0:T(8,128)S(1)}, f32[8,128]{1,0:T(8,128)S(1)}, u32[]{:S(2)}, u32[]{:S(2)}) collective-permute-start(f32[8,128]{1,0:T(8,128)S(1)} %add_add_fusion.1), channel_id=1, source_target_pairs={{2,0},{3,1},{0,2},{1,3},{6,4},{7,5},{4,6},{5,7},{10,8},{11,9},{8,1... | collective-permute-start | bytes 12296 | tf_op jit(solution)/shard_map/ppermute | solution.py:40
  196.5 3.8 %collective-permute-start.47 = (f32[8,128]{1,0:T(8,128)S(1)}, f32[8,128]{1,0:T(8,128)S(1)}, u32[]{:S(2)}, u32[]{:S(2)}) collective-permute-start(f32[8,128]{1,0:T(8,128)S(1)} %add_add_fusion.1), channel_id=1, source_target_pairs={{1,0},{2,1},{3,2},{0,3},{5,4},{6,5},{7,6},{4,7},{9,8},{10,9},{11,1... | collective-permute-start | bytes 12296 | tf_op jit(solution)/shard_map/ppermute | solution.py:40
  (30 other events, 175.5 us)
Sparse Core Ops, SparseCore 0:
  10.7 65.2 all-gather.1
where the time goes:
time: 216 us; the launch traced here: 213 us
  starting transfers between devices  75.8 us (35%)
  waiting for transfers between devices  57.2 us (26%)
  Pallas kernels  31 us (14%)
  local copies, waits for them, and re-layouts  20.9 us (10%)
  between operations  15.8 us (7%)
  matrix products  7.74 us (4%)
  other arithmetic  4.44 us (2%)
    ppermute x24, waiting for transfers between devices, from_plane(): return lax.ppermute(value, ('pipe', 'dp'), pairs)  44.8 us
    ppermute x24, starting transfers between devices, from_plane(): return lax.ppermute(value, ('pipe', 'dp'), pairs)  40.4 us
    pallas_call x16, Pallas kernels, run(): pl.pallas_call(kernel, out_shape=[jax.ShapeDtypeStruct(o[0], o[1]) for o...  31 us
    ppermute x16, starting transfers between devices, across(): return lax.ppermute(value, ('pipe', 'tensor'), pairs)  19.9 us
    ppermute x9, starting transfers between devices, from_z(): return lax.ppermute(value, 'tensor', pairs)  15.6 us
    unnamed x95, local copies, waits for them, and re-layouts  13.6 us
    dot_general x3, matrix products, moved(): return jnp.dot(turned(rows), mover, preferred_element_type=F32).astype(BF16)  7.74 us
    ppermute x9, waiting for transfers between devices, from_z(): return lax.ppermute(value, 'tensor', pairs)  6.39 us
  transfers between devices with their start and end apart: 51, of which 23 were waited for; matrix products, arithmetic and copies ran while one was open for 9% of the time, Pallas kernels for 14%

commit v1 on v0

--- a/solution.py
+++ b/solution.py
@@ -57,7 +57,7 @@
     return total
 
 
-def run(kernel, ins, outs, scratch=(), flops=0, name=None):
+def run(kernel, ins, outs, scratch=(), flops=0, name=None, limit=VMEM_LIMIT):
     arrays, specs = [], []
     for item in ins:
         array, space = item if isinstance(item, tuple) else (item, pltpu.VMEM)
@@ -71,7 +71,7 @@
         in_specs=specs,
         out_specs=[pl.BlockSpec(memory_space=o[2] if o[2:] else pltpu.VMEM) for o in outs],
         scratch_shapes=list(scratch),
-        compiler_params=pltpu.CompilerParams(vmem_limit_bytes=VMEM_LIMIT),
+        compiler_params=pltpu.CompilerParams(vmem_limit_bytes=limit),
         cost_estimate=pl.CostEstimate(flops=flops, bytes_accessed=moved, transcendentals=0),
         name=name,
     )(*arrays)
@@ -92,7 +92,7 @@
 
 
 def gate_parts(normed, weights, units):
-    both = dot(normed, weights[:, : 2 * units])
+    both = dot(normed, weights[0][...])
     gate, up_rows = both[:, :units], both[:, units:]
     sigmoid_gate = jax.nn.sigmoid(gate)
     activated = gate * sigmoid_gate
@@ -102,7 +102,7 @@
 
 
 def both_grads(cotangent, slope, activated, weights, units):
-    hidden_grad = dot(cotangent, weights[:, 2 * units :])
+    hidden_grad = dot(cotangent, weights[1][...])
     return jnp.concatenate(
         [(hidden_grad * slope).astype(BF16), (hidden_grad * activated).astype(BF16)], 1
     )
@@ -110,7 +110,7 @@
 
 def store_branch(grads, inputs, weights, units, outs):
     branch = lax.dot_general(
-        grads, weights[:, : 2 * units], (((1,), (1,)), ((), ())), preferred_element_type=F32
+        grads, weights[0][...], (((1,), (1,)), ((), ())), preferred_element_type=F32
     )
     unit_rows, root_mean = normalized(inputs)
     centered = branch - unit_rows * jnp.mean(branch * unit_rows, axis=-1, keepdims=True)
@@ -144,17 +144,21 @@
     )
 
 
-def order_kernel(mover, whole, out, matrix, weights, sems):
-    rows, columns = out.shape[0] // SIDE, out.shape[1] // 3
+def apart(weights, units):
+    return weights.at[:, pl.ds(0, 2 * units)], weights.at[:, pl.ds(2 * units, units)]
+
+
+def order_kernel(first, mover, whole, out, matrix, weights, sems):
+    count = sems.shape[0] - 1
+    columns = out.shape[1] // count
     copies = [pltpu.make_async_copy(mover, matrix, sems.at[0])]
-    for i in range(3):
-        part = pl.ds(i * columns, columns)
-        copies.append(
-            pltpu.make_async_copy(whole.at[:, part], weights.at[:, part], sems.at[i + 1])
-        )
+    for i in range(count):
+        source = whole.at[:, pl.ds(first + i * columns, columns)]
+        target = weights.at[:, pl.ds(i * columns, columns)]
+        copies.append(pltpu.make_async_copy(source, target, sems.at[i + 1]))
     started(copies)
     copies[0].wait()
-    for i in range(3):
+    for i in range(count):
         copies[i + 1].wait()
         part = slice(i * columns, (i + 1) * columns)
         out[:, part] = dot(matrix[...], weights[:, part]).astype(BF16)
@@ -163,13 +167,14 @@
 def gate_kernel(units, x, weights, *outs):
     normed = normalized(x[...])[0].astype(BF16)
     outs[0][...] = normed.T
-    outs[1][...], outs[2][...], outs[3][...] = gate_parts(normed, weights, units)
+    outs[1][...], outs[2][...], outs[3][...] = gate_parts(normed, (weights,), units)
 
 
 def first_kernel(units, x, d, *refs):
     pieces, halves, outs = refs[:4], refs[4:8], refs[8:12]
     weights, sems, stages, out_sems = refs[12], refs[13], refs[14:18], refs[18]
     copies = weight_copies(pieces, weights, sems)
+    weights = apart(weights, units)
     sends = [
         pltpu.make_async_copy(stage, half, out_sems.at[i])
         for i, (stage, half) in enumerate(zip(stages, halves))
@@ -186,14 +191,14 @@
     waited(sends)
 
 
-def chain_kernel(units, active, x, slope, activated, weights, *refs):
+def chain_kernel(units, active, x, slope, activated, ins, down, *refs):
     groups, outs = refs[:4], refs[4:]
 
     @pl.when(active[0] != 0)
     def _():
         cotangent = jnp.concatenate([g[...] for g in groups], 0)
-        grads = both_grads(cotangent, slope[...], activated[...], weights, units)
-        store_branch(grads, x[...], weights, units, outs)
+        grads = both_grads(cotangent, slope[...], activated[...], (ins, down), units)
+        store_branch(grads, x[...], (ins, down), units, outs)
 
     @pl.when(active[0] == 0)
     def _():
@@ -216,8 +221,8 @@
         )
         cotangent = jnp.concatenate([g[...] for g in groups], 0)
         waited(copies)
-        grads = both_grads(cotangent, slope_here[...], activated_here[...], weights, units)
-        store_branch(grads, x[...], weights, units, outs)
+        grads = both_grads(cotangent, slope_here[...], activated_here[...], apart(weights, units), units)
+        store_branch(grads, x[...], apart(weights, units), units, outs)
 
     @pl.when(active[0] == 0)
     def _():
@@ -226,11 +231,11 @@
 
 
 def early_kernel(units, x, d, *refs):
-    if len(refs) > 5:
+    if len(refs) > 6:
         pieces, outs, weights, sems = refs[:4], refs[4:8], refs[8], refs[9]
-        copies = weight_copies(pieces, weights, sems)
+        copies, weights = weight_copies(pieces, weights, sems), apart(weights, units)
     else:
-        weights, outs, copies = refs[0], refs[1:], []
+        weights, outs, copies = refs[:2], refs[2:], []
     normed = normalized(x[...])[0].astype(BF16)
     outs[0][...] = normed.T
     outs[1][...] = d[...].T
@@ -250,7 +255,6 @@
         copies = weight_copies(pieces, weights, sems)
     else:
         weights, outs, copies = refs[16], refs[17:21], []
-    down = slice(weights.shape[1] - units, weights.shape[1])
     tokens = normed_early.shape[1]
     cotangent = jnp.concatenate(
         [jnp.where(use_first[0] != 0, a[...], b[...]) for a, b in zip(first, second)], 0
@@ -263,7 +267,7 @@
     hiddens[:tokens] = hidden_early[...]
     hiddens[tokens:] = hidden_last[...]
     waited(copies)
-    hidden_grad = dot(cotangent, weights[:, down])
+    hidden_grad = dot(cotangent, weights[...])
     grads[tokens:, :units] = (hidden_grad * slope[...]).astype(BF16)
     grads[tokens:, units:] = (hidden_grad * activated[...]).astype(BF16)
     for i, out in enumerate(outs):
@@ -402,7 +406,6 @@
     final_groups = [final[i * group : (i + 1) * group] for i in range(SIDE)]
 
     flop = 2 * tokens * width * units
-    whole = [((width, wide), BF16)]
     half_outs = [
         ((width, tokens), BF16),
         ((tokens, units), BF16),
@@ -418,7 +421,7 @@
         return [pltpu.VMEM((width, columns), BF16), pltpu.SemaphoreType.DMA((6,))]
 
     def early_parts(leg, leg_inputs, weights):
-        one = len(weights) == 1
+        one = len(weights) < 4
         return run(
             functools.partial(early_kernel, units),
             [leg_inputs, early[leg], *(weights if one else far(weights))],
@@ -434,7 +437,7 @@
         )
 
     def terms(use_first, first, second, early_half, half, weights):
-        one = len(weights) == 1
+        one = len(weights) < 4
         return run(
             functools.partial(terms_kernel, units),
             [
@@ -488,24 +491,33 @@
     )
 
     got = [across(part2[by], -by, 1) for by in range(SIDE)]
-    lower_whole = after(lower_whole, part2[0])
-    (lower_weights,) = run(
-        order_kernel,
-        far([mover.T, lower_whole]),
-        whole,
-        [pltpu.VMEM((width, width), BF16), *fetched(wide)],
-        2 * width * width * wide,
-        "order",
-    )
-    mine1 = reduced_group(after(mine2, lower_weights), got, None)
+
+    def ordered(columns, count, *others):
+        first, last = columns
+        return run(
+            functools.partial(order_kernel, first),
+            far([mover.T, after(lower_whole, *others)]),
+            [((width, last - first), BF16)],
+            [
+                pltpu.VMEM((width, width), BF16),
+                pltpu.VMEM((width, last - first), BF16),
+                pltpu.SemaphoreType.DMA((count + 1,)),
+            ],
+            2 * width * width * (last - first),
+            "order",
+        )[0]
+
+    lower_ins = ordered((0, 2 * units), 2, part2[0])
+    mine1 = reduced_group(after(mine2, lower_ins), got, None)
     cot1 = [across(mine1, by, 0) for by in range(SIDE)]
     lower_half = run(
         functools.partial(gate_kernel, units),
-        [after(inputs[0, 1], mine1), lower_weights],
+        [after(inputs[0, 1], mine1), lower_ins],
         half_outs,
         flops=2 * flop,
         name="gate",
     )
+    lower_down = ordered((2 * units, 3 * units), 1, mine1)
     part1 = run(
         functools.partial(chain_kernel, units),
         [
@@ -513,7 +525,8 @@
             inputs[0, 1],
             lower_half[2],
             lower_half[3],
-            lower_weights,
+            lower_ins,
+            lower_down,
             *cot1,
         ],
         group_outs,
@@ -526,9 +539,10 @@
     mine0 = reduced_group(after(mine1, upper_terms[0]), got, swap)
     cot0 = shared_groups(mine0)
     upper_got = near_pieces(after(upper_terms, mine0))
-    early_zero = early_parts(0, after(inputs[0, 0], mine0), [lower_weights])
+    early_zero = early_parts(0, after(inputs[0, 0], mine0), [lower_ins, lower_down])
     upper_got |= far_piece(after(upper_terms[2], cot0))
-    lower_terms = terms(on_second, cot1, cot0, early_zero, lower_half, [lower_weights])
+    early_zero = after(early_zero, [upper_got[by] for by in (1, 3)])
+    lower_terms = terms(on_second, cot1, cot0, early_zero, lower_half, [lower_down])
 
     lower_got = near_pieces(lower_terms) | far_piece(lower_terms[2])
     upper_sums = add_pieces(after(upper_terms[0], lower_terms[0]), upper_got)

time: 216 us -> 215 us (level)
  waiting for transfers between devices: 57.2 us -> 64.2 us
  starting transfers between devices: 75.8 us -> 71.1 us
  local copies, waits for them, and re-layouts: 20.9 us -> 17.8 us
    ppermute x9, waiting for transfers between devices: 6.39 us -> 10.2 us  [from_z(): return lax.ppermute(value, 'tensor', pairs)]
    ppermute x24, starting transfers between devices: 40.4 us -> 37.6 us  [from_plane(): return lax.ppermute(value, ('pipe', 'dp'), pairs)]
    unnamed x95 -> x101, local copies, waits for them, and re-layouts: 13.6 us -> 11.2 us
    pallas_call x16 -> x17, Pallas kernels: 31 us -> 31.5 us  [run(): pl.pallas_call(kernel, out_shape=[jax.ShapeDtypeStruct(o[0], o[1]) for o...]
  transfers between devices with their start and end apart: 51 -> 51, of which waited for: 23 -> 23; matrix products, arithmetic and copies ran while one was open for 9% -> 8% of each run, Pallas kernels for 14% -> 14%
where the time goes in v1:
time: 215 us; the launch traced here: 211 us
  starting transfers between devices  71.1 us (33%)
  waiting for transfers between devices  64.2 us (30%)
  Pallas kernels  31.5 us (15%)
  local copies, waits for them, and re-layouts  17.8 us (8%)
  between operations  16 us (7%)
  matrix products  7.74 us (4%)
  other arithmetic  3.23 us (2%)
    ppermute x24, waiting for transfers between devices, from_plane(): return lax.ppermute(value, ('pipe', 'dp'), pairs)  46.9 us
    ppermute x24, starting transfers between devices, from_plane(): return lax.ppermute(value, ('pipe', 'dp'), pairs)  37.6 us
    pallas_call x17, Pallas kernels, run(): pl.pallas_call(kernel, out_shape=[jax.ShapeDtypeStruct(o[0], o[1]) for o...  31.5 us
    ppermute x16, starting transfers between devices, across(): return lax.ppermute(value, ('pipe', 'tensor'), pairs)  18.9 us
    ppermute x9, starting transfers between devices, from_z(): return lax.ppermute(value, 'tensor', pairs)  14.5 us
    unnamed x101, local copies, waits for them, and re-layouts  11.2 us
    ppermute x9, waiting for transfers between devices, from_z(): return lax.ppermute(value, 'tensor', pairs)  10.2 us
    dot_general x3, matrix products, moved(): return jnp.dot(turned(rows), mover, preferred_element_type=F32).astype(BF16)  7.74 us
  transfers between devices with their start and end apart: 51, of which 23 were waited for; matrix products, arithmetic and copies ran while one was open for 8% of the time, Pallas kernels for 14%

profile of v1, /device:TPU:0, one launch (start us, length us, event | category | flops | bytes accessed | tf_op | source)
XLA Modules:
  0.0 211.5 jit_solution(3413729026433919506)
XLA Ops:
  7.2 1.2 copy.43
  9.5 1.6 collective-permute-start.2
  11.1 2.7 %collective-permute-start.1 = (bf16[56,1920]{1,0:T(8,128)(2,1)S(1)}, bf16[56,1920]{1,0:T(8,128)(2,1)}, u32[]{:S(2)}, u32[]{:S(2)}) collective-permute-start(bf16[56,1920]{1,0:T(8,128)(2,1)S(1)} %bitcast.110), channel_id=1, source_target_pairs={{8,0},{12,4},{0,8},{4,12},{24,16},{28,20},{16,24},{20,28},{40,32},... | collective-permute-start | bytes 645128 | tf_op jit(solution)/shard_map/ppermute | solution.py:35
  13.9 1.4 collective-permute-start
  15.9 1.4 broadcast_compare_fusion
  18.0 2.0 collective-permute-done
  21.9 1.7 collective-permute-start.5
  23.6 2.9 %collective-permute-start.4 = (bf16[224,1920]{1,0:T(8,128)(2,1)S(1)}, bf16[224,1920]{1,0:T(8,128)(2,1)S(1)}, u32[]{:S(2)}, u32[]{:S(2)}) collective-permute-start(bf16[224,1920]{1,0:T(8,128)(2,1)S(1)} %constant_dynamic-update-slice_fusion.refs_0_.refs_16_), channel_id=1, source_target_pairs={{32,0},{36,4},{40,8},{44,12},{48,16},{52,20},{56,24},{60,28},{0,32... | collective-permute-start | bytes 2580488 | tf_op jit(solution)/shard_map/ppermute | solution.py:35
  26.5 1.6 collective-permute-start.3
  28.1 1.2 constant_dynamic-slice_fusion.3
  29.8 1.0 fusion.35.d
  31.6 1.8 broadcast_select_fusion
  34.4 4.9 %fusion.16 = bf16[2,2,384,896]{3,2,1,0:T(8,128)(2,1)S(1)} fusion(bf16[2,2,96,896]{3,2,1,0:T(8,128)(2,1)S(1)} %get-tuple-element.164, bf16[2,2,96,896]{3,2,1,0:T(8,128)(2,1)S(1)} %get-tuple-element.165, bf16[2,2,96,896]{3,2,1,0:T(8,128)(2,1)S(1)} %get-tuple-element.166, bf16[2,2,96,896]{3,2,1,0:T(8,128)(2,1)S(1)} %get-tuple-element.163, s32[896]{0:T(1024)S(1)} %fusion.61), kind=kOutput, calls=%fused_computation.17 | convolution fusion | flops 2479439872 | bytes 5508608 | tf_op jit(solution)/shard_map/dot_general | solution.py:400
  39.3 1.3 slice_bitcast_fusion.1
  40.7 8.6 %collective-permute-done.4.refs_2_.refs_18_ = bf16[224,1920]{1,0:T(8,128)(2,1)S(1)} collective-permute-done((bf16[224,1920]{1,0:T(8,128)(2,1)S(1)}, bf16[224,1920]{1,0:T(8,128)(2,1)S(1)}, u32[]{:S(2)}, u32[]{:S(2)}) %collective-permute-start.4) | collective-permute-done | bytes 860192 | tf_op jit(solution)/shard_map/ppermute | solution.py:35
  49.3 6.0 %first.1 = (bf16[896,384]{1,0:T(8,128)(2,1)S(1)}, bf16[384,640]{1,0:T(8,128)(2,1)S(1)}, f32[384,640]{1,0:T(8,128)S(1)}, f32[384,640]{1,0:T(8,128)S(1)}, bf16[96,...) custom-call(bf16[384,896]{1,0:T(8,128)(2,1)S(1)} %get-tuple-element., ...), custom_call_target="tpu_custom_call" | custom-call | flops 2202009600 | bytes 8650752 | tf_op jit(solution)/shard_map/first/pallas_call | solution.py:68
  57.0 1.5 collective-permute-start.6
  58.6 3.4 %collective-permute-start.7 = (bf16[96,896]{1,0:T(8,128)(2,1)S(1)}, bf16[96,896]{1,0:T(8,128)(2,1)S(1)}, u32[]{:S(2)}, u32[]{:S(2)}) collective-permute-start(bf16[96,896]{1,0:T(8,128)(2,1)S(1)} %get-tuple-element.93), channel_id=1, source_target_pairs={{2,0},{3,1},{0,2},{1,3},{6,4},{7,5},{4,6},{5,7},{10,8},{11,9},{8,1... | collective-permute-start | bytes 516104 | tf_op jit(solution)/shard_map/ppermute | solution.py:40
  62.0 1.5 collective-permute-start.8
  63.5 3.2 %early.2 = (bf16[896,384]{1,0:T(8,128)(2,1)S(1)}, bf16[896,384]{1,0:T(8,128)(2,1)S(1)}, bf16[384,640]{1,0:T(8,128)(2,1)S(1)}, bf16[384,1280]{1,0:T(8,128)(2,1)S(1)}) custom-call(bf16[384,896]{1,0:T(8,128)(2,1)S(1)} %get-tuple-element.86.x, bf16[384,896]{1,0:T(8,128)(2,1)S(1)} %get-tuple-element.168.d, ...), custom_call_target="tpu_custom_call" | custom-call | flops 2202009600 | bytes 7667712 | tf_op jit(solution)/shard_map/early/pallas_call | solution.py:68
  66.7 2.1 collective-permute-done.7.refs_2_
  70.1 1.5 collective-permute-start.11
  73.1 1.8 collective-permute-done.11.refs_6_
  74.9 1.7 collective-permute-done.10.refs_5_
  76.6 1.0 chain.2
  77.7 4.3 %collective-permute-start.14 = (bf16[96,896]{1,0:T(8,128)(2,1)}, bf16[96,896]{1,0:T(8,128)(2,1)}, u32[]{:S(2)}, u32[]{:S(2)}) collective-permute-start(bf16[96,896]{1,0:T(8,128)(2,1)} %get-tuple-element.100), channel_id=1, source_target_pairs={{67,0},{64,1},{65,2},{66,3},{0,64},{1,65},{2,66},{3,67},{71,4},{68... | collective-permute-start | bytes 516104 | tf_op jit(solution)/shard_map/ppermute | solution.py:46
  82.0 2.6 %collective-permute-start.16 = (bf16[96,896]{1,0:T(8,128)(2,1)}, bf16[96,896]{1,0:T(8,128)(2,1)}, u32[]{:S(2)}, u32[]{:S(2)}) collective-permute-start(bf16[96,896]{1,0:T(8,128)(2,1)} %get-tuple-element.102), channel_id=1, source_target_pairs={{65,0},{66,1},{67,2},{64,3},{0,64},{1,65},{2,66},{3,67},{69,4},{70... | collective-permute-start | bytes 516104 | tf_op jit(solution)/shard_map/ppermute | solution.py:46
  84.7 2.0 copy-done
  86.7 4.0 %order.2.weights.ins.refs_0_ = bf16[896,1280]{1,0:T(8,128)(2,1)S(1)} custom-call(bf16[896,896]{1,0:T(8,128)(2,1)S(1)} %fusion.8.mover, bf16[896,1920]{1,0:T(8,128)(2,1)S(1)} %copy-done), custom_call_target="tpu_custom_call" | custom-call | flops 2055208960 | bytes 7340032 | tf_op jit(solution)/shard_map/order/pallas_call | solution.py:68
  90.7 1.4 mix.4.d
  93.4 2.3 %collective-permute-start.18 = (bf16[96,896]{1,0:T(8,128)(2,1)S(1)}, bf16[96,896]{1,0:T(8,128)(2,1)S(1)}, u32[]{:S(2)}, u32[]{:S(2)}) collective-permute-start(bf16[96,896]{1,0:T(8,128)(2,1)S(1)} %mix.4.d), channel_id=1, source_target_pairs={{1,64},{2,65},{3,66},{0,67},{64,0},{65,1},{66,2},{67,3},{5,68},{6,... | collective-permute-start | bytes 516104 | tf_op jit(solution)/shard_map/ppermute | solution.py:46
  95.9 1.5 gate.1
  97.5 1.8 order.3.down.refs_1_.refs_16_
  99.5 3.4 %collective-permute-start.21 = (bf16[96,896]{1,0:T(8,128)(2,1)S(1)}, bf16[96,896]{1,0:T(8,128)(2,1)S(1)}, u32[]{:S(2)}, u32[]{:S(2)}) collective-permute-start(bf16[96,896]{1,0:T(8,128)(2,1)S(1)} %get-tuple-element.107), channel_id=1, source_target_pairs={{64,0},{65,1},{66,2},{67,3},{0,64},{1,65},{2,66},{3,67},{68,4},{69... | collective-permute-start | bytes 516104 | tf_op jit(solution)/shard_map/ppermute | solution.py:46
  103.4 1.4 collective-permute-start.24
  104.9 4.4 %terms.2 = (bf16[224,1920]{1,0:T(8,128)(2,1)S(1)}, bf16[224,1920]{1,0:T(8,128)(2,1)S(1)}, bf16[224,1920]{1,0:T(8,128)(2,1)S(1)}, bf16[224,1920]{1,0:T(8,128)(2,1)S(1)}) custom-call(s32[1]{0:T(128)} %bitcast.4.use_first, bf16[96,896]{1,0:T(8,128)(2,1)S(1)} %get-tuple-element.91.d.refs_0_, bf16[96,896]{1,0:T(8,128)(2,1)S(1)} %copy-done.27, ...), custom_call_target="tpu_custom_call" | custom-call | flops 3082813440 | bytes 14254084 | tf_op jit(solution)/shard_map/terms/pallas_call | solution.py:68
  109.4 1.8 collective-permute-done.23.refs_2_
  111.6 1.6 collective-permute-start.28
  113.2 1.7 collective-permute-start.29
  115.1 3.4 %collective-permute-start.26 = (bf16[96,896]{1,0:T(8,128)(2,1)S(1)}, bf16[96,896]{1,0:T(8,128)(2,1)S(1)}, u32[]{:S(2)}, u32[]{:S(2)}) collective-permute-start(bf16[96,896]{1,0:T(8,128)(2,1)S(1)} %mix.5.refs_4_), channel_id=1, source_target_pairs={{2,0},{3,1},{0,2},{1,3},{6,4},{7,5},{4,6},{5,7},{10,8},{11,9},{8,1... | collective-permute-start | bytes 516104 | tf_op jit(solution)/shard_map/ppermute | solution.py:40
  118.9 2.2 %early.3 = (bf16[896,384]{1,0:T(8,128)(2,1)S(1)}, bf16[896,384]{1,0:T(8,128)(2,1)S(1)}, bf16[384,640]{1,0:T(8,128)(2,1)S(1)}, bf16[384,1280]{1,0:T(8,128)(2,1)S(1)}) custom-call(bf16[384,896]{1,0:T(8,128)(2,1)S(1)} %copy-done.16, bf16[384,896]{1,0:T(8,128)(2,1)S(1)} %copy-done.15, bf16[896,1280]{1,0:T(8,128)(2,1)S(1)} %order.2.weights.ins.refs_0_, ...), custom_call_target="tpu_custom_call" | custom-call | flops 2202009600 | bytes 7667712 | tf_op jit(solution)/shard_map/early/pallas_call | solution.py:68
  121.1 4.4 %collective-permute-done.27.refs_7_ = bf16[96,896]{1,0:T(8,128)(2,1)S(1)} collective-permute-done((bf16[96,896]{1,0:T(8,128)(2,1)S(1)}, bf16[96,896]{1,0:T(8,128)(2,1)S(1)}, u32[]{:S(2)}, u32[]{:S(2)}) %collective-permute-start.27) | collective-permute-done | bytes 172064 | tf_op jit(solution)/shard_map/ppermute | solution.py:40
  126.1 2.9 %collective-permute-start.36 = (bf16[224,1920]{1,0:T(8,128)(2,1)S(1)}, bf16[224,1920]{1,0:T(8,128)(2,1)S(1)}, u32[]{:S(2)}, u32[]{:S(2)}) collective-permute-start(bf16[224,1920]{1,0:T(8,128)(2,1)S(1)} %get-tuple-element.145), channel_id=1, source_target_pairs={{32,0},{36,4},{40,8},{44,12},{48,16},{52,20},{56,24},{60,28},{0,32... | collective-permute-start | bytes 2580488 | tf_op jit(solution)/shard_map/ppermute | solution.py:35
  128.9 3.8 %terms.3 = (bf16[224,1920]{1,0:T(8,128)(2,1)S(1)}, bf16[224,1920]{1,0:T(8,128)(2,1)S(1)}, bf16[224,1920]{1,0:T(8,128)(2,1)S(1)}, bf16[224,1920]{1,0:T(8,128)(2,1)S(1)}) custom-call(s32[1]{0:T(128)S(6)} %sub.36.active.use_first, bf16[96,896]{1,0:T(8,128)(2,1)S(1)} %collective-permute-done.17.refs_0_, bf16[96,896]{1,0:T(8,128)(2,1)S(1)} %collective-permute-done.18.refs_1_, ...), custom_call_target="tpu_custom_call" | custom-call | flops 3082813440 | bytes 11960324 | tf_op jit(solution)/shard_map/terms/pallas_call | solution.py:68
  133.2 2.4 %collective-permute-start.31 = (bf16[224,1920]{1,0:T(8,128)(2,1)S(1)}, bf16[224,1920]{1,0:T(8,128)(2,1)S(1)}, u32[]{:S(2)}, u32[]{:S(2)}) collective-permute-start(bf16[224,1920]{1,0:T(8,128)(2,1)S(1)} %get-tuple-element.137), channel_id=1, source_target_pairs={{32,0},{36,4},{40,8},{44,12},{48,16},{52,20},{56,24},{60,28},{0,32... | collective-permute-start | bytes 2580488 | tf_op jit(solution)/shard_map/ppermute | solution.py:35
  136.1 4.4 %collective-permute-done.36.refs_2_ = bf16[224,1920]{1,0:T(8,128)(2,1)S(1)} collective-permute-done((bf16[224,1920]{1,0:T(8,128)(2,1)S(1)}, bf16[224,1920]{1,0:T(8,128)(2,1)S(1)}, u32[]{:S(2)}, u32[]{:S(2)}) %collective-permute-start.36) | collective-permute-done | bytes 860192 | tf_op jit(solution)/shard_map/ppermute | solution.py:35
  141.0 2.1 %collective-permute-start.38 = (bf16[56,1920]{1,0:T(8,128)(2,1)S(1)}, bf16[56,1920]{1,0:T(8,128)(2,1)S(1)}, u32[]{:S(2)}, u32[]{:S(2)}) collective-permute-start(bf16[56,1920]{1,0:T(8,128)(2,1)S(1)} %get-tuple-element.148), channel_id=1, source_target_pairs={{8,0},{12,4},{0,8},{4,12},{24,16},{28,20},{16,24},{20,28},{40,32},... | collective-permute-start | bytes 645128 | tf_op jit(solution)/shard_map/ppermute | solution.py:35
  143.1 11.1 %collective-permute-done.30.refs_1_ = bf16[224,1920]{1,0:T(8,128)(2,1)S(1)} collective-permute-done((bf16[224,1920]{1,0:T(8,128)(2,1)S(1)}, bf16[224,1920]{1,0:T(8,128)(2,1)S(1)}, u32[]{:S(2)}, u32[]{:S(2)}) %collective-permute-start.30) | collective-permute-done | bytes 860192 | tf_op jit(solution)/shard_map/ppermute | solution.py:35
  154.9 8.6 %collective-permute-done.31.refs_2_ = bf16[224,1920]{1,0:T(8,128)(2,1)S(1)} collective-permute-done((bf16[224,1920]{1,0:T(8,128)(2,1)S(1)}, bf16[224,1920]{1,0:T(8,128)(2,1)S(1)}, u32[]{:S(2)}, u32[]{:S(2)}) %collective-permute-start.31) | collective-permute-done | bytes 860192 | tf_op jit(solution)/shard_map/ppermute | solution.py:35
  163.9 3.0 %collective-permute-start.34 = (bf16[56,1920]{1,0:T(8,128)(2,1)S(1)}, bf16[56,1920]{1,0:T(8,128)(2,1)S(1)}, u32[]{:S(2)}, u32[]{:S(2)}) collective-permute-start(bf16[56,1920]{1,0:T(8,128)(2,1)S(1)} %get-tuple-element.141), channel_id=1, source_target_pairs={{8,0},{12,4},{0,8},{4,12},{24,16},{28,20},{16,24},{20,28},{40,32},... | collective-permute-start | bytes 645128 | tf_op jit(solution)/shard_map/ppermute | solution.py:35
  167.5 5.8 %collective-permute-done.33.refs_1_ = bf16[56,1920]{1,0:T(8,128)(2,1)S(1)} collective-permute-done((bf16[56,1920]{1,0:T(8,128)(2,1)S(1)}, bf16[56,1920]{1,0:T(8,128)(2,1)S(1)}, u32[]{:S(2)}, u32[]{:S(2)}) %collective-permute-start.33) | collective-permute-done | bytes 215072 | tf_op jit(solution)/shard_map/ppermute | solution.py:35
  174.5 1.2 collective-permute-done.40
  175.7 3.8 %collective-permute-start.42 = (f32[8,128]{1,0:T(8,128)S(1)}, f32[8,128]{1,0:T(8,128)S(1)}, u32[]{:S(2)}, u32[]{:S(2)}) collective-permute-start(f32[8,128]{1,0:T(8,128)S(1)} %add.249), channel_id=1, source_target_pairs={{8,0},{12,4},{0,8},{4,12},{24,16},{28,20},{16,24},{20,28},{40,32},... | collective-permute-start | bytes 12296 | tf_op jit(solution)/shard_map/ppermute | solution.py:35
  179.5 1.0 collective-permute-done.43
  181.1 2.0 collective-permute-done.41
  183.1 1.5 collective-permute-start.46
  184.6 2.6 %collective-permute-start.45 = (f32[8,128]{1,0:T(8,128)S(1)}, f32[8,128]{1,0:T(8,128)S(1)}, u32[]{:S(2)}, u32[]{:S(2)}) collective-permute-start(f32[8,128]{1,0:T(8,128)S(1)} %add_add_fusion.2), channel_id=1, source_target_pairs={{32,0},{36,4},{40,8},{44,12},{48,16},{52,20},{56,24},{60,28},{0,32... | collective-permute-start | bytes 12296 | tf_op jit(solution)/shard_map/ppermute | solution.py:35
  187.2 1.9 collective-permute-start.44
  189.7 1.4 collective-permute-done.44
  191.3 3.8 %collective-permute-start.48 = (f32[8,128]{1,0:T(8,128)S(1)}, f32[8,128]{1,0:T(8,128)S(1)}, u32[]{:S(2)}, u32[]{:S(2)}) collective-permute-start(f32[8,128]{1,0:T(8,128)S(1)} %add_add_fusion.1), channel_id=1, source_target_pairs={{2,0},{3,1},{0,2},{1,3},{6,4},{7,5},{4,6},{5,7},{10,8},{11,9},{8,1... | collective-permute-start | bytes 12296 | tf_op jit(solution)/shard_map/ppermute | solution.py:40
  196.7 2.0 collective-permute-done.47
  200.8 1.1 copy.27
  201.9 1.1 copy.26
  203.0 1.3 copy.25
  (189 shorter events, 23.3 us)
Async XLA Ops:
  7.2 77.5 %all-gather.2.cloned.1.call-start = ((), (), s32[]{:S(2)}) async-start(), calls=%async_computation | async-start | bytes 3655680 | tf_op jit(solution)/shard_map/all_gather | solution.py:376
  9.5 19.9 %copy-start.42 = (bf16[1,2,384,896]{3,2,1,0:T(8,128)(2,1)S(1)}, bf16[1,2,384,896]{3,2,1,0:T(8,128)(2,1)}, u32[]{:S(2)}) copy-start(bf16[1,2,384,896]{3,2,1,0:T(8,128)(2,1)} %param.8) | copy-start | bytes 4128772
  9.5 12.3 %collective-permute-start.2 = (bf16[56,1920]{1,0:T(8,128)(2,1)S(1)}, bf16[56,1920]{1,0:T(8,128)(2,1)S(1)}, u32[]{:S(2)}, u32[]{:S(2)}) collective-permute-start(bf16[56,1920]{1,0:T(8,128)(2,1)S(1)} %bitcast.109), channel_id=1, source_target_pairs={{12,0},{0,4},{4,8},{8,12},{28,16},{16,20},{20,24},{24,28},{44,32},... | collective-permute-start | bytes 645128 | tf_op jit(solution)/shard_map/ppermute | solution.py:35
  11.1 9.7 %collective-permute-start.1 = (bf16[56,1920]{1,0:T(8,128)(2,1)S(1)}, bf16[56,1920]{1,0:T(8,128)(2,1)}, u32[]{:S(2)}, u32[]{:S(2)}) collective-permute-start(bf16[56,1920]{1,0:T(8,128)(2,1)S(1)} %bitcast.110), channel_id=1, source_target_pairs={{8,0},{12,4},{0,8},{4,12},{24,16},{28,20},{16,24},{20,28},{40,32},... | collective-permute-start | bytes 645128 | tf_op jit(solution)/shard_map/ppermute | solution.py:35
  13.9 6.0 %collective-permute-start = (bf16[56,1920]{1,0:T(8,128)(2,1)S(1)}, bf16[56,1920]{1,0:T(8,128)(2,1)}, u32[]{:S(2)}, u32[]{:S(2)}) collective-permute-start(bf16[56,1920]{1,0:T(8,128)(2,1)S(1)} %bitcast.111), channel_id=1, source_target_pairs={{4,0},{8,4},{12,8},{0,12},{20,16},{24,20},{28,24},{16,28},{36,32},... | collective-permute-start | bytes 645128 | tf_op jit(solution)/shard_map/ppermute | solution.py:35
  17.9 11.6 %copy-start.41 = (bf16[1,2,2,384,896]{4,3,2,1,0:T(8,128)(2,1)S(1)}, bf16[1,2,2,384,896]{4,3,2,1,0:T(8,128)(2,1)}, u32[]{:S(2)}) copy-start(bf16[1,2,2,384,896]{4,3,2,1,0:T(8,128)(2,1)} %param.7) | copy-start | bytes 8257540
  21.9 54.7 %copy-start.3 = (bf16[224,1920]{1,0:T(8,128)(2,1)}, bf16[224,1920]{1,0:T(8,128)(2,1)S(1)}, u32[]{:S(2)}) copy-start(bf16[224,1920]{1,0:T(8,128)(2,1)S(1)} %constant_dynamic-update-slice_fusion.refs_0_.refs_16_) | copy-start | bytes 2580484
  21.9 18.8 %collective-permute-start.5 = (bf16[224,1920]{1,0:T(8,128)(2,1)S(1)}, bf16[224,1920]{1,0:T(8,128)(2,1)S(1)}, u32[]{:S(2)}, u32[]{:S(2)}) collective-permute-start(bf16[224,1920]{1,0:T(8,128)(2,1)S(1)} %constant_dynamic-update-slice_fusion.refs_0_.refs_16_), channel_id=1, source_target_pairs={{48,0},{52,4},{56,8},{60,12},{0,16},{4,20},{8,24},{12,28},{16,32},... | collective-permute-start | bytes 2580488 | tf_op jit(solution)/shard_map/ppermute | solution.py:35
  23.6 25.7 %collective-permute-start.4 = (bf16[224,1920]{1,0:T(8,128)(2,1)S(1)}, bf16[224,1920]{1,0:T(8,128)(2,1)S(1)}, u32[]{:S(2)}, u32[]{:S(2)}) collective-permute-start(bf16[224,1920]{1,0:T(8,128)(2,1)S(1)} %constant_dynamic-update-slice_fusion.refs_0_.refs_16_), channel_id=1, source_target_pairs={{32,0},{36,4},{40,8},{44,12},{48,16},{52,20},{56,24},{60,28},{0,32... | collective-permute-start | bytes 2580488 | tf_op jit(solution)/shard_map/ppermute | solution.py:35
  26.5 22.8 %collective-permute-start.3 = (bf16[224,1920]{1,0:T(8,128)(2,1)S(1)}, bf16[224,1920]{1,0:T(8,128)(2,1)S(1)}, u32[]{:S(2)}, u32[]{:S(2)}) collective-permute-start(bf16[224,1920]{1,0:T(8,128)(2,1)S(1)} %constant_dynamic-update-slice_fusion.refs_0_.refs_16_), channel_id=1, source_target_pairs={{16,0},{20,4},{24,8},{28,12},{32,16},{36,20},{40,24},{44,28},{48,3... | collective-permute-start | bytes 2580488 | tf_op jit(solution)/shard_map/ppermute | solution.py:35
  40.7 35.9 %copy-start.9 = (bf16[224,1920]{1,0:T(8,128)(2,1)}, bf16[224,1920]{1,0:T(8,128)(2,1)S(1)}, u32[]{:S(2)}) copy-start(bf16[224,1920]{1,0:T(8,128)(2,1)S(1)} %collective-permute-done.5.refs_3_.refs_19_) | copy-start | bytes 2580484
  49.3 27.3 %copy-start.11 = (bf16[224,1920]{1,0:T(8,128)(2,1)}, bf16[224,1920]{1,0:T(8,128)(2,1)S(1)}, u32[]{:S(2)}) copy-start(bf16[224,1920]{1,0:T(8,128)(2,1)S(1)} %collective-permute-done.4.refs_2_.refs_18_) | copy-start | bytes 2580484
  49.3 27.3 %copy-start.13 = (bf16[224,1920]{1,0:T(8,128)(2,1)}, bf16[224,1920]{1,0:T(8,128)(2,1)S(1)}, u32[]{:S(2)}) copy-start(bf16[224,1920]{1,0:T(8,128)(2,1)S(1)} %collective-permute-done.3.refs_1_.refs_17_) | copy-start | bytes 2580484
  57.0 19.6 %copy-start.5 = (f32[384,640]{1,0:T(8,128)}, f32[384,640]{1,0:T(8,128)S(1)}, u32[]{:S(2)}) copy-start(f32[384,640]{1,0:T(8,128)S(1)} %get-tuple-element.95.slope.refs_14_) | copy-start | bytes 2949124
  57.0 19.6 %copy-start.7 = (f32[384,640]{1,0:T(8,128)}, f32[384,640]{1,0:T(8,128)S(1)}, u32[]{:S(2)}) copy-start(f32[384,640]{1,0:T(8,128)S(1)} %get-tuple-element.96.activated.refs_15_) | copy-start | bytes 2949124
  57.0 9.7 %collective-permute-start.6 = (bf16[96,896]{1,0:T(8,128)(2,1)S(1)}, bf16[96,896]{1,0:T(8,128)(2,1)S(1)}, u32[]{:S(2)}, u32[]{:S(2)}) collective-permute-start(bf16[96,896]{1,0:T(8,128)(2,1)S(1)} %get-tuple-element.92), channel_id=1, source_target_pairs={{3,0},{0,1},{1,2},{2,3},{7,4},{4,5},{5,6},{6,7},{11,8},{8,9},{9,10... | collective-permute-start | bytes 516104 | tf_op jit(solution)/shard_map/ppermute | solution.py:40
  58.6 10.3 %collective-permute-start.7 = (bf16[96,896]{1,0:T(8,128)(2,1)S(1)}, bf16[96,896]{1,0:T(8,128)(2,1)S(1)}, u32[]{:S(2)}, u32[]{:S(2)}) collective-permute-start(bf16[96,896]{1,0:T(8,128)(2,1)S(1)} %get-tuple-element.93), channel_id=1, source_target_pairs={{2,0},{3,1},{0,2},{1,3},{6,4},{7,5},{4,6},{5,7},{10,8},{11,9},{8,1... | collective-permute-start | bytes 516104 | tf_op jit(solution)/shard_map/ppermute | solution.py:40
  62.0 6.8 %collective-permute-start.8 = (bf16[96,896]{1,0:T(8,128)(2,1)S(1)}, bf16[96,896]{1,0:T(8,128)(2,1)S(1)}, u32[]{:S(2)}, u32[]{:S(2)}) collective-permute-start(bf16[96,896]{1,0:T(8,128)(2,1)S(1)} %get-tuple-element.94), channel_id=1, source_target_pairs={{1,0},{2,1},{3,2},{0,3},{5,4},{6,5},{7,6},{4,7},{9,8},{10,9},{11,1... | collective-permute-start | bytes 516104 | tf_op jit(solution)/shard_map/ppermute | solution.py:40
  69.2 3.8 %collective-permute-start.12 = (bf16[96,896]{1,0:T(8,128)(2,1)S(1)}, bf16[96,896]{1,0:T(8,128)(2,1)S(1)}, u32[]{:S(2)}, u32[]{:S(2)}) collective-permute-start(bf16[96,896]{1,0:T(8,128)(2,1)S(1)} %mix.3.d), channel_id=1, source_target_pairs={{3,64},{0,65},{1,66},{2,67},{64,0},{65,1},{66,2},{67,3},{7,68},{4,... | collective-permute-start | bytes 516104 | tf_op jit(solution)/shard_map/ppermute | solution.py:46
  70.1 4.8 %collective-permute-start.11 = (bf16[96,896]{1,0:T(8,128)(2,1)S(1)}, bf16[96,896]{1,0:T(8,128)(2,1)S(1)}, u32[]{:S(2)}, u32[]{:S(2)}) collective-permute-start(bf16[96,896]{1,0:T(8,128)(2,1)S(1)} %mix.3.d), channel_id=1, source_target_pairs={{2,64},{3,65},{0,66},{1,67},{64,0},{65,1},{66,2},{67,3},{6,68},{7,... | collective-permute-start | bytes 516104 | tf_op jit(solution)/shard_map/ppermute | solution.py:46
  71.7 4.9 %collective-permute-start.10 = (bf16[96,896]{1,0:T(8,128)(2,1)S(1)}, bf16[96,896]{1,0:T(8,128)(2,1)S(1)}, u32[]{:S(2)}, u32[]{:S(2)}) collective-permute-start(bf16[96,896]{1,0:T(8,128)(2,1)S(1)} %mix.3.d), channel_id=1, source_target_pairs={{1,64},{2,65},{3,66},{0,67},{64,0},{65,1},{66,2},{67,3},{5,68},{6,... | collective-permute-start | bytes 516104 | tf_op jit(solution)/shard_map/ppermute | solution.py:46
  71.8 4.8 %collective-permute-start.9 = (bf16[96,896]{1,0:T(8,128)(2,1)S(1)}, bf16[96,896]{1,0:T(8,128)(2,1)S(1)}, u32[]{:S(2)}, u32[]{:S(2)}) collective-permute-start(bf16[96,896]{1,0:T(8,128)(2,1)S(1)} %mix.3.d), channel_id=1, source_target_pairs={{0,64},{1,65},{2,66},{3,67},{64,0},{65,1},{66,2},{67,3},{4,68},{5,... | collective-permute-start | bytes 516104 | tf_op jit(solution)/shard_map/ppermute | solution.py:46
  77.7 13.0 %collective-permute-start.14 = (bf16[96,896]{1,0:T(8,128)(2,1)}, bf16[96,896]{1,0:T(8,128)(2,1)}, u32[]{:S(2)}, u32[]{:S(2)}) collective-permute-start(bf16[96,896]{1,0:T(8,128)(2,1)} %get-tuple-element.100), channel_id=1, source_target_pairs={{67,0},{64,1},{65,2},{66,3},{0,64},{1,65},{2,66},{3,67},{71,4},{68... | collective-permute-start | bytes 516104 | tf_op jit(solution)/shard_map/ppermute | solution.py:46
  82.0 8.8 %collective-permute-start.15 = (bf16[96,896]{1,0:T(8,128)(2,1)}, bf16[96,896]{1,0:T(8,128)(2,1)}, u32[]{:S(2)}, u32[]{:S(2)}) collective-permute-start(bf16[96,896]{1,0:T(8,128)(2,1)} %get-tuple-element.101), channel_id=1, source_target_pairs={{66,0},{67,1},{64,2},{65,3},{0,64},{1,65},{2,66},{3,67},{70,4},{71... | collective-permute-start | bytes 516104 | tf_op jit(solution)/shard_map/ppermute | solution.py:46
  82.0 8.7 %collective-permute-start.16 = (bf16[96,896]{1,0:T(8,128)(2,1)}, bf16[96,896]{1,0:T(8,128)(2,1)}, u32[]{:S(2)}, u32[]{:S(2)}) collective-permute-start(bf16[96,896]{1,0:T(8,128)(2,1)} %get-tuple-element.102), channel_id=1, source_target_pairs={{65,0},{66,1},{67,2},{64,3},{0,64},{1,65},{2,66},{3,67},{69,4},{70... | collective-permute-start | bytes 516104 | tf_op jit(solution)/shard_map/ppermute | solution.py:46
  84.7 6.1 %collective-permute-start.13 = (bf16[96,896]{1,0:T(8,128)(2,1)}, bf16[96,896]{1,0:T(8,128)(2,1)}, u32[]{:S(2)}, u32[]{:S(2)}) collective-permute-start(bf16[96,896]{1,0:T(8,128)(2,1)} %get-tuple-element.97), channel_id=1, source_target_pairs={{64,0},{65,1},{66,2},{67,3},{0,64},{1,65},{2,66},{3,67},{68,4},{69... | collective-permute-start | bytes 516104 | tf_op jit(solution)/shard_map/ppermute | solution.py:46
  92.2 7.1 %collective-permute-start.20 = (bf16[96,896]{1,0:T(8,128)(2,1)S(1)}, bf16[96,896]{1,0:T(8,128)(2,1)S(1)}, u32[]{:S(2)}, u32[]{:S(2)}) collective-permute-start(bf16[96,896]{1,0:T(8,128)(2,1)S(1)} %mix.4.d), channel_id=1, source_target_pairs={{3,64},{0,65},{1,66},{2,67},{64,0},{65,1},{66,2},{67,3},{7,68},{4,... | collective-permute-start | bytes 516104 | tf_op jit(solution)/shard_map/ppermute | solution.py:46
  93.0 6.3 %collective-permute-start.19 = (bf16[96,896]{1,0:T(8,128)(2,1)S(1)}, bf16[96,896]{1,0:T(8,128)(2,1)S(1)}, u32[]{:S(2)}, u32[]{:S(2)}) collective-permute-start(bf16[96,896]{1,0:T(8,128)(2,1)S(1)} %mix.4.d), channel_id=1, source_target_pairs={{2,64},{3,65},{0,66},{1,67},{64,0},{65,1},{66,2},{67,3},{6,68},{7,... | collective-permute-start | bytes 516104 | tf_op jit(solution)/shard_map/ppermute | solution.py:46
  93.4 5.9 %collective-permute-start.18 = (bf16[96,896]{1,0:T(8,128)(2,1)S(1)}, bf16[96,896]{1,0:T(8,128)(2,1)S(1)}, u32[]{:S(2)}, u32[]{:S(2)}) collective-permute-start(bf16[96,896]{1,0:T(8,128)(2,1)S(1)} %mix.4.d), channel_id=1, source_target_pairs={{1,64},{2,65},{3,66},{0,67},{64,0},{65,1},{66,2},{67,3},{5,68},{6,... | collective-permute-start | bytes 516104 | tf_op jit(solution)/shard_map/ppermute | solution.py:46
  95.7 3.6 %collective-permute-start.17 = (bf16[96,896]{1,0:T(8,128)(2,1)S(1)}, bf16[96,896]{1,0:T(8,128)(2,1)S(1)}, u32[]{:S(2)}, u32[]{:S(2)}) collective-permute-start(bf16[96,896]{1,0:T(8,128)(2,1)S(1)} %mix.4.d), channel_id=1, source_target_pairs={{0,64},{1,65},{2,66},{3,67},{64,0},{65,1},{66,2},{67,3},{4,68},{5,... | collective-permute-start | bytes 516104 | tf_op jit(solution)/shard_map/ppermute | solution.py:46
  99.5 11.7 %collective-permute-start.21 = (bf16[96,896]{1,0:T(8,128)(2,1)S(1)}, bf16[96,896]{1,0:T(8,128)(2,1)S(1)}, u32[]{:S(2)}, u32[]{:S(2)}) collective-permute-start(bf16[96,896]{1,0:T(8,128)(2,1)S(1)} %get-tuple-element.107), channel_id=1, source_target_pairs={{64,0},{65,1},{66,2},{67,3},{0,64},{1,65},{2,66},{3,67},{68,4},{69... | collective-permute-start | bytes 516104 | tf_op jit(solution)/shard_map/ppermute | solution.py:46
  103.0 6.4 %collective-permute-start.22 = (bf16[96,896]{1,0:T(8,128)(2,1)S(1)}, bf16[96,896]{1,0:T(8,128)(2,1)S(1)}, u32[]{:S(2)}, u32[]{:S(2)}) collective-permute-start(bf16[96,896]{1,0:T(8,128)(2,1)S(1)} %get-tuple-element.116), channel_id=1, source_target_pairs={{67,0},{64,1},{65,2},{66,3},{0,64},{1,65},{2,66},{3,67},{71,4},{68... | collective-permute-start | bytes 516104 | tf_op jit(solution)/shard_map/ppermute | solution.py:46
  103.0 8.2 %collective-permute-start.23 = (bf16[96,896]{1,0:T(8,128)(2,1)S(1)}, bf16[96,896]{1,0:T(8,128)(2,1)S(1)}, u32[]{:S(2)}, u32[]{:S(2)}) collective-permute-start(bf16[96,896]{1,0:T(8,128)(2,1)S(1)} %get-tuple-element.117), channel_id=1, source_target_pairs={{66,0},{67,1},{64,2},{65,3},{0,64},{1,65},{2,66},{3,67},{70,4},{71... | collective-permute-start | bytes 516104 | tf_op jit(solution)/shard_map/ppermute | solution.py:46
  103.4 7.8 %collective-permute-start.24 = (bf16[96,896]{1,0:T(8,128)(2,1)S(1)}, bf16[96,896]{1,0:T(8,128)(2,1)S(1)}, u32[]{:S(2)}, u32[]{:S(2)}) collective-permute-start(bf16[96,896]{1,0:T(8,128)(2,1)S(1)} %get-tuple-element.118), channel_id=1, source_target_pairs={{65,0},{66,1},{67,2},{64,3},{0,64},{1,65},{2,66},{3,67},{69,4},{70... | collective-permute-start | bytes 516104 | tf_op jit(solution)/shard_map/ppermute | solution.py:46
  104.9 14.0 %copy-start.15 = (bf16[384,896]{1,0:T(8,128)(2,1)S(1)}, bf16[384,896]{1,0:T(8,128)(2,1)}, u32[]{:S(2)}) copy-start(bf16[384,896]{1,0:T(8,128)(2,1)} %get-tuple-element.167.d) | copy-start | bytes 2064388
  104.9 14.0 %copy-start.16 = (bf16[384,896]{1,0:T(8,128)(2,1)S(1)}, bf16[384,896]{1,0:T(8,128)(2,1)}, u32[]{:S(2)}) copy-start(bf16[384,896]{1,0:T(8,128)(2,1)} %get-tuple-element.119.x) | copy-start | bytes 2064388
  111.6 17.3 %collective-permute-start.28 = (bf16[224,1920]{1,0:T(8,128)(2,1)S(1)}, bf16[224,1920]{1,0:T(8,128)(2,1)S(1)}, u32[]{:S(2)}, u32[]{:S(2)}) collective-permute-start(bf16[224,1920]{1,0:T(8,128)(2,1)S(1)} %get-tuple-element.127), channel_id=1, source_target_pairs={{48,0},{52,4},{56,8},{60,12},{0,16},{4,20},{8,24},{12,28},{16,32},... | collective-permute-start | bytes 2580488 | tf_op jit(solution)/shard_map/ppermute | solution.py:35
  113.2 15.7 %collective-permute-start.29 = (bf16[224,1920]{1,0:T(8,128)(2,1)S(1)}, bf16[224,1920]{1,0:T(8,128)(2,1)S(1)}, u32[]{:S(2)}, u32[]{:S(2)}) collective-permute-start(bf16[224,1920]{1,0:T(8,128)(2,1)S(1)} %get-tuple-element.128), channel_id=1, source_target_pairs={{16,0},{20,4},{24,8},{28,12},{32,16},{36,20},{40,24},{44,28},{48,3... | collective-permute-start | bytes 2580488 | tf_op jit(solution)/shard_map/ppermute | solution.py:35
  114.9 10.5 %collective-permute-start.27 = (bf16[96,896]{1,0:T(8,128)(2,1)S(1)}, bf16[96,896]{1,0:T(8,128)(2,1)S(1)}, u32[]{:S(2)}, u32[]{:S(2)}) collective-permute-start(bf16[96,896]{1,0:T(8,128)(2,1)S(1)} %mix.5.refs_4_), channel_id=1, source_target_pairs={{3,0},{0,1},{1,2},{2,3},{7,4},{4,5},{5,6},{6,7},{11,8},{8,9},{9,10... | collective-permute-start | bytes 516104 | tf_op jit(solution)/shard_map/ppermute | solution.py:40
  115.1 10.3 %collective-permute-start.26 = (bf16[96,896]{1,0:T(8,128)(2,1)S(1)}, bf16[96,896]{1,0:T(8,128)(2,1)S(1)}, u32[]{:S(2)}, u32[]{:S(2)}) collective-permute-start(bf16[96,896]{1,0:T(8,128)(2,1)S(1)} %mix.5.refs_4_), channel_id=1, source_target_pairs={{2,0},{3,1},{0,2},{1,3},{6,4},{7,5},{4,6},{5,7},{10,8},{11,9},{8,1... | collective-permute-start | bytes 516104 | tf_op jit(solution)/shard_map/ppermute | solution.py:40
  118.5 7.6 %collective-permute-start.25 = (bf16[96,896]{1,0:T(8,128)(2,1)S(1)}, bf16[96,896]{1,0:T(8,128)(2,1)S(1)}, u32[]{:S(2)}, u32[]{:S(2)}) collective-permute-start(bf16[96,896]{1,0:T(8,128)(2,1)S(1)} %mix.5.refs_4_), channel_id=1, source_target_pairs={{1,0},{2,1},{3,2},{0,3},{5,4},{6,5},{7,6},{4,7},{9,8},{10,9},{11,1... | collective-permute-start | bytes 516104 | tf_op jit(solution)/shard_map/ppermute | solution.py:40
  126.1 14.4 %collective-permute-start.36 = (bf16[224,1920]{1,0:T(8,128)(2,1)S(1)}, bf16[224,1920]{1,0:T(8,128)(2,1)S(1)}, u32[]{:S(2)}, u32[]{:S(2)}) collective-permute-start(bf16[224,1920]{1,0:T(8,128)(2,1)S(1)} %get-tuple-element.145), channel_id=1, source_target_pairs={{32,0},{36,4},{40,8},{44,12},{48,16},{52,20},{56,24},{60,28},{0,32... | collective-permute-start | bytes 2580488 | tf_op jit(solution)/shard_map/ppermute | solution.py:35
  132.7 21.5 %collective-permute-start.30 = (bf16[224,1920]{1,0:T(8,128)(2,1)S(1)}, bf16[224,1920]{1,0:T(8,128)(2,1)S(1)}, u32[]{:S(2)}, u32[]{:S(2)}) collective-permute-start(bf16[224,1920]{1,0:T(8,128)(2,1)S(1)} %get-tuple-element.136), channel_id=1, source_target_pairs={{48,0},{52,4},{56,8},{60,12},{0,16},{4,20},{8,24},{12,28},{16,32},... | collective-permute-start | bytes 2580488 | tf_op jit(solution)/shard_map/ppermute | solution.py:35
  133.2 30.2 %collective-permute-start.31 = (bf16[224,1920]{1,0:T(8,128)(2,1)S(1)}, bf16[224,1920]{1,0:T(8,128)(2,1)S(1)}, u32[]{:S(2)}, u32[]{:S(2)}) collective-permute-start(bf16[224,1920]{1,0:T(8,128)(2,1)S(1)} %get-tuple-element.137), channel_id=1, source_target_pairs={{32,0},{36,4},{40,8},{44,12},{48,16},{52,20},{56,24},{60,28},{0,32... | collective-permute-start | bytes 2580488 | tf_op jit(solution)/shard_map/ppermute | solution.py:35
  135.6 27.9 %collective-permute-start.32 = (bf16[224,1920]{1,0:T(8,128)(2,1)S(1)}, bf16[224,1920]{1,0:T(8,128)(2,1)S(1)}, u32[]{:S(2)}, u32[]{:S(2)}) collective-permute-start(bf16[224,1920]{1,0:T(8,128)(2,1)S(1)} %get-tuple-element.138), channel_id=1, source_target_pairs={{16,0},{20,4},{24,8},{28,12},{32,16},{36,20},{40,24},{44,28},{48,3... | collective-permute-start | bytes 2580488 | tf_op jit(solution)/shard_map/ppermute | solution.py:35
  140.9 26.1 %collective-permute-start.37 = (bf16[56,1920]{1,0:T(8,128)(2,1)S(1)}, bf16[56,1920]{1,0:T(8,128)(2,1)S(1)}, u32[]{:S(2)}, u32[]{:S(2)}) collective-permute-start(bf16[56,1920]{1,0:T(8,128)(2,1)S(1)} %get-tuple-element.147), channel_id=1, source_target_pairs={{12,0},{0,4},{4,8},{8,12},{28,16},{16,20},{20,24},{24,28},{44,32},... | collective-permute-start | bytes 645128 | tf_op jit(solution)/shard_map/ppermute | solution.py:35
  141.0 26.2 %collective-permute-start.38 = (bf16[56,1920]{1,0:T(8,128)(2,1)S(1)}, bf16[56,1920]{1,0:T(8,128)(2,1)S(1)}, u32[]{:S(2)}, u32[]{:S(2)}) collective-permute-start(bf16[56,1920]{1,0:T(8,128)(2,1)S(1)} %get-tuple-element.148), channel_id=1, source_target_pairs={{8,0},{12,4},{0,8},{4,12},{24,16},{28,20},{16,24},{20,28},{40,32},... | collective-permute-start | bytes 645128 | tf_op jit(solution)/shard_map/ppermute | solution.py:35
  154.2 13.0 %collective-permute-start.39 = (bf16[56,1920]{1,0:T(8,128)(2,1)S(1)}, bf16[56,1920]{1,0:T(8,128)(2,1)S(1)}, u32[]{:S(2)}, u32[]{:S(2)}) collective-permute-start(bf16[56,1920]{1,0:T(8,128)(2,1)S(1)} %get-tuple-element.149), channel_id=1, source_target_pairs={{4,0},{8,4},{12,8},{0,12},{20,16},{24,20},{28,24},{16,28},{36,32},... | collective-permute-start | bytes 645128 | tf_op jit(solution)/shard_map/ppermute | solution.py:35
  163.9 9.5 %collective-permute-start.33 = (bf16[56,1920]{1,0:T(8,128)(2,1)S(1)}, bf16[56,1920]{1,0:T(8,128)(2,1)S(1)}, u32[]{:S(2)}, u32[]{:S(2)}) collective-permute-start(bf16[56,1920]{1,0:T(8,128)(2,1)S(1)} %get-tuple-element.140), channel_id=1, source_target_pairs={{12,0},{0,4},{4,8},{8,12},{28,16},{16,20},{20,24},{24,28},{44,32},... | collective-permute-start | bytes 645128 | tf_op jit(solution)/shard_map/ppermute | solution.py:35
  163.9 9.4 %collective-permute-start.34 = (bf16[56,1920]{1,0:T(8,128)(2,1)S(1)}, bf16[56,1920]{1,0:T(8,128)(2,1)S(1)}, u32[]{:S(2)}, u32[]{:S(2)}) collective-permute-start(bf16[56,1920]{1,0:T(8,128)(2,1)S(1)} %get-tuple-element.141), channel_id=1, source_target_pairs={{8,0},{12,4},{0,8},{4,12},{24,16},{28,20},{16,24},{20,28},{40,32},... | collective-permute-start | bytes 645128 | tf_op jit(solution)/shard_map/ppermute | solution.py:35
  167.0 7.2 %collective-permute-start.35 = (bf16[56,1920]{1,0:T(8,128)(2,1)S(1)}, bf16[56,1920]{1,0:T(8,128)(2,1)S(1)}, u32[]{:S(2)}, u32[]{:S(2)}) collective-permute-start(bf16[56,1920]{1,0:T(8,128)(2,1)S(1)} %get-tuple-element.142), channel_id=1, source_target_pairs={{4,0},{8,4},{12,8},{0,12},{20,16},{24,20},{28,24},{16,28},{36,32},... | collective-permute-start | bytes 645128 | tf_op jit(solution)/shard_map/ppermute | solution.py:35
  167.4 32.5 %copy-start.40 = (f32[1,56,2,3,640]{4,2,3,1,0:T(2,128)S(1)}, f32[1,56,2,3,640]{4,2,3,1,0:T(2,128)}, u32[]{:S(2)}) copy-start(f32[1,56,2,3,640]{4,2,3,1,0:T(2,128)} %param.11) | copy-start | bytes 2580484
  167.5 32.5 %copy-start.43 = (bf16[1,56,2,3,640]{4,2,3,1,0:T(2,128)(2,1)S(1)}, bf16[1,56,2,3,640]{4,2,3,1,0:T(2,128)(2,1)}, u32[]{:S(2)}) copy-start(bf16[1,56,2,3,640]{4,2,3,1,0:T(2,128)(2,1)} %param.13) | copy-start | bytes 1290244
  167.5 32.5 %copy-start.44 = (bf16[1,56,2,3,640]{4,2,3,1,0:T(2,128)(2,1)S(1)}, bf16[1,56,2,3,640]{4,2,3,1,0:T(2,128)(2,1)}, u32[]{:S(2)}) copy-start(bf16[1,56,2,3,640]{4,2,3,1,0:T(2,128)(2,1)} %param.12) | copy-start | bytes 1290244
  174.5 1.2 collective-permute-start.40
  175.7 4.8 %collective-permute-start.43 = (f32[8,128]{1,0:T(8,128)S(1)}, f32[8,128]{1,0:T(8,128)S(1)}, u32[]{:S(2)}, u32[]{:S(2)}) collective-permute-start(f32[8,128]{1,0:T(8,128)S(1)} %add.249), channel_id=1, source_target_pairs={{12,0},{0,4},{4,8},{8,12},{28,16},{16,20},{20,24},{24,28},{44,32},... | collective-permute-start | bytes 12296 | tf_op jit(solution)/shard_map/ppermute | solution.py:35
  175.7 5.4 %collective-permute-start.42 = (f32[8,128]{1,0:T(8,128)S(1)}, f32[8,128]{1,0:T(8,128)S(1)}, u32[]{:S(2)}, u32[]{:S(2)}) collective-permute-start(f32[8,128]{1,0:T(8,128)S(1)} %add.249), channel_id=1, source_target_pairs={{8,0},{12,4},{0,8},{4,12},{24,16},{28,20},{16,24},{20,28},{40,32},... | collective-permute-start | bytes 12296 | tf_op jit(solution)/shard_map/ppermute | solution.py:35
  179.5 3.6 %collective-permute-start.41 = (f32[8,128]{1,0:T(8,128)S(1)}, f32[8,128]{1,0:T(8,128)S(1)}, u32[]{:S(2)}, u32[]{:S(2)}) collective-permute-start(f32[8,128]{1,0:T(8,128)S(1)} %add.249), channel_id=1, source_target_pairs={{4,0},{8,4},{12,8},{0,12},{20,16},{24,20},{28,24},{16,28},{36,32},... | collective-permute-start | bytes 12296 | tf_op jit(solution)/shard_map/ppermute | solution.py:35
  183.1 6.0 %collective-permute-start.46 = (f32[8,128]{1,0:T(8,128)S(1)}, f32[8,128]{1,0:T(8,128)S(1)}, u32[]{:S(2)}, u32[]{:S(2)}) collective-permute-start(f32[8,128]{1,0:T(8,128)S(1)} %add_add_fusion.2), channel_id=1, source_target_pairs={{48,0},{52,4},{56,8},{60,12},{0,16},{4,20},{8,24},{12,28},{16,32},... | collective-permute-start | bytes 12296 | tf_op jit(solution)/shard_map/ppermute | solution.py:35
  184.6 5.1 %collective-permute-start.45 = (f32[8,128]{1,0:T(8,128)S(1)}, f32[8,128]{1,0:T(8,128)S(1)}, u32[]{:S(2)}, u32[]{:S(2)}) collective-permute-start(f32[8,128]{1,0:T(8,128)S(1)} %add_add_fusion.2), channel_id=1, source_target_pairs={{32,0},{36,4},{40,8},{44,12},{48,16},{52,20},{56,24},{60,28},{0,32... | collective-permute-start | bytes 12296 | tf_op jit(solution)/shard_map/ppermute | solution.py:35
  187.2 3.8 %collective-permute-start.44 = (f32[8,128]{1,0:T(8,128)S(1)}, f32[8,128]{1,0:T(8,128)S(1)}, u32[]{:S(2)}, u32[]{:S(2)}) collective-permute-start(f32[8,128]{1,0:T(8,128)S(1)} %add_add_fusion.2), channel_id=1, source_target_pairs={{16,0},{20,4},{24,8},{28,12},{32,16},{36,20},{40,24},{44,28},{48,3... | collective-permute-start | bytes 12296 | tf_op jit(solution)/shard_map/ppermute | solution.py:35
  191.0 4.8 %collective-permute-start.49 = (f32[8,128]{1,0:T(8,128)S(1)}, f32[8,128]{1,0:T(8,128)S(1)}, u32[]{:S(2)}, u32[]{:S(2)}) collective-permute-start(f32[8,128]{1,0:T(8,128)S(1)} %add_add_fusion.1), channel_id=1, source_target_pairs={{3,0},{0,1},{1,2},{2,3},{7,4},{4,5},{5,6},{6,7},{11,8},{8,9},{9,10... | collective-permute-start | bytes 12296 | tf_op jit(solution)/shard_map/ppermute | solution.py:40
  191.3 5.4 %collective-permute-start.48 = (f32[8,128]{1,0:T(8,128)S(1)}, f32[8,128]{1,0:T(8,128)S(1)}, u32[]{:S(2)}, u32[]{:S(2)}) collective-permute-start(f32[8,128]{1,0:T(8,128)S(1)} %add_add_fusion.1), channel_id=1, source_target_pairs={{2,0},{3,1},{0,2},{1,3},{6,4},{7,5},{4,6},{5,7},{10,8},{11,9},{8,1... | collective-permute-start | bytes 12296 | tf_op jit(solution)/shard_map/ppermute | solution.py:40
  195.1 3.6 %collective-permute-start.47 = (f32[8,128]{1,0:T(8,128)S(1)}, f32[8,128]{1,0:T(8,128)S(1)}, u32[]{:S(2)}, u32[]{:S(2)}) collective-permute-start(f32[8,128]{1,0:T(8,128)S(1)} %add_add_fusion.1), channel_id=1, source_target_pairs={{1,0},{2,1},{3,2},{0,3},{5,4},{6,5},{7,6},{4,7},{9,8},{10,9},{11,1... | collective-permute-start | bytes 12296 | tf_op jit(solution)/shard_map/ppermute | solution.py:40
  (33 other events, 181.8 us)
Sparse Core Ops, SparseCore 0:
  10.7 64.5 all-gather.1

commit v2 on v1

--- a/solution.py
+++ b/solution.py
@@ -337,8 +337,16 @@
 
 def summed_everywhere(value):
     value = value + from_other_core(value)
-    value = total_of([value] + peers(lambda by: from_plane(value, by, True)))
-    value = total_of([value] + peers(lambda by: from_plane(value, by, False)))
+    for stride in (1, SIDE):
+
+        def along(by):
+            pairs = []
+            for i in range(SIDE * SIDE):
+                at = i // stride % SIDE
+                pairs.append((i + ((at + by) % SIDE - at) * stride, i))
+            return lax.ppermute(value, "dp", pairs)
+
+        value = total_of([value] + peers(along))
     return total_of([value] + peers(lambda by: from_z(value, by)))[0, 0]
 
 

time: 215 us -> 215 us (level)
    ppermute x0 -> x6, starting transfers between devices: none -> 9.82 us  [along(): return lax.ppermute(value, 'dp', pairs)]
    ppermute x24 -> x18, starting transfers between devices: 37.6 us -> 27.8 us  [from_plane(): return lax.ppermute(value, ('pipe', 'dp'), pairs)]
    ppermute x0 -> x6, waiting for transfers between devices: none -> 5.5 us  [along(): return lax.ppermute(value, 'dp', pairs)]
    ppermute x24 -> x18, waiting for transfers between devices: 46.9 us -> 41.4 us  [from_plane(): return lax.ppermute(value, ('pipe', 'dp'), pairs)]
where the time goes in v2:
time: 215 us; the launch traced here: 211 us
  starting transfers between devices  71.1 us (33%)
  waiting for transfers between devices  64.2 us (30%)
  Pallas kernels  31.5 us (15%)
  local copies, waits for them, and re-layouts  17.8 us (8%)
  between operations  16 us (7%)
  matrix products  7.74 us (4%)
  other arithmetic  3.23 us (2%)
    ppermute x18, waiting for transfers between devices, from_plane(): return lax.ppermute(value, ('pipe', 'dp'), pairs)  41.4 us
    pallas_call x17, Pallas kernels, run(): pl.pallas_call(kernel, out_shape=[jax.ShapeDtypeStruct(o[0], o[1]) for o...  31.5 us
    ppermute x18, starting transfers between devices, from_plane(): return lax.ppermute(value, ('pipe', 'dp'), pairs)  27.8 us
    ppermute x16, starting transfers between devices, across(): return lax.ppermute(value, ('pipe', 'tensor'), pairs)  18.9 us
    ppermute x9, starting transfers between devices, from_z(): return lax.ppermute(value, 'tensor', pairs)  14.5 us
    unnamed x101, local copies, waits for them, and re-layouts  11.2 us
    ppermute x9, waiting for transfers between devices, from_z(): return lax.ppermute(value, 'tensor', pairs)  10.2 us
    ppermute x6, starting transfers between devices, along(): return lax.ppermute(value, 'dp', pairs)  9.82 us
  transfers between devices with their start and end apart: 51, of which 23 were waited for; matrix products, arithmetic and copies ran while one was open for 8% of the time, Pallas kernels for 14%

profile of v2, /device:TPU:0, one launch (start us, length us, event | category | flops | bytes accessed | tf_op | source)
XLA Modules:
  0.0 211.5 jit_solution(1921377725035877242)
XLA Ops:
  7.2 1.2 copy.43
  9.5 1.6 collective-permute-start.2
  11.1 2.7 %collective-permute-start.1 = (bf16[56,1920]{1,0:T(8,128)(2,1)S(1)}, bf16[56,1920]{1,0:T(8,128)(2,1)}, u32[]{:S(2)}, u32[]{:S(2)}) collective-permute-start(bf16[56,1920]{1,0:T(8,128)(2,1)S(1)} %bitcast.110), channel_id=1, source_target_pairs={{8,0},{12,4},{0,8},{4,12},{24,16},{28,20},{16,24},{20,28},{40,32},... | collective-permute-start | bytes 645128 | tf_op jit(solution)/shard_map/ppermute | solution.py:35
  13.9 1.4 collective-permute-start
  15.9 1.4 broadcast_compare_fusion
  18.0 2.0 collective-permute-done
  21.9 1.7 collective-permute-start.5
  23.6 2.9 %collective-permute-start.4 = (bf16[224,1920]{1,0:T(8,128)(2,1)S(1)}, bf16[224,1920]{1,0:T(8,128)(2,1)S(1)}, u32[]{:S(2)}, u32[]{:S(2)}) collective-permute-start(bf16[224,1920]{1,0:T(8,128)(2,1)S(1)} %constant_dynamic-update-slice_fusion.refs_0_.refs_16_), channel_id=1, source_target_pairs={{32,0},{36,4},{40,8},{44,12},{48,16},{52,20},{56,24},{60,28},{0,32... | collective-permute-start | bytes 2580488 | tf_op jit(solution)/shard_map/ppermute | solution.py:35
  26.5 1.6 collective-permute-start.3
  28.1 1.2 constant_dynamic-slice_fusion.3
  29.8 1.0 fusion.35.d
  31.6 1.8 broadcast_select_fusion
  34.4 4.9 %fusion.16 = bf16[2,2,384,896]{3,2,1,0:T(8,128)(2,1)S(1)} fusion(bf16[2,2,96,896]{3,2,1,0:T(8,128)(2,1)S(1)} %get-tuple-element.164, bf16[2,2,96,896]{3,2,1,0:T(8,128)(2,1)S(1)} %get-tuple-element.165, bf16[2,2,96,896]{3,2,1,0:T(8,128)(2,1)S(1)} %get-tuple-element.166, bf16[2,2,96,896]{3,2,1,0:T(8,128)(2,1)S(1)} %get-tuple-element.163, s32[896]{0:T(1024)S(1)} %fusion.61), kind=kOutput, calls=%fused_computation.17 | convolution fusion | flops 2479439872 | bytes 5508608 | tf_op jit(solution)/shard_map/dot_general | solution.py:408
  39.3 1.3 slice_bitcast_fusion.1
  40.7 8.6 %collective-permute-done.4.refs_2_.refs_18_ = bf16[224,1920]{1,0:T(8,128)(2,1)S(1)} collective-permute-done((bf16[224,1920]{1,0:T(8,128)(2,1)S(1)}, bf16[224,1920]{1,0:T(8,128)(2,1)S(1)}, u32[]{:S(2)}, u32[]{:S(2)}) %collective-permute-start.4) | collective-permute-done | bytes 860192 | tf_op jit(solution)/shard_map/ppermute | solution.py:35
  49.3 6.0 %first.1 = (bf16[896,384]{1,0:T(8,128)(2,1)S(1)}, bf16[384,640]{1,0:T(8,128)(2,1)S(1)}, f32[384,640]{1,0:T(8,128)S(1)}, f32[384,640]{1,0:T(8,128)S(1)}, bf16[96,...) custom-call(bf16[384,896]{1,0:T(8,128)(2,1)S(1)} %get-tuple-element., ...), custom_call_target="tpu_custom_call" | custom-call | flops 2202009600 | bytes 8650752 | tf_op jit(solution)/shard_map/first/pallas_call | solution.py:68
  57.0 1.5 collective-permute-start.6
  58.6 3.4 %collective-permute-start.7 = (bf16[96,896]{1,0:T(8,128)(2,1)S(1)}, bf16[96,896]{1,0:T(8,128)(2,1)S(1)}, u32[]{:S(2)}, u32[]{:S(2)}) collective-permute-start(bf16[96,896]{1,0:T(8,128)(2,1)S(1)} %get-tuple-element.93), channel_id=1, source_target_pairs={{2,0},{3,1},{0,2},{1,3},{6,4},{7,5},{4,6},{5,7},{10,8},{11,9},{8,1... | collective-permute-start | bytes 516104 | tf_op jit(solution)/shard_map/ppermute | solution.py:40
  62.0 1.5 collective-permute-start.8
  63.5 3.2 %early.2 = (bf16[896,384]{1,0:T(8,128)(2,1)S(1)}, bf16[896,384]{1,0:T(8,128)(2,1)S(1)}, bf16[384,640]{1,0:T(8,128)(2,1)S(1)}, bf16[384,1280]{1,0:T(8,128)(2,1)S(1)}) custom-call(bf16[384,896]{1,0:T(8,128)(2,1)S(1)} %get-tuple-element.86.x, bf16[384,896]{1,0:T(8,128)(2,1)S(1)} %get-tuple-element.168.d, ...), custom_call_target="tpu_custom_call" | custom-call | flops 2202009600 | bytes 7667712 | tf_op jit(solution)/shard_map/early/pallas_call | solution.py:68
  66.7 2.1 collective-permute-done.7.refs_2_
  70.1 1.5 collective-permute-start.11
  73.1 1.8 collective-permute-done.11.refs_6_
  74.9 1.7 collective-permute-done.10.refs_5_
  76.6 1.0 chain.2
  77.7 4.3 %collective-permute-start.14 = (bf16[96,896]{1,0:T(8,128)(2,1)}, bf16[96,896]{1,0:T(8,128)(2,1)}, u32[]{:S(2)}, u32[]{:S(2)}) collective-permute-start(bf16[96,896]{1,0:T(8,128)(2,1)} %get-tuple-element.100), channel_id=1, source_target_pairs={{67,0},{64,1},{65,2},{66,3},{0,64},{1,65},{2,66},{3,67},{71,4},{68... | collective-permute-start | bytes 516104 | tf_op jit(solution)/shard_map/ppermute | solution.py:46
  82.0 2.6 %collective-permute-start.16 = (bf16[96,896]{1,0:T(8,128)(2,1)}, bf16[96,896]{1,0:T(8,128)(2,1)}, u32[]{:S(2)}, u32[]{:S(2)}) collective-permute-start(bf16[96,896]{1,0:T(8,128)(2,1)} %get-tuple-element.102), channel_id=1, source_target_pairs={{65,0},{66,1},{67,2},{64,3},{0,64},{1,65},{2,66},{3,67},{69,4},{70... | collective-permute-start | bytes 516104 | tf_op jit(solution)/shard_map/ppermute | solution.py:46
  84.7 2.0 copy-done
  86.7 4.0 %order.2.weights.ins.refs_0_ = bf16[896,1280]{1,0:T(8,128)(2,1)S(1)} custom-call(bf16[896,896]{1,0:T(8,128)(2,1)S(1)} %fusion.8.mover, bf16[896,1920]{1,0:T(8,128)(2,1)S(1)} %copy-done), custom_call_target="tpu_custom_call" | custom-call | flops 2055208960 | bytes 7340032 | tf_op jit(solution)/shard_map/order/pallas_call | solution.py:68
  90.7 1.4 mix.4.d
  93.4 2.3 %collective-permute-start.18 = (bf16[96,896]{1,0:T(8,128)(2,1)S(1)}, bf16[96,896]{1,0:T(8,128)(2,1)S(1)}, u32[]{:S(2)}, u32[]{:S(2)}) collective-permute-start(bf16[96,896]{1,0:T(8,128)(2,1)S(1)} %mix.4.d), channel_id=1, source_target_pairs={{1,64},{2,65},{3,66},{0,67},{64,0},{65,1},{66,2},{67,3},{5,68},{6,... | collective-permute-start | bytes 516104 | tf_op jit(solution)/shard_map/ppermute | solution.py:46
  95.9 1.5 gate.1
  97.5 1.8 order.3.down.refs_1_.refs_16_
  99.5 3.4 %collective-permute-start.21 = (bf16[96,896]{1,0:T(8,128)(2,1)S(1)}, bf16[96,896]{1,0:T(8,128)(2,1)S(1)}, u32[]{:S(2)}, u32[]{:S(2)}) collective-permute-start(bf16[96,896]{1,0:T(8,128)(2,1)S(1)} %get-tuple-element.107), channel_id=1, source_target_pairs={{64,0},{65,1},{66,2},{67,3},{0,64},{1,65},{2,66},{3,67},{68,4},{69... | collective-permute-start | bytes 516104 | tf_op jit(solution)/shard_map/ppermute | solution.py:46
  103.4 1.4 collective-permute-start.24
  104.9 4.4 %terms.2 = (bf16[224,1920]{1,0:T(8,128)(2,1)S(1)}, bf16[224,1920]{1,0:T(8,128)(2,1)S(1)}, bf16[224,1920]{1,0:T(8,128)(2,1)S(1)}, bf16[224,1920]{1,0:T(8,128)(2,1)S(1)}) custom-call(s32[1]{0:T(128)} %bitcast.4.use_first, bf16[96,896]{1,0:T(8,128)(2,1)S(1)} %get-tuple-element.91.d.refs_0_, bf16[96,896]{1,0:T(8,128)(2,1)S(1)} %copy-done.27, ...), custom_call_target="tpu_custom_call" | custom-call | flops 3082813440 | bytes 14254084 | tf_op jit(solution)/shard_map/terms/pallas_call | solution.py:68
  109.4 1.8 collective-permute-done.23.refs_2_
  111.6 1.6 collective-permute-start.28
  113.2 1.7 collective-permute-start.29
  115.1 3.4 %collective-permute-start.26 = (bf16[96,896]{1,0:T(8,128)(2,1)S(1)}, bf16[96,896]{1,0:T(8,128)(2,1)S(1)}, u32[]{:S(2)}, u32[]{:S(2)}) collective-permute-start(bf16[96,896]{1,0:T(8,128)(2,1)S(1)} %mix.5.refs_4_), channel_id=1, source_target_pairs={{2,0},{3,1},{0,2},{1,3},{6,4},{7,5},{4,6},{5,7},{10,8},{11,9},{8,1... | collective-permute-start | bytes 516104 | tf_op jit(solution)/shard_map/ppermute | solution.py:40
  118.9 2.2 %early.3 = (bf16[896,384]{1,0:T(8,128)(2,1)S(1)}, bf16[896,384]{1,0:T(8,128)(2,1)S(1)}, bf16[384,640]{1,0:T(8,128)(2,1)S(1)}, bf16[384,1280]{1,0:T(8,128)(2,1)S(1)}) custom-call(bf16[384,896]{1,0:T(8,128)(2,1)S(1)} %copy-done.16, bf16[384,896]{1,0:T(8,128)(2,1)S(1)} %copy-done.15, bf16[896,1280]{1,0:T(8,128)(2,1)S(1)} %order.2.weights.ins.refs_0_, ...), custom_call_target="tpu_custom_call" | custom-call | flops 2202009600 | bytes 7667712 | tf_op jit(solution)/shard_map/early/pallas_call | solution.py:68
  121.1 4.4 %collective-permute-done.27.refs_7_ = bf16[96,896]{1,0:T(8,128)(2,1)S(1)} collective-permute-done((bf16[96,896]{1,0:T(8,128)(2,1)S(1)}, bf16[96,896]{1,0:T(8,128)(2,1)S(1)}, u32[]{:S(2)}, u32[]{:S(2)}) %collective-permute-start.27) | collective-permute-done | bytes 172064 | tf_op jit(solution)/shard_map/ppermute | solution.py:40
  126.1 2.9 %collective-permute-start.36 = (bf16[224,1920]{1,0:T(8,128)(2,1)S(1)}, bf16[224,1920]{1,0:T(8,128)(2,1)S(1)}, u32[]{:S(2)}, u32[]{:S(2)}) collective-permute-start(bf16[224,1920]{1,0:T(8,128)(2,1)S(1)} %get-tuple-element.145), channel_id=1, source_target_pairs={{32,0},{36,4},{40,8},{44,12},{48,16},{52,20},{56,24},{60,28},{0,32... | collective-permute-start | bytes 2580488 | tf_op jit(solution)/shard_map/ppermute | solution.py:35
  128.9 3.8 %terms.3 = (bf16[224,1920]{1,0:T(8,128)(2,1)S(1)}, bf16[224,1920]{1,0:T(8,128)(2,1)S(1)}, bf16[224,1920]{1,0:T(8,128)(2,1)S(1)}, bf16[224,1920]{1,0:T(8,128)(2,1)S(1)}) custom-call(s32[1]{0:T(128)S(6)} %sub.36.active.use_first, bf16[96,896]{1,0:T(8,128)(2,1)S(1)} %collective-permute-done.17.refs_0_, bf16[96,896]{1,0:T(8,128)(2,1)S(1)} %collective-permute-done.18.refs_1_, ...), custom_call_target="tpu_custom_call" | custom-call | flops 3082813440 | bytes 11960324 | tf_op jit(solution)/shard_map/terms/pallas_call | solution.py:68
  133.2 2.4 %collective-permute-start.31 = (bf16[224,1920]{1,0:T(8,128)(2,1)S(1)}, bf16[224,1920]{1,0:T(8,128)(2,1)S(1)}, u32[]{:S(2)}, u32[]{:S(2)}) collective-permute-start(bf16[224,1920]{1,0:T(8,128)(2,1)S(1)} %get-tuple-element.137), channel_id=1, source_target_pairs={{32,0},{36,4},{40,8},{44,12},{48,16},{52,20},{56,24},{60,28},{0,32... | collective-permute-start | bytes 2580488 | tf_op jit(solution)/shard_map/ppermute | solution.py:35
  136.1 4.4 %collective-permute-done.36.refs_2_ = bf16[224,1920]{1,0:T(8,128)(2,1)S(1)} collective-permute-done((bf16[224,1920]{1,0:T(8,128)(2,1)S(1)}, bf16[224,1920]{1,0:T(8,128)(2,1)S(1)}, u32[]{:S(2)}, u32[]{:S(2)}) %collective-permute-start.36) | collective-permute-done | bytes 860192 | tf_op jit(solution)/shard_map/ppermute | solution.py:35
  141.0 2.1 %collective-permute-start.38 = (bf16[56,1920]{1,0:T(8,128)(2,1)S(1)}, bf16[56,1920]{1,0:T(8,128)(2,1)S(1)}, u32[]{:S(2)}, u32[]{:S(2)}) collective-permute-start(bf16[56,1920]{1,0:T(8,128)(2,1)S(1)} %get-tuple-element.148), channel_id=1, source_target_pairs={{8,0},{12,4},{0,8},{4,12},{24,16},{28,20},{16,24},{20,28},{40,32},... | collective-permute-start | bytes 645128 | tf_op jit(solution)/shard_map/ppermute | solution.py:35
  143.1 11.1 %collective-permute-done.30.refs_1_ = bf16[224,1920]{1,0:T(8,128)(2,1)S(1)} collective-permute-done((bf16[224,1920]{1,0:T(8,128)(2,1)S(1)}, bf16[224,1920]{1,0:T(8,128)(2,1)S(1)}, u32[]{:S(2)}, u32[]{:S(2)}) %collective-permute-start.30) | collective-permute-done | bytes 860192 | tf_op jit(solution)/shard_map/ppermute | solution.py:35
  154.9 8.6 %collective-permute-done.31.refs_2_ = bf16[224,1920]{1,0:T(8,128)(2,1)S(1)} collective-permute-done((bf16[224,1920]{1,0:T(8,128)(2,1)S(1)}, bf16[224,1920]{1,0:T(8,128)(2,1)S(1)}, u32[]{:S(2)}, u32[]{:S(2)}) %collective-permute-start.31) | collective-permute-done | bytes 860192 | tf_op jit(solution)/shard_map/ppermute | solution.py:35
  163.9 3.0 %collective-permute-start.34 = (bf16[56,1920]{1,0:T(8,128)(2,1)S(1)}, bf16[56,1920]{1,0:T(8,128)(2,1)S(1)}, u32[]{:S(2)}, u32[]{:S(2)}) collective-permute-start(bf16[56,1920]{1,0:T(8,128)(2,1)S(1)} %get-tuple-element.141), channel_id=1, source_target_pairs={{8,0},{12,4},{0,8},{4,12},{24,16},{28,20},{16,24},{20,28},{40,32},... | collective-permute-start | bytes 645128 | tf_op jit(solution)/shard_map/ppermute | solution.py:35
  167.5 5.8 %collective-permute-done.33.refs_1_ = bf16[56,1920]{1,0:T(8,128)(2,1)S(1)} collective-permute-done((bf16[56,1920]{1,0:T(8,128)(2,1)S(1)}, bf16[56,1920]{1,0:T(8,128)(2,1)S(1)}, u32[]{:S(2)}, u32[]{:S(2)}) %collective-permute-start.33) | collective-permute-done | bytes 215072 | tf_op jit(solution)/shard_map/ppermute | solution.py:35
  174.5 1.2 collective-permute-done.40
  175.7 3.8 %collective-permute-start.42 = (f32[8,128]{1,0:T(8,128)S(1)}, f32[8,128]{1,0:T(8,128)S(1)}, u32[]{:S(2)}, u32[]{:S(2)}) collective-permute-start(f32[8,128]{1,0:T(8,128)S(1)} %add.249), channel_id=1, source_target_pairs={{8,0},{12,4},{0,8},{4,12},{24,16},{28,20},{16,24},{20,28},{40,32},... | collective-permute-start | bytes 12296 | tf_op jit(solution)/shard_map/ppermute | solution.py:347
  179.5 1.0 collective-permute-done.43
  181.1 2.0 collective-permute-done.41
  183.1 1.5 collective-permute-start.46
  184.6 2.6 %collective-permute-start.45 = (f32[8,128]{1,0:T(8,128)S(1)}, f32[8,128]{1,0:T(8,128)S(1)}, u32[]{:S(2)}, u32[]{:S(2)}) collective-permute-start(f32[8,128]{1,0:T(8,128)S(1)} %add_add_fusion.2), channel_id=1, source_target_pairs={{32,0},{36,4},{40,8},{44,12},{48,16},{52,20},{56,24},{60,28},{0,32... | collective-permute-start | bytes 12296 | tf_op jit(solution)/shard_map/ppermute | solution.py:347
  187.2 1.9 collective-permute-start.44
  189.7 1.4 collective-permute-done.44
  191.3 3.8 %collective-permute-start.48 = (f32[8,128]{1,0:T(8,128)S(1)}, f32[8,128]{1,0:T(8,128)S(1)}, u32[]{:S(2)}, u32[]{:S(2)}) collective-permute-start(f32[8,128]{1,0:T(8,128)S(1)} %add_add_fusion.1), channel_id=1, source_target_pairs={{2,0},{3,1},{0,2},{1,3},{6,4},{7,5},{4,6},{5,7},{10,8},{11,9},{8,1... | collective-permute-start | bytes 12296 | tf_op jit(solution)/shard_map/ppermute | solution.py:40
  196.7 2.0 collective-permute-done.47
  200.8 1.1 copy.27
  201.9 1.1 copy.26
  203.0 1.3 copy.25
  (189 shorter events, 23.3 us)
Async XLA Ops:
  7.2 77.5 %all-gather.2.cloned.1.call-start = ((), (), s32[]{:S(2)}) async-start(), calls=%async_computation | async-start | bytes 3655680 | tf_op jit(solution)/shard_map/all_gather | solution.py:384
  9.5 19.9 %copy-start.42 = (bf16[1,2,384,896]{3,2,1,0:T(8,128)(2,1)S(1)}, bf16[1,2,384,896]{3,2,1,0:T(8,128)(2,1)}, u32[]{:S(2)}) copy-start(bf16[1,2,384,896]{3,2,1,0:T(8,128)(2,1)} %param.8) | copy-start | bytes 4128772
  9.5 12.3 %collective-permute-start.2 = (bf16[56,1920]{1,0:T(8,128)(2,1)S(1)}, bf16[56,1920]{1,0:T(8,128)(2,1)S(1)}, u32[]{:S(2)}, u32[]{:S(2)}) collective-permute-start(bf16[56,1920]{1,0:T(8,128)(2,1)S(1)} %bitcast.109), channel_id=1, source_target_pairs={{12,0},{0,4},{4,8},{8,12},{28,16},{16,20},{20,24},{24,28},{44,32},... | collective-permute-start | bytes 645128 | tf_op jit(solution)/shard_map/ppermute | solution.py:35
  11.1 9.7 %collective-permute-start.1 = (bf16[56,1920]{1,0:T(8,128)(2,1)S(1)}, bf16[56,1920]{1,0:T(8,128)(2,1)}, u32[]{:S(2)}, u32[]{:S(2)}) collective-permute-start(bf16[56,1920]{1,0:T(8,128)(2,1)S(1)} %bitcast.110), channel_id=1, source_target_pairs={{8,0},{12,4},{0,8},{4,12},{24,16},{28,20},{16,24},{20,28},{40,32},... | collective-permute-start | bytes 645128 | tf_op jit(solution)/shard_map/ppermute | solution.py:35
  13.9 6.0 %collective-permute-start = (bf16[56,1920]{1,0:T(8,128)(2,1)S(1)}, bf16[56,1920]{1,0:T(8,128)(2,1)}, u32[]{:S(2)}, u32[]{:S(2)}) collective-permute-start(bf16[56,1920]{1,0:T(8,128)(2,1)S(1)} %bitcast.111), channel_id=1, source_target_pairs={{4,0},{8,4},{12,8},{0,12},{20,16},{24,20},{28,24},{16,28},{36,32},... | collective-permute-start | bytes 645128 | tf_op jit(solution)/shard_map/ppermute | solution.py:35
  17.9 11.6 %copy-start.41 = (bf16[1,2,2,384,896]{4,3,2,1,0:T(8,128)(2,1)S(1)}, bf16[1,2,2,384,896]{4,3,2,1,0:T(8,128)(2,1)}, u32[]{:S(2)}) copy-start(bf16[1,2,2,384,896]{4,3,2,1,0:T(8,128)(2,1)} %param.7) | copy-start | bytes 8257540
  21.9 54.7 %copy-start.3 = (bf16[224,1920]{1,0:T(8,128)(2,1)}, bf16[224,1920]{1,0:T(8,128)(2,1)S(1)}, u32[]{:S(2)}) copy-start(bf16[224,1920]{1,0:T(8,128)(2,1)S(1)} %constant_dynamic-update-slice_fusion.refs_0_.refs_16_) | copy-start | bytes 2580484
  21.9 18.8 %collective-permute-start.5 = (bf16[224,1920]{1,0:T(8,128)(2,1)S(1)}, bf16[224,1920]{1,0:T(8,128)(2,1)S(1)}, u32[]{:S(2)}, u32[]{:S(2)}) collective-permute-start(bf16[224,1920]{1,0:T(8,128)(2,1)S(1)} %constant_dynamic-update-slice_fusion.refs_0_.refs_16_), channel_id=1, source_target_pairs={{48,0},{52,4},{56,8},{60,12},{0,16},{4,20},{8,24},{12,28},{16,32},... | collective-permute-start | bytes 2580488 | tf_op jit(solution)/shard_map/ppermute | solution.py:35
  23.6 25.7 %collective-permute-start.4 = (bf16[224,1920]{1,0:T(8,128)(2,1)S(1)}, bf16[224,1920]{1,0:T(8,128)(2,1)S(1)}, u32[]{:S(2)}, u32[]{:S(2)}) collective-permute-start(bf16[224,1920]{1,0:T(8,128)(2,1)S(1)} %constant_dynamic-update-slice_fusion.refs_0_.refs_16_), channel_id=1, source_target_pairs={{32,0},{36,4},{40,8},{44,12},{48,16},{52,20},{56,24},{60,28},{0,32... | collective-permute-start | bytes 2580488 | tf_op jit(solution)/shard_map/ppermute | solution.py:35
  26.5 22.8 %collective-permute-start.3 = (bf16[224,1920]{1,0:T(8,128)(2,1)S(1)}, bf16[224,1920]{1,0:T(8,128)(2,1)S(1)}, u32[]{:S(2)}, u32[]{:S(2)}) collective-permute-start(bf16[224,1920]{1,0:T(8,128)(2,1)S(1)} %constant_dynamic-update-slice_fusion.refs_0_.refs_16_), channel_id=1, source_target_pairs={{16,0},{20,4},{24,8},{28,12},{32,16},{36,20},{40,24},{44,28},{48,3... | collective-permute-start | bytes 2580488 | tf_op jit(solution)/shard_map/ppermute | solution.py:35
  40.7 35.9 %copy-start.9 = (bf16[224,1920]{1,0:T(8,128)(2,1)}, bf16[224,1920]{1,0:T(8,128)(2,1)S(1)}, u32[]{:S(2)}) copy-start(bf16[224,1920]{1,0:T(8,128)(2,1)S(1)} %collective-permute-done.5.refs_3_.refs_19_) | copy-start | bytes 2580484
  49.3 27.3 %copy-start.11 = (bf16[224,1920]{1,0:T(8,128)(2,1)}, bf16[224,1920]{1,0:T(8,128)(2,1)S(1)}, u32[]{:S(2)}) copy-start(bf16[224,1920]{1,0:T(8,128)(2,1)S(1)} %collective-permute-done.4.refs_2_.refs_18_) | copy-start | bytes 2580484
  49.3 27.3 %copy-start.13 = (bf16[224,1920]{1,0:T(8,128)(2,1)}, bf16[224,1920]{1,0:T(8,128)(2,1)S(1)}, u32[]{:S(2)}) copy-start(bf16[224,1920]{1,0:T(8,128)(2,1)S(1)} %collective-permute-done.3.refs_1_.refs_17_) | copy-start | bytes 2580484
  57.0 19.6 %copy-start.5 = (f32[384,640]{1,0:T(8,128)}, f32[384,640]{1,0:T(8,128)S(1)}, u32[]{:S(2)}) copy-start(f32[384,640]{1,0:T(8,128)S(1)} %get-tuple-element.95.slope.refs_14_) | copy-start | bytes 2949124
  57.0 19.6 %copy-start.7 = (f32[384,640]{1,0:T(8,128)}, f32[384,640]{1,0:T(8,128)S(1)}, u32[]{:S(2)}) copy-start(f32[384,640]{1,0:T(8,128)S(1)} %get-tuple-element.96.activated.refs_15_) | copy-start | bytes 2949124
  57.0 9.7 %collective-permute-start.6 = (bf16[96,896]{1,0:T(8,128)(2,1)S(1)}, bf16[96,896]{1,0:T(8,128)(2,1)S(1)}, u32[]{:S(2)}, u32[]{:S(2)}) collective-permute-start(bf16[96,896]{1,0:T(8,128)(2,1)S(1)} %get-tuple-element.92), channel_id=1, source_target_pairs={{3,0},{0,1},{1,2},{2,3},{7,4},{4,5},{5,6},{6,7},{11,8},{8,9},{9,10... | collective-permute-start | bytes 516104 | tf_op jit(solution)/shard_map/ppermute | solution.py:40
  58.6 10.3 %collective-permute-start.7 = (bf16[96,896]{1,0:T(8,128)(2,1)S(1)}, bf16[96,896]{1,0:T(8,128)(2,1)S(1)}, u32[]{:S(2)}, u32[]{:S(2)}) collective-permute-start(bf16[96,896]{1,0:T(8,128)(2,1)S(1)} %get-tuple-element.93), channel_id=1, source_target_pairs={{2,0},{3,1},{0,2},{1,3},{6,4},{7,5},{4,6},{5,7},{10,8},{11,9},{8,1... | collective-permute-start | bytes 516104 | tf_op jit(solution)/shard_map/ppermute | solution.py:40
  62.0 6.8 %collective-permute-start.8 = (bf16[96,896]{1,0:T(8,128)(2,1)S(1)}, bf16[96,896]{1,0:T(8,128)(2,1)S(1)}, u32[]{:S(2)}, u32[]{:S(2)}) collective-permute-start(bf16[96,896]{1,0:T(8,128)(2,1)S(1)} %get-tuple-element.94), channel_id=1, source_target_pairs={{1,0},{2,1},{3,2},{0,3},{5,4},{6,5},{7,6},{4,7},{9,8},{10,9},{11,1... | collective-permute-start | bytes 516104 | tf_op jit(solution)/shard_map/ppermute | solution.py:40
  69.2 3.8 %collective-permute-start.12 = (bf16[96,896]{1,0:T(8,128)(2,1)S(1)}, bf16[96,896]{1,0:T(8,128)(2,1)S(1)}, u32[]{:S(2)}, u32[]{:S(2)}) collective-permute-start(bf16[96,896]{1,0:T(8,128)(2,1)S(1)} %mix.3.d), channel_id=1, source_target_pairs={{3,64},{0,65},{1,66},{2,67},{64,0},{65,1},{66,2},{67,3},{7,68},{4,... | collective-permute-start | bytes 516104 | tf_op jit(solution)/shard_map/ppermute | solution.py:46
  70.1 4.8 %collective-permute-start.11 = (bf16[96,896]{1,0:T(8,128)(2,1)S(1)}, bf16[96,896]{1,0:T(8,128)(2,1)S(1)}, u32[]{:S(2)}, u32[]{:S(2)}) collective-permute-start(bf16[96,896]{1,0:T(8,128)(2,1)S(1)} %mix.3.d), channel_id=1, source_target_pairs={{2,64},{3,65},{0,66},{1,67},{64,0},{65,1},{66,2},{67,3},{6,68},{7,... | collective-permute-start | bytes 516104 | tf_op jit(solution)/shard_map/ppermute | solution.py:46
  71.7 4.9 %collective-permute-start.10 = (bf16[96,896]{1,0:T(8,128)(2,1)S(1)}, bf16[96,896]{1,0:T(8,128)(2,1)S(1)}, u32[]{:S(2)}, u32[]{:S(2)}) collective-permute-start(bf16[96,896]{1,0:T(8,128)(2,1)S(1)} %mix.3.d), channel_id=1, source_target_pairs={{1,64},{2,65},{3,66},{0,67},{64,0},{65,1},{66,2},{67,3},{5,68},{6,... | collective-permute-start | bytes 516104 | tf_op jit(solution)/shard_map/ppermute | solution.py:46
  71.8 4.8 %collective-permute-start.9 = (bf16[96,896]{1,0:T(8,128)(2,1)S(1)}, bf16[96,896]{1,0:T(8,128)(2,1)S(1)}, u32[]{:S(2)}, u32[]{:S(2)}) collective-permute-start(bf16[96,896]{1,0:T(8,128)(2,1)S(1)} %mix.3.d), channel_id=1, source_target_pairs={{0,64},{1,65},{2,66},{3,67},{64,0},{65,1},{66,2},{67,3},{4,68},{5,... | collective-permute-start | bytes 516104 | tf_op jit(solution)/shard_map/ppermute | solution.py:46
  77.7 13.0 %collective-permute-start.14 = (bf16[96,896]{1,0:T(8,128)(2,1)}, bf16[96,896]{1,0:T(8,128)(2,1)}, u32[]{:S(2)}, u32[]{:S(2)}) collective-permute-start(bf16[96,896]{1,0:T(8,128)(2,1)} %get-tuple-element.100), channel_id=1, source_target_pairs={{67,0},{64,1},{65,2},{66,3},{0,64},{1,65},{2,66},{3,67},{71,4},{68... | collective-permute-start | bytes 516104 | tf_op jit(solution)/shard_map/ppermute | solution.py:46
  82.0 8.8 %collective-permute-start.15 = (bf16[96,896]{1,0:T(8,128)(2,1)}, bf16[96,896]{1,0:T(8,128)(2,1)}, u32[]{:S(2)}, u32[]{:S(2)}) collective-permute-start(bf16[96,896]{1,0:T(8,128)(2,1)} %get-tuple-element.101), channel_id=1, source_target_pairs={{66,0},{67,1},{64,2},{65,3},{0,64},{1,65},{2,66},{3,67},{70,4},{71... | collective-permute-start | bytes 516104 | tf_op jit(solution)/shard_map/ppermute | solution.py:46
  82.0 8.7 %collective-permute-start.16 = (bf16[96,896]{1,0:T(8,128)(2,1)}, bf16[96,896]{1,0:T(8,128)(2,1)}, u32[]{:S(2)}, u32[]{:S(2)}) collective-permute-start(bf16[96,896]{1,0:T(8,128)(2,1)} %get-tuple-element.102), channel_id=1, source_target_pairs={{65,0},{66,1},{67,2},{64,3},{0,64},{1,65},{2,66},{3,67},{69,4},{70... | collective-permute-start | bytes 516104 | tf_op jit(solution)/shard_map/ppermute | solution.py:46
  84.7 6.1 %collective-permute-start.13 = (bf16[96,896]{1,0:T(8,128)(2,1)}, bf16[96,896]{1,0:T(8,128)(2,1)}, u32[]{:S(2)}, u32[]{:S(2)}) collective-permute-start(bf16[96,896]{1,0:T(8,128)(2,1)} %get-tuple-element.97), channel_id=1, source_target_pairs={{64,0},{65,1},{66,2},{67,3},{0,64},{1,65},{2,66},{3,67},{68,4},{69... | collective-permute-start | bytes 516104 | tf_op jit(solution)/shard_map/ppermute | solution.py:46
  92.2 7.1 %collective-permute-start.20 = (bf16[96,896]{1,0:T(8,128)(2,1)S(1)}, bf16[96,896]{1,0:T(8,128)(2,1)S(1)}, u32[]{:S(2)}, u32[]{:S(2)}) collective-permute-start(bf16[96,896]{1,0:T(8,128)(2,1)S(1)} %mix.4.d), channel_id=1, source_target_pairs={{3,64},{0,65},{1,66},{2,67},{64,0},{65,1},{66,2},{67,3},{7,68},{4,... | collective-permute-start | bytes 516104 | tf_op jit(solution)/shard_map/ppermute | solution.py:46
  93.0 6.3 %collective-permute-start.19 = (bf16[96,896]{1,0:T(8,128)(2,1)S(1)}, bf16[96,896]{1,0:T(8,128)(2,1)S(1)}, u32[]{:S(2)}, u32[]{:S(2)}) collective-permute-start(bf16[96,896]{1,0:T(8,128)(2,1)S(1)} %mix.4.d), channel_id=1, source_target_pairs={{2,64},{3,65},{0,66},{1,67},{64,0},{65,1},{66,2},{67,3},{6,68},{7,... | collective-permute-start | bytes 516104 | tf_op jit(solution)/shard_map/ppermute | solution.py:46
  93.4 5.9 %collective-permute-start.18 = (bf16[96,896]{1,0:T(8,128)(2,1)S(1)}, bf16[96,896]{1,0:T(8,128)(2,1)S(1)}, u32[]{:S(2)}, u32[]{:S(2)}) collective-permute-start(bf16[96,896]{1,0:T(8,128)(2,1)S(1)} %mix.4.d), channel_id=1, source_target_pairs={{1,64},{2,65},{3,66},{0,67},{64,0},{65,1},{66,2},{67,3},{5,68},{6,... | collective-permute-start | bytes 516104 | tf_op jit(solution)/shard_map/ppermute | solution.py:46
  95.7 3.6 %collective-permute-start.17 = (bf16[96,896]{1,0:T(8,128)(2,1)S(1)}, bf16[96,896]{1,0:T(8,128)(2,1)S(1)}, u32[]{:S(2)}, u32[]{:S(2)}) collective-permute-start(bf16[96,896]{1,0:T(8,128)(2,1)S(1)} %mix.4.d), channel_id=1, source_target_pairs={{0,64},{1,65},{2,66},{3,67},{64,0},{65,1},{66,2},{67,3},{4,68},{5,... | collective-permute-start | bytes 516104 | tf_op jit(solution)/shard_map/ppermute | solution.py:46
  99.5 11.7 %collective-permute-start.21 = (bf16[96,896]{1,0:T(8,128)(2,1)S(1)}, bf16[96,896]{1,0:T(8,128)(2,1)S(1)}, u32[]{:S(2)}, u32[]{:S(2)}) collective-permute-start(bf16[96,896]{1,0:T(8,128)(2,1)S(1)} %get-tuple-element.107), channel_id=1, source_target_pairs={{64,0},{65,1},{66,2},{67,3},{0,64},{1,65},{2,66},{3,67},{68,4},{69... | collective-permute-start | bytes 516104 | tf_op jit(solution)/shard_map/ppermute | solution.py:46
  103.0 6.4 %collective-permute-start.22 = (bf16[96,896]{1,0:T(8,128)(2,1)S(1)}, bf16[96,896]{1,0:T(8,128)(2,1)S(1)}, u32[]{:S(2)}, u32[]{:S(2)}) collective-permute-start(bf16[96,896]{1,0:T(8,128)(2,1)S(1)} %get-tuple-element.116), channel_id=1, source_target_pairs={{67,0},{64,1},{65,2},{66,3},{0,64},{1,65},{2,66},{3,67},{71,4},{68... | collective-permute-start | bytes 516104 | tf_op jit(solution)/shard_map/ppermute | solution.py:46
  103.0 8.2 %collective-permute-start.23 = (bf16[96,896]{1,0:T(8,128)(2,1)S(1)}, bf16[96,896]{1,0:T(8,128)(2,1)S(1)}, u32[]{:S(2)}, u32[]{:S(2)}) collective-permute-start(bf16[96,896]{1,0:T(8,128)(2,1)S(1)} %get-tuple-element.117), channel_id=1, source_target_pairs={{66,0},{67,1},{64,2},{65,3},{0,64},{1,65},{2,66},{3,67},{70,4},{71... | collective-permute-start | bytes 516104 | tf_op jit(solution)/shard_map/ppermute | solution.py:46
  103.4 7.8 %collective-permute-start.24 = (bf16[96,896]{1,0:T(8,128)(2,1)S(1)}, bf16[96,896]{1,0:T(8,128)(2,1)S(1)}, u32[]{:S(2)}, u32[]{:S(2)}) collective-permute-start(bf16[96,896]{1,0:T(8,128)(2,1)S(1)} %get-tuple-element.118), channel_id=1, source_target_pairs={{65,0},{66,1},{67,2},{64,3},{0,64},{1,65},{2,66},{3,67},{69,4},{70... | collective-permute-start | bytes 516104 | tf_op jit(solution)/shard_map/ppermute | solution.py:46
  104.9 14.0 %copy-start.15 = (bf16[384,896]{1,0:T(8,128)(2,1)S(1)}, bf16[384,896]{1,0:T(8,128)(2,1)}, u32[]{:S(2)}) copy-start(bf16[384,896]{1,0:T(8,128)(2,1)} %get-tuple-element.167.d) | copy-start | bytes 2064388
  104.9 14.0 %copy-start.16 = (bf16[384,896]{1,0:T(8,128)(2,1)S(1)}, bf16[384,896]{1,0:T(8,128)(2,1)}, u32[]{:S(2)}) copy-start(bf16[384,896]{1,0:T(8,128)(2,1)} %get-tuple-element.119.x) | copy-start | bytes 2064388
  111.6 17.3 %collective-permute-start.28 = (bf16[224,1920]{1,0:T(8,128)(2,1)S(1)}, bf16[224,1920]{1,0:T(8,128)(2,1)S(1)}, u32[]{:S(2)}, u32[]{:S(2)}) collective-permute-start(bf16[224,1920]{1,0:T(8,128)(2,1)S(1)} %get-tuple-element.127), channel_id=1, source_target_pairs={{48,0},{52,4},{56,8},{60,12},{0,16},{4,20},{8,24},{12,28},{16,32},... | collective-permute-start | bytes 2580488 | tf_op jit(solution)/shard_map/ppermute | solution.py:35
  113.2 15.7 %collective-permute-start.29 = (bf16[224,1920]{1,0:T(8,128)(2,1)S(1)}, bf16[224,1920]{1,0:T(8,128)(2,1)S(1)}, u32[]{:S(2)}, u32[]{:S(2)}) collective-permute-start(bf16[224,1920]{1,0:T(8,128)(2,1)S(1)} %get-tuple-element.128), channel_id=1, source_target_pairs={{16,0},{20,4},{24,8},{28,12},{32,16},{36,20},{40,24},{44,28},{48,3... | collective-permute-start | bytes 2580488 | tf_op jit(solution)/shard_map/ppermute | solution.py:35
  114.9 10.5 %collective-permute-start.27 = (bf16[96,896]{1,0:T(8,128)(2,1)S(1)}, bf16[96,896]{1,0:T(8,128)(2,1)S(1)}, u32[]{:S(2)}, u32[]{:S(2)}) collective-permute-start(bf16[96,896]{1,0:T(8,128)(2,1)S(1)} %mix.5.refs_4_), channel_id=1, source_target_pairs={{3,0},{0,1},{1,2},{2,3},{7,4},{4,5},{5,6},{6,7},{11,8},{8,9},{9,10... | collective-permute-start | bytes 516104 | tf_op jit(solution)/shard_map/ppermute | solution.py:40
  115.1 10.3 %collective-permute-start.26 = (bf16[96,896]{1,0:T(8,128)(2,1)S(1)}, bf16[96,896]{1,0:T(8,128)(2,1)S(1)}, u32[]{:S(2)}, u32[]{:S(2)}) collective-permute-start(bf16[96,896]{1,0:T(8,128)(2,1)S(1)} %mix.5.refs_4_), channel_id=1, source_target_pairs={{2,0},{3,1},{0,2},{1,3},{6,4},{7,5},{4,6},{5,7},{10,8},{11,9},{8,1... | collective-permute-start | bytes 516104 | tf_op jit(solution)/shard_map/ppermute | solution.py:40
  118.5 7.6 %collective-permute-start.25 = (bf16[96,896]{1,0:T(8,128)(2,1)S(1)}, bf16[96,896]{1,0:T(8,128)(2,1)S(1)}, u32[]{:S(2)}, u32[]{:S(2)}) collective-permute-start(bf16[96,896]{1,0:T(8,128)(2,1)S(1)} %mix.5.refs_4_), channel_id=1, source_target_pairs={{1,0},{2,1},{3,2},{0,3},{5,4},{6,5},{7,6},{4,7},{9,8},{10,9},{11,1... | collective-permute-start | bytes 516104 | tf_op jit(solution)/shard_map/ppermute | solution.py:40
  126.1 14.4 %collective-permute-start.36 = (bf16[224,1920]{1,0:T(8,128)(2,1)S(1)}, bf16[224,1920]{1,0:T(8,128)(2,1)S(1)}, u32[]{:S(2)}, u32[]{:S(2)}) collective-permute-start(bf16[224,1920]{1,0:T(8,128)(2,1)S(1)} %get-tuple-element.145), channel_id=1, source_target_pairs={{32,0},{36,4},{40,8},{44,12},{48,16},{52,20},{56,24},{60,28},{0,32... | collective-permute-start | bytes 2580488 | tf_op jit(solution)/shard_map/ppermute | solution.py:35
  132.7 21.5 %collective-permute-start.30 = (bf16[224,1920]{1,0:T(8,128)(2,1)S(1)}, bf16[224,1920]{1,0:T(8,128)(2,1)S(1)}, u32[]{:S(2)}, u32[]{:S(2)}) collective-permute-start(bf16[224,1920]{1,0:T(8,128)(2,1)S(1)} %get-tuple-element.136), channel_id=1, source_target_pairs={{48,0},{52,4},{56,8},{60,12},{0,16},{4,20},{8,24},{12,28},{16,32},... | collective-permute-start | bytes 2580488 | tf_op jit(solution)/shard_map/ppermute | solution.py:35
  133.2 30.2 %collective-permute-start.31 = (bf16[224,1920]{1,0:T(8,128)(2,1)S(1)}, bf16[224,1920]{1,0:T(8,128)(2,1)S(1)}, u32[]{:S(2)}, u32[]{:S(2)}) collective-permute-start(bf16[224,1920]{1,0:T(8,128)(2,1)S(1)} %get-tuple-element.137), channel_id=1, source_target_pairs={{32,0},{36,4},{40,8},{44,12},{48,16},{52,20},{56,24},{60,28},{0,32... | collective-permute-start | bytes 2580488 | tf_op jit(solution)/shard_map/ppermute | solution.py:35
  135.6 27.9 %collective-permute-start.32 = (bf16[224,1920]{1,0:T(8,128)(2,1)S(1)}, bf16[224,1920]{1,0:T(8,128)(2,1)S(1)}, u32[]{:S(2)}, u32[]{:S(2)}) collective-permute-start(bf16[224,1920]{1,0:T(8,128)(2,1)S(1)} %get-tuple-element.138), channel_id=1, source_target_pairs={{16,0},{20,4},{24,8},{28,12},{32,16},{36,20},{40,24},{44,28},{48,3... | collective-permute-start | bytes 2580488 | tf_op jit(solution)/shard_map/ppermute | solution.py:35
  140.9 26.1 %collective-permute-start.37 = (bf16[56,1920]{1,0:T(8,128)(2,1)S(1)}, bf16[56,1920]{1,0:T(8,128)(2,1)S(1)}, u32[]{:S(2)}, u32[]{:S(2)}) collective-permute-start(bf16[56,1920]{1,0:T(8,128)(2,1)S(1)} %get-tuple-element.147), channel_id=1, source_target_pairs={{12,0},{0,4},{4,8},{8,12},{28,16},{16,20},{20,24},{24,28},{44,32},... | collective-permute-start | bytes 645128 | tf_op jit(solution)/shard_map/ppermute | solution.py:35
  141.0 26.2 %collective-permute-start.38 = (bf16[56,1920]{1,0:T(8,128)(2,1)S(1)}, bf16[56,1920]{1,0:T(8,128)(2,1)S(1)}, u32[]{:S(2)}, u32[]{:S(2)}) collective-permute-start(bf16[56,1920]{1,0:T(8,128)(2,1)S(1)} %get-tuple-element.148), channel_id=1, source_target_pairs={{8,0},{12,4},{0,8},{4,12},{24,16},{28,20},{16,24},{20,28},{40,32},... | collective-permute-start | bytes 645128 | tf_op jit(solution)/shard_map/ppermute | solution.py:35
  154.2 13.0 %collective-permute-start.39 = (bf16[56,1920]{1,0:T(8,128)(2,1)S(1)}, bf16[56,1920]{1,0:T(8,128)(2,1)S(1)}, u32[]{:S(2)}, u32[]{:S(2)}) collective-permute-start(bf16[56,1920]{1,0:T(8,128)(2,1)S(1)} %get-tuple-element.149), channel_id=1, source_target_pairs={{4,0},{8,4},{12,8},{0,12},{20,16},{24,20},{28,24},{16,28},{36,32},... | collective-permute-start | bytes 645128 | tf_op jit(solution)/shard_map/ppermute | solution.py:35
  163.9 9.5 %collective-permute-start.33 = (bf16[56,1920]{1,0:T(8,128)(2,1)S(1)}, bf16[56,1920]{1,0:T(8,128)(2,1)S(1)}, u32[]{:S(2)}, u32[]{:S(2)}) collective-permute-start(bf16[56,1920]{1,0:T(8,128)(2,1)S(1)} %get-tuple-element.140), channel_id=1, source_target_pairs={{12,0},{0,4},{4,8},{8,12},{28,16},{16,20},{20,24},{24,28},{44,32},... | collective-permute-start | bytes 645128 | tf_op jit(solution)/shard_map/ppermute | solution.py:35
  163.9 9.4 %collective-permute-start.34 = (bf16[56,1920]{1,0:T(8,128)(2,1)S(1)}, bf16[56,1920]{1,0:T(8,128)(2,1)S(1)}, u32[]{:S(2)}, u32[]{:S(2)}) collective-permute-start(bf16[56,1920]{1,0:T(8,128)(2,1)S(1)} %get-tuple-element.141), channel_id=1, source_target_pairs={{8,0},{12,4},{0,8},{4,12},{24,16},{28,20},{16,24},{20,28},{40,32},... | collective-permute-start | bytes 645128 | tf_op jit(solution)/shard_map/ppermute | solution.py:35
  167.0 7.2 %collective-permute-start.35 = (bf16[56,1920]{1,0:T(8,128)(2,1)S(1)}, bf16[56,1920]{1,0:T(8,128)(2,1)S(1)}, u32[]{:S(2)}, u32[]{:S(2)}) collective-permute-start(bf16[56,1920]{1,0:T(8,128)(2,1)S(1)} %get-tuple-element.142), channel_id=1, source_target_pairs={{4,0},{8,4},{12,8},{0,12},{20,16},{24,20},{28,24},{16,28},{36,32},... | collective-permute-start | bytes 645128 | tf_op jit(solution)/shard_map/ppermute | solution.py:35
  167.4 32.5 %copy-start.40 = (f32[1,56,2,3,640]{4,2,3,1,0:T(2,128)S(1)}, f32[1,56,2,3,640]{4,2,3,1,0:T(2,128)}, u32[]{:S(2)}) copy-start(f32[1,56,2,3,640]{4,2,3,1,0:T(2,128)} %param.11) | copy-start | bytes 2580484
  167.5 32.5 %copy-start.43 = (bf16[1,56,2,3,640]{4,2,3,1,0:T(2,128)(2,1)S(1)}, bf16[1,56,2,3,640]{4,2,3,1,0:T(2,128)(2,1)}, u32[]{:S(2)}) copy-start(bf16[1,56,2,3,640]{4,2,3,1,0:T(2,128)(2,1)} %param.13) | copy-start | bytes 1290244
  167.5 32.5 %copy-start.44 = (bf16[1,56,2,3,640]{4,2,3,1,0:T(2,128)(2,1)S(1)}, bf16[1,56,2,3,640]{4,2,3,1,0:T(2,128)(2,1)}, u32[]{:S(2)}) copy-start(bf16[1,56,2,3,640]{4,2,3,1,0:T(2,128)(2,1)} %param.12) | copy-start | bytes 1290244
  174.5 1.2 collective-permute-start.40
  175.7 4.8 %collective-permute-start.43 = (f32[8,128]{1,0:T(8,128)S(1)}, f32[8,128]{1,0:T(8,128)S(1)}, u32[]{:S(2)}, u32[]{:S(2)}) collective-permute-start(f32[8,128]{1,0:T(8,128)S(1)} %add.249), channel_id=1, source_target_pairs={{12,0},{0,4},{4,8},{8,12},{28,16},{16,20},{20,24},{24,28},{44,32},... | collective-permute-start | bytes 12296 | tf_op jit(solution)/shard_map/ppermute | solution.py:347
  175.7 5.4 %collective-permute-start.42 = (f32[8,128]{1,0:T(8,128)S(1)}, f32[8,128]{1,0:T(8,128)S(1)}, u32[]{:S(2)}, u32[]{:S(2)}) collective-permute-start(f32[8,128]{1,0:T(8,128)S(1)} %add.249), channel_id=1, source_target_pairs={{8,0},{12,4},{0,8},{4,12},{24,16},{28,20},{16,24},{20,28},{40,32},... | collective-permute-start | bytes 12296 | tf_op jit(solution)/shard_map/ppermute | solution.py:347
  179.5 3.6 %collective-permute-start.41 = (f32[8,128]{1,0:T(8,128)S(1)}, f32[8,128]{1,0:T(8,128)S(1)}, u32[]{:S(2)}, u32[]{:S(2)}) collective-permute-start(f32[8,128]{1,0:T(8,128)S(1)} %add.249), channel_id=1, source_target_pairs={{4,0},{8,4},{12,8},{0,12},{20,16},{24,20},{28,24},{16,28},{36,32},... | collective-permute-start | bytes 12296 | tf_op jit(solution)/shard_map/ppermute | solution.py:347
  183.1 6.0 %collective-permute-start.46 = (f32[8,128]{1,0:T(8,128)S(1)}, f32[8,128]{1,0:T(8,128)S(1)}, u32[]{:S(2)}, u32[]{:S(2)}) collective-permute-start(f32[8,128]{1,0:T(8,128)S(1)} %add_add_fusion.2), channel_id=1, source_target_pairs={{48,0},{52,4},{56,8},{60,12},{0,16},{4,20},{8,24},{12,28},{16,32},... | collective-permute-start | bytes 12296 | tf_op jit(solution)/shard_map/ppermute | solution.py:347
  184.6 5.1 %collective-permute-start.45 = (f32[8,128]{1,0:T(8,128)S(1)}, f32[8,128]{1,0:T(8,128)S(1)}, u32[]{:S(2)}, u32[]{:S(2)}) collective-permute-start(f32[8,128]{1,0:T(8,128)S(1)} %add_add_fusion.2), channel_id=1, source_target_pairs={{32,0},{36,4},{40,8},{44,12},{48,16},{52,20},{56,24},{60,28},{0,32... | collective-permute-start | bytes 12296 | tf_op jit(solution)/shard_map/ppermute | solution.py:347
  187.2 3.8 %collective-permute-start.44 = (f32[8,128]{1,0:T(8,128)S(1)}, f32[8,128]{1,0:T(8,128)S(1)}, u32[]{:S(2)}, u32[]{:S(2)}) collective-permute-start(f32[8,128]{1,0:T(8,128)S(1)} %add_add_fusion.2), channel_id=1, source_target_pairs={{16,0},{20,4},{24,8},{28,12},{32,16},{36,20},{40,24},{44,28},{48,3... | collective-permute-start | bytes 12296 | tf_op jit(solution)/shard_map/ppermute | solution.py:347
  191.0 4.8 %collective-permute-start.49 = (f32[8,128]{1,0:T(8,128)S(1)}, f32[8,128]{1,0:T(8,128)S(1)}, u32[]{:S(2)}, u32[]{:S(2)}) collective-permute-start(f32[8,128]{1,0:T(8,128)S(1)} %add_add_fusion.1), channel_id=1, source_target_pairs={{3,0},{0,1},{1,2},{2,3},{7,4},{4,5},{5,6},{6,7},{11,8},{8,9},{9,10... | collective-permute-start | bytes 12296 | tf_op jit(solution)/shard_map/ppermute | solution.py:40
  191.3 5.4 %collective-permute-start.48 = (f32[8,128]{1,0:T(8,128)S(1)}, f32[8,128]{1,0:T(8,128)S(1)}, u32[]{:S(2)}, u32[]{:S(2)}) collective-permute-start(f32[8,128]{1,0:T(8,128)S(1)} %add_add_fusion.1), channel_id=1, source_target_pairs={{2,0},{3,1},{0,2},{1,3},{6,4},{7,5},{4,6},{5,7},{10,8},{11,9},{8,1... | collective-permute-start | bytes 12296 | tf_op jit(solution)/shard_map/ppermute | solution.py:40
  195.1 3.6 %collective-permute-start.47 = (f32[8,128]{1,0:T(8,128)S(1)}, f32[8,128]{1,0:T(8,128)S(1)}, u32[]{:S(2)}, u32[]{:S(2)}) collective-permute-start(f32[8,128]{1,0:T(8,128)S(1)} %add_add_fusion.1), channel_id=1, source_target_pairs={{1,0},{2,1},{3,2},{0,3},{5,4},{6,5},{7,6},{4,7},{9,8},{10,9},{11,1... | collective-permute-start | bytes 12296 | tf_op jit(solution)/shard_map/ppermute | solution.py:40
  (33 other events, 181.8 us)
Sparse Core Ops, SparseCore 0:
  10.7 64.5 all-gather.1

commit v3 on v1

--- a/solution.py
+++ b/solution.py
@@ -373,7 +373,6 @@
 
     shard = shard_of(1)
     block = jnp.concatenate([shard] + peers(lambda by: from_plane(shard, by, True)), 0)
-    lower_whole = lax.all_gather(shard_of(0), "dp", axis=0, tiled=True)
     upper = [block] + peers(lambda by: from_plane(block, by, False))
     saved_inputs, early_cotangents, final_cotangent = after(
         (saved_inputs, early_cotangents, final_cotangent), block
@@ -403,6 +402,7 @@
     position = turned(lax.broadcasted_iota(jnp.int32, (tokens, 1), 0))
     early = jnp.where(position < valid_counts[0, 0], moved(early_cotangents[0]), 0)
     final = jnp.where(position < valid_counts[0, 1], moved(final_cotangent), 0)
+    lower_whole = lax.all_gather(after(shard_of(0), final), "dp", axis=0, tiled=True)
     final_groups = [final[i * group : (i + 1) * group] for i in range(SIDE)]
 
     flop = 2 * tokens * width * units

time: 215 us -> 215 us (level)
  waiting for transfers between devices: 64.2 us -> 59.9 us
  starting transfers between devices: 71.1 us -> 74.3 us
    ppermute x24, starting transfers between devices: 37.6 us -> 41.5 us  [from_plane(): return lax.ppermute(value, ('pipe', 'dp'), pairs)]
    ppermute x9, waiting for transfers between devices: 10.2 us -> 7.44 us  [from_z(): return lax.ppermute(value, 'tensor', pairs)]
    unnamed x101 -> x107, local copies, waits for them, and re-layouts: 11.2 us -> 11.3 us
  transfers between devices with their start and end apart: 51 -> 51, of which waited for: 23 -> 22; matrix products, arithmetic and copies ran while one was open for 8% -> 7% of each run, Pallas kernels for 14% -> 14%
where the time goes in v3:
time: 215 us; the launch traced here: 211 us
  starting transfers between devices  74.3 us (35%)
  waiting for transfers between devices  59.9 us (28%)
  Pallas kernels  31.5 us (15%)
  local copies, waits for them, and re-layouts  17.9 us (8%)
  between operations  16.1 us (7%)
  matrix products  7.75 us (4%)
  other arithmetic  3.22 us (1%)
    ppermute x24, waiting for transfers between devices, from_plane(): return lax.ppermute(value, ('pipe', 'dp'), pairs)  45.1 us
    ppermute x24, starting transfers between devices, from_plane(): return lax.ppermute(value, ('pipe', 'dp'), pairs)  41.5 us
    pallas_call x17, Pallas kernels, run(): pl.pallas_call(kernel, out_shape=[jax.ShapeDtypeStruct(o[0], o[1]) for o...  31.5 us
    ppermute x16, starting transfers between devices, across(): return lax.ppermute(value, ('pipe', 'tensor'), pairs)  18.5 us
    ppermute x9, starting transfers between devices, from_z(): return lax.ppermute(value, 'tensor', pairs)  14.2 us
    unnamed x107, local copies, waits for them, and re-layouts  11.3 us
    dot_general x3, matrix products, moved(): return jnp.dot(turned(rows), mover, preferred_element_type=F32).astype(BF16)  7.75 us
    ppermute x9, waiting for transfers between devices, from_z(): return lax.ppermute(value, 'tensor', pairs)  7.44 us
  transfers between devices with their start and end apart: 51, of which 22 were waited for; matrix products, arithmetic and copies ran while one was open for 7% of the time, Pallas kernels for 14%

profile of v3, /device:TPU:0, one launch (start us, length us, event | category | flops | bytes accessed | tf_op | source)
XLA Modules:
  0.0 210.8 jit_solution(12621518627940513004)
XLA Ops:
  7.2 1.3 copy.43
  8.7 1.6 collective-permute-start.2
  10.4 2.7 %collective-permute-start.1 = (bf16[56,1920]{1,0:T(8,128)(2,1)S(1)}, bf16[56,1920]{1,0:T(8,128)(2,1)S(1)}, u32[]{:S(2)}, u32[]{:S(2)}) collective-permute-start(bf16[56,1920]{1,0:T(8,128)(2,1)S(1)} %bitcast.110), channel_id=1, source_target_pairs={{8,0},{12,4},{0,8},{4,12},{24,16},{28,20},{16,24},{20,28},{40,32},... | collective-permute-start | bytes 645128 | tf_op jit(solution)/shard_map/ppermute | solution.py:35
  13.1 1.4 collective-permute-start
  16.0 1.4 broadcast_compare_fusion
  17.4 1.6 collective-permute-done
  19.4 1.0 fusion.35.d
  21.1 1.6 collective-permute-start.5
  22.7 2.9 %collective-permute-start.4 = (bf16[224,1920]{1,0:T(8,128)(2,1)S(1)}, bf16[224,1920]{1,0:T(8,128)(2,1)S(1)}, u32[]{:S(2)}, u32[]{:S(2)}) collective-permute-start(bf16[224,1920]{1,0:T(8,128)(2,1)S(1)} %constant_dynamic-update-slice_fusion.refs_0_.refs_16_), channel_id=1, source_target_pairs={{32,0},{36,4},{40,8},{44,12},{48,16},{52,20},{56,24},{60,28},{0,32... | collective-permute-start | bytes 2580488 | tf_op jit(solution)/shard_map/ppermute | solution.py:35
  25.6 1.9 collective-permute-start.3
  27.5 1.4 dynamic-slice_bitcast_fusion.7
  29.9 1.8 broadcast_select_fusion
  32.7 4.9 %fusion.16 = bf16[2,2,384,896]{3,2,1,0:T(8,128)(2,1)S(1)} fusion(bf16[2,2,96,896]{3,2,1,0:T(8,128)(2,1)S(1)} %get-tuple-element.166, bf16[2,2,96,896]{3,2,1,0:T(8,128)(2,1)S(1)} %get-tuple-element.167, bf16[2,2,96,896]{3,2,1,0:T(8,128)(2,1)S(1)} %get-tuple-element.168, bf16[2,2,96,896]{3,2,1,0:T(8,128)(2,1)S(1)} %get-tuple-element.165, s32[896]{0:T(1024)S(1)} %fusion.61), kind=kOutput, calls=%fused_computation.17 | convolution fusion | flops 2479439872 | bytes 5508608 | tf_op jit(solution)/shard_map/dot_general | solution.py:399
  37.7 1.4 slice_bitcast_fusion.1
  39.0 9.9 %collective-permute-done.4.refs_2_.refs_18_ = bf16[224,1920]{1,0:T(8,128)(2,1)S(1)} collective-permute-done((bf16[224,1920]{1,0:T(8,128)(2,1)S(1)}, bf16[224,1920]{1,0:T(8,128)(2,1)S(1)}, u32[]{:S(2)}, u32[]{:S(2)}) %collective-permute-start.4) | collective-permute-done | bytes 860192 | tf_op jit(solution)/shard_map/ppermute | solution.py:35
  49.0 6.0 %first.1 = (bf16[896,384]{1,0:T(8,128)(2,1)S(1)}, bf16[384,640]{1,0:T(8,128)(2,1)S(1)}, f32[384,640]{1,0:T(8,128)S(1)}, f32[384,640]{1,0:T(8,128)S(1)}, bf16[96,...) custom-call(bf16[384,896]{1,0:T(8,128)(2,1)S(1)} %get-tuple-element., ...), custom_call_target="tpu_custom_call" | custom-call | flops 2202009600 | bytes 8650752 | tf_op jit(solution)/shard_map/first/pallas_call | solution.py:68
  56.7 1.8 collective-permute-start.6
  58.5 3.7 %collective-permute-start.7 = (bf16[96,896]{1,0:T(8,128)(2,1)S(1)}, bf16[96,896]{1,0:T(8,128)(2,1)S(1)}, u32[]{:S(2)}, u32[]{:S(2)}) collective-permute-start(bf16[96,896]{1,0:T(8,128)(2,1)S(1)} %get-tuple-element.94), channel_id=1, source_target_pairs={{2,0},{3,1},{0,2},{1,3},{6,4},{7,5},{4,6},{5,7},{10,8},{11,9},{8,1... | collective-permute-start | bytes 516104 | tf_op jit(solution)/shard_map/ppermute | solution.py:40
  63.2 3.2 %early.2 = (bf16[896,384]{1,0:T(8,128)(2,1)S(1)}, bf16[896,384]{1,0:T(8,128)(2,1)S(1)}, bf16[384,640]{1,0:T(8,128)(2,1)S(1)}, bf16[384,1280]{1,0:T(8,128)(2,1)S(1)}) custom-call(bf16[384,896]{1,0:T(8,128)(2,1)S(1)} %get-tuple-element.87.x, bf16[384,896]{1,0:T(8,128)(2,1)S(1)} %get-tuple-element.170.d, ...), custom_call_target="tpu_custom_call" | custom-call | flops 2202009600 | bytes 7667712 | tf_op jit(solution)/shard_map/early/pallas_call | solution.py:68
  68.9 2.2 %collective-permute-start.11 = (bf16[96,896]{1,0:T(8,128)(2,1)S(1)}, bf16[96,896]{1,0:T(8,128)(2,1)S(1)}, u32[]{:S(2)}, u32[]{:S(2)}) collective-permute-start(bf16[96,896]{1,0:T(8,128)(2,1)S(1)} %mix.3.d), channel_id=1, source_target_pairs={{2,64},{3,65},{0,66},{1,67},{64,0},{65,1},{66,2},{67,3},{6,68},{7,... | collective-permute-start | bytes 516104 | tf_op jit(solution)/shard_map/ppermute | solution.py:46
  71.9 2.0 collective-permute-done.11.refs_6_
  74.0 1.9 collective-permute-done.10.refs_5_
  77.0 4.3 %collective-permute-start.14 = (bf16[96,896]{1,0:T(8,128)(2,1)}, bf16[96,896]{1,0:T(8,128)(2,1)}, u32[]{:S(2)}, u32[]{:S(2)}) collective-permute-start(bf16[96,896]{1,0:T(8,128)(2,1)} %get-tuple-element.102), channel_id=1, source_target_pairs={{67,0},{64,1},{65,2},{66,3},{0,64},{1,65},{2,66},{3,67},{71,4},{68... | collective-permute-start | bytes 516104 | tf_op jit(solution)/shard_map/ppermute | solution.py:46
  81.4 2.3 %collective-permute-start.16 = (bf16[96,896]{1,0:T(8,128)(2,1)}, bf16[96,896]{1,0:T(8,128)(2,1)}, u32[]{:S(2)}, u32[]{:S(2)}) collective-permute-start(bf16[96,896]{1,0:T(8,128)(2,1)} %get-tuple-element.104), channel_id=1, source_target_pairs={{65,0},{66,1},{67,2},{64,3},{0,64},{1,65},{2,66},{3,67},{69,4},{70... | collective-permute-start | bytes 516104 | tf_op jit(solution)/shard_map/ppermute | solution.py:46
  84.0 2.0 copy-done
  85.9 4.0 %order.2.weights.ins.refs_0_ = bf16[896,1280]{1,0:T(8,128)(2,1)S(1)} custom-call(bf16[896,896]{1,0:T(8,128)(2,1)S(1)} %fusion.8.mover, bf16[896,1920]{1,0:T(8,128)(2,1)S(1)} %copy-done), custom_call_target="tpu_custom_call" | custom-call | flops 2055208960 | bytes 7340032 | tf_op jit(solution)/shard_map/order/pallas_call | solution.py:68
  90.0 1.4 mix.4.d
  92.8 2.0 collective-permute-start.18
  94.8 1.4 gate.1
  96.3 1.8 order.3.down.refs_1_.refs_16_
  99.0 3.2 %collective-permute-start.21 = (bf16[96,896]{1,0:T(8,128)(2,1)S(1)}, bf16[96,896]{1,0:T(8,128)(2,1)S(1)}, u32[]{:S(2)}, u32[]{:S(2)}) collective-permute-start(bf16[96,896]{1,0:T(8,128)(2,1)S(1)} %get-tuple-element.109), channel_id=1, source_target_pairs={{64,0},{65,1},{66,2},{67,3},{0,64},{1,65},{2,66},{3,67},{68,4},{69... | collective-permute-start | bytes 516104 | tf_op jit(solution)/shard_map/ppermute | solution.py:46
  102.7 1.6 collective-permute-start.24
  104.5 4.4 %terms.2 = (bf16[224,1920]{1,0:T(8,128)(2,1)S(1)}, bf16[224,1920]{1,0:T(8,128)(2,1)S(1)}, bf16[224,1920]{1,0:T(8,128)(2,1)S(1)}, bf16[224,1920]{1,0:T(8,128)(2,1)S(1)}) custom-call(s32[1]{0:T(128)} %bitcast.4.use_first, bf16[96,896]{1,0:T(8,128)(2,1)S(1)} %get-tuple-element.92.d.refs_0_, bf16[96,896]{1,0:T(8,128)(2,1)S(1)} %copy-done.28, ...), custom_call_target="tpu_custom_call" | custom-call | flops 3082813440 | bytes 14254084 | tf_op jit(solution)/shard_map/terms/pallas_call | solution.py:68
  108.9 1.7 collective-permute-done.23.refs_2_
  111.0 2.0 collective-permute-start.28
  113.0 1.3 collective-permute-start.29
  114.6 3.3 %collective-permute-start.26 = (bf16[96,896]{1,0:T(8,128)(2,1)S(1)}, bf16[96,896]{1,0:T(8,128)(2,1)S(1)}, u32[]{:S(2)}, u32[]{:S(2)}) collective-permute-start(bf16[96,896]{1,0:T(8,128)(2,1)S(1)} %mix.5.refs_4_), channel_id=1, source_target_pairs={{2,0},{3,1},{0,2},{1,3},{6,4},{7,5},{4,6},{5,7},{10,8},{11,9},{8,1... | collective-permute-start | bytes 516104 | tf_op jit(solution)/shard_map/ppermute | solution.py:40
  117.9 2.1 early.3
  120.0 4.6 %collective-permute-done.27.refs_7_ = bf16[96,896]{1,0:T(8,128)(2,1)S(1)} collective-permute-done((bf16[96,896]{1,0:T(8,128)(2,1)S(1)}, bf16[96,896]{1,0:T(8,128)(2,1)S(1)}, u32[]{:S(2)}, u32[]{:S(2)}) %collective-permute-start.27) | collective-permute-done | bytes 172064 | tf_op jit(solution)/shard_map/ppermute | solution.py:40
  125.2 3.1 %collective-permute-start.36 = (bf16[224,1920]{1,0:T(8,128)(2,1)S(1)}, bf16[224,1920]{1,0:T(8,128)(2,1)S(1)}, u32[]{:S(2)}, u32[]{:S(2)}) collective-permute-start(bf16[224,1920]{1,0:T(8,128)(2,1)S(1)} %get-tuple-element.147), channel_id=1, source_target_pairs={{32,0},{36,4},{40,8},{44,12},{48,16},{52,20},{56,24},{60,28},{0,32... | collective-permute-start | bytes 2580488 | tf_op jit(solution)/shard_map/ppermute | solution.py:35
  128.3 3.7 %terms.3 = (bf16[224,1920]{1,0:T(8,128)(2,1)S(1)}, bf16[224,1920]{1,0:T(8,128)(2,1)S(1)}, bf16[224,1920]{1,0:T(8,128)(2,1)S(1)}, bf16[224,1920]{1,0:T(8,128)(2,1)S(1)}) custom-call(s32[1]{0:T(128)S(6)} %sub.36.active.use_first, bf16[96,896]{1,0:T(8,128)(2,1)S(1)} %collective-permute-done.17.refs_0_, bf16[96,896]{1,0:T(8,128)(2,1)S(1)} %collective-permute-done.18.refs_1_, ...), custom_call_target="tpu_custom_call" | custom-call | flops 3082813440 | bytes 11960324 | tf_op jit(solution)/shard_map/terms/pallas_call | solution.py:68
  132.4 3.2 %collective-permute-start.31 = (bf16[224,1920]{1,0:T(8,128)(2,1)S(1)}, bf16[224,1920]{1,0:T(8,128)(2,1)S(1)}, u32[]{:S(2)}, u32[]{:S(2)}) collective-permute-start(bf16[224,1920]{1,0:T(8,128)(2,1)S(1)} %get-tuple-element.139), channel_id=1, source_target_pairs={{32,0},{36,4},{40,8},{44,12},{48,16},{52,20},{56,24},{60,28},{0,32... | collective-permute-start | bytes 2580488 | tf_op jit(solution)/shard_map/ppermute | solution.py:35
  135.6 4.2 %collective-permute-done.36.refs_2_ = bf16[224,1920]{1,0:T(8,128)(2,1)S(1)} collective-permute-done((bf16[224,1920]{1,0:T(8,128)(2,1)S(1)}, bf16[224,1920]{1,0:T(8,128)(2,1)S(1)}, u32[]{:S(2)}, u32[]{:S(2)}) %collective-permute-start.36) | collective-permute-done | bytes 860192 | tf_op jit(solution)/shard_map/ppermute | solution.py:35
  141.1 2.1 %collective-permute-start.38 = (bf16[56,1920]{1,0:T(8,128)(2,1)S(1)}, bf16[56,1920]{1,0:T(8,128)(2,1)S(1)}, u32[]{:S(2)}, u32[]{:S(2)}) collective-permute-start(bf16[56,1920]{1,0:T(8,128)(2,1)S(1)} %get-tuple-element.150), channel_id=1, source_target_pairs={{8,0},{12,4},{0,8},{4,12},{24,16},{28,20},{16,24},{20,28},{40,32},... | collective-permute-start | bytes 645128 | tf_op jit(solution)/shard_map/ppermute | solution.py:35
  143.3 10.3 %collective-permute-done.30.refs_1_ = bf16[224,1920]{1,0:T(8,128)(2,1)S(1)} collective-permute-done((bf16[224,1920]{1,0:T(8,128)(2,1)S(1)}, bf16[224,1920]{1,0:T(8,128)(2,1)S(1)}, u32[]{:S(2)}, u32[]{:S(2)}) %collective-permute-start.30) | collective-permute-done | bytes 860192 | tf_op jit(solution)/shard_map/ppermute | solution.py:35
  153.5 1.5 collective-permute-start.39
  155.0 7.8 %collective-permute-done.31.refs_2_ = bf16[224,1920]{1,0:T(8,128)(2,1)S(1)} collective-permute-done((bf16[224,1920]{1,0:T(8,128)(2,1)S(1)}, bf16[224,1920]{1,0:T(8,128)(2,1)S(1)}, u32[]{:S(2)}, u32[]{:S(2)}) %collective-permute-start.31) | collective-permute-done | bytes 860192 | tf_op jit(solution)/shard_map/ppermute | solution.py:35
  164.2 2.2 %collective-permute-start.34 = (bf16[56,1920]{1,0:T(8,128)(2,1)S(1)}, bf16[56,1920]{1,0:T(8,128)(2,1)S(1)}, u32[]{:S(2)}, u32[]{:S(2)}) collective-permute-start(bf16[56,1920]{1,0:T(8,128)(2,1)S(1)} %get-tuple-element.143), channel_id=1, source_target_pairs={{8,0},{12,4},{0,8},{4,12},{24,16},{28,20},{16,24},{20,28},{40,32},... | collective-permute-start | bytes 645128 | tf_op jit(solution)/shard_map/ppermute | solution.py:35
  166.4 1.4 collective-permute-start.35
  168.1 4.6 %collective-permute-done.33.refs_1_ = bf16[56,1920]{1,0:T(8,128)(2,1)S(1)} collective-permute-done((bf16[56,1920]{1,0:T(8,128)(2,1)S(1)}, bf16[56,1920]{1,0:T(8,128)(2,1)S(1)}, u32[]{:S(2)}, u32[]{:S(2)}) %collective-permute-start.33) | collective-permute-done | bytes 215072 | tf_op jit(solution)/shard_map/ppermute | solution.py:35
  173.9 1.2 collective-permute-done.40
  175.0 1.3 collective-permute-start.43
  176.3 2.9 %collective-permute-start.42 = (f32[8,128]{1,0:T(8,128)S(1)}, f32[8,128]{1,0:T(8,128)S(1)}, u32[]{:S(2)}, u32[]{:S(2)}) collective-permute-start(f32[8,128]{1,0:T(8,128)S(1)} %add.249), channel_id=1, source_target_pairs={{8,0},{12,4},{0,8},{4,12},{24,16},{28,20},{16,24},{20,28},{40,32},... | collective-permute-start | bytes 12296 | tf_op jit(solution)/shard_map/ppermute | solution.py:35
  179.9 1.6 collective-permute-done.42
  181.4 1.4 collective-permute-done.41
  182.8 3.0 %collective-permute-start.46 = (f32[8,128]{1,0:T(8,128)S(1)}, f32[8,128]{1,0:T(8,128)S(1)}, u32[]{:S(2)}, u32[]{:S(2)}) collective-permute-start(f32[8,128]{1,0:T(8,128)S(1)} %add_add_fusion.2), channel_id=1, source_target_pairs={{48,0},{52,4},{56,8},{60,12},{0,16},{4,20},{8,24},{12,28},{16,32},... | collective-permute-start | bytes 12296 | tf_op jit(solution)/shard_map/ppermute | solution.py:35
  186.5 2.1 collective-permute-start.44
  188.6 2.4 %collective-permute-done.45 = f32[8,128]{1,0:T(8,128)S(1)} collective-permute-done((f32[8,128]{1,0:T(8,128)S(1)}, f32[8,128]{1,0:T(8,128)S(1)}, u32[]{:S(2)}, u32[]{:S(2)}) %collective-permute-start.45) | collective-permute-done | bytes 4128 | tf_op jit(solution)/shard_map/ppermute | solution.py:35
  191.0 2.9 %collective-permute-start.48 = (f32[8,128]{1,0:T(8,128)S(1)}, f32[8,128]{1,0:T(8,128)S(1)}, u32[]{:S(2)}, u32[]{:S(2)}) collective-permute-start(f32[8,128]{1,0:T(8,128)S(1)} %add_add_fusion.1), channel_id=1, source_target_pairs={{2,0},{3,1},{0,2},{1,3},{6,4},{7,5},{4,6},{5,7},{10,8},{11,9},{8,1... | collective-permute-start | bytes 12296 | tf_op jit(solution)/shard_map/ppermute | solution.py:40
  193.9 1.2 collective-permute-start.47
  196.2 1.6 collective-permute-done.47
  199.9 1.1 copy.27
  201.0 1.1 copy.26
  202.1 1.3 copy.25
  (195 shorter events, 24.4 us)
Async XLA Ops:
  7.2 12.1 %copy-start.43 = (bf16[384,896]{1,0:T(8,128)(2,1)S(1)}, bf16[384,896]{1,0:T(8,128)(2,1)}, u32[]{:S(2)}) copy-start(bf16[384,896]{1,0:T(8,128)(2,1)} %param.9) | copy-start | bytes 2064388
  7.2 76.8 %all-gather.2.cloned.1.call-start = ((), (), s32[]{:S(2)}) async-start(), calls=%async_computation | async-start | bytes 3655680 | tf_op jit(solution)/shard_map/all_gather | solution.py:405
  8.7 10.5 %collective-permute-start.2 = (bf16[56,1920]{1,0:T(8,128)(2,1)S(1)}, bf16[56,1920]{1,0:T(8,128)(2,1)S(1)}, u32[]{:S(2)}, u32[]{:S(2)}) collective-permute-start(bf16[56,1920]{1,0:T(8,128)(2,1)S(1)} %bitcast.109), channel_id=1, source_target_pairs={{12,0},{0,4},{4,8},{8,12},{28,16},{16,20},{20,24},{24,28},{44,32},... | collective-permute-start | bytes 645128 | tf_op jit(solution)/shard_map/ppermute | solution.py:35
  10.4 8.9 %collective-permute-start.1 = (bf16[56,1920]{1,0:T(8,128)(2,1)S(1)}, bf16[56,1920]{1,0:T(8,128)(2,1)S(1)}, u32[]{:S(2)}, u32[]{:S(2)}) collective-permute-start(bf16[56,1920]{1,0:T(8,128)(2,1)S(1)} %bitcast.110), channel_id=1, source_target_pairs={{8,0},{12,4},{0,8},{4,12},{24,16},{28,20},{16,24},{20,28},{40,32},... | collective-permute-start | bytes 645128 | tf_op jit(solution)/shard_map/ppermute | solution.py:35
  13.1 5.9 %collective-permute-start = (bf16[56,1920]{1,0:T(8,128)(2,1)S(1)}, bf16[56,1920]{1,0:T(8,128)(2,1)S(1)}, u32[]{:S(2)}, u32[]{:S(2)}) collective-permute-start(bf16[56,1920]{1,0:T(8,128)(2,1)S(1)} %bitcast.111), channel_id=1, source_target_pairs={{4,0},{8,4},{12,8},{0,12},{20,16},{24,20},{28,24},{16,28},{36,32},... | collective-permute-start | bytes 645128 | tf_op jit(solution)/shard_map/ppermute | solution.py:35
  16.0 16.8 %copy-start.46 = (s32[896]{0:T(1024)}, s32[896]{0:T(1024)S(1)}, u32[]{:S(2)}) copy-start(s32[896]{0:T(1024)S(1)} %fusion.61) | copy-start | bytes 10756
  19.3 43.9 %copy-start.3 = (bf16[224,1920]{1,0:T(8,128)(2,1)}, bf16[224,1920]{1,0:T(8,128)(2,1)S(1)}, u32[]{:S(2)}) copy-start(bf16[224,1920]{1,0:T(8,128)(2,1)S(1)} %constant_dynamic-update-slice_fusion.refs_0_.refs_16_) | copy-start | bytes 2580484
  21.1 17.9 %collective-permute-start.5 = (bf16[224,1920]{1,0:T(8,128)(2,1)S(1)}, bf16[224,1920]{1,0:T(8,128)(2,1)S(1)}, u32[]{:S(2)}, u32[]{:S(2)}) collective-permute-start(bf16[224,1920]{1,0:T(8,128)(2,1)S(1)} %constant_dynamic-update-slice_fusion.refs_0_.refs_16_), channel_id=1, source_target_pairs={{48,0},{52,4},{56,8},{60,12},{0,16},{4,20},{8,24},{12,28},{16,32},... | collective-permute-start | bytes 2580488 | tf_op jit(solution)/shard_map/ppermute | solution.py:35
  22.7 26.2 %collective-permute-start.4 = (bf16[224,1920]{1,0:T(8,128)(2,1)S(1)}, bf16[224,1920]{1,0:T(8,128)(2,1)S(1)}, u32[]{:S(2)}, u32[]{:S(2)}) collective-permute-start(bf16[224,1920]{1,0:T(8,128)(2,1)S(1)} %constant_dynamic-update-slice_fusion.refs_0_.refs_16_), channel_id=1, source_target_pairs={{32,0},{36,4},{40,8},{44,12},{48,16},{52,20},{56,24},{60,28},{0,32... | collective-permute-start | bytes 2580488 | tf_op jit(solution)/shard_map/ppermute | solution.py:35
  25.6 23.3 %collective-permute-start.3 = (bf16[224,1920]{1,0:T(8,128)(2,1)S(1)}, bf16[224,1920]{1,0:T(8,128)(2,1)S(1)}, u32[]{:S(2)}, u32[]{:S(2)}) collective-permute-start(bf16[224,1920]{1,0:T(8,128)(2,1)S(1)} %constant_dynamic-update-slice_fusion.refs_0_.refs_16_), channel_id=1, source_target_pairs={{16,0},{20,4},{24,8},{28,12},{32,16},{36,20},{40,24},{44,28},{48,3... | collective-permute-start | bytes 2580488 | tf_op jit(solution)/shard_map/ppermute | solution.py:35
  39.0 36.9 %copy-start.10 = (bf16[224,1920]{1,0:T(8,128)(2,1)}, bf16[224,1920]{1,0:T(8,128)(2,1)S(1)}, u32[]{:S(2)}) copy-start(bf16[224,1920]{1,0:T(8,128)(2,1)S(1)} %collective-permute-done.5.refs_3_.refs_19_) | copy-start | bytes 2580484
  49.0 27.0 %copy-start.12 = (bf16[224,1920]{1,0:T(8,128)(2,1)}, bf16[224,1920]{1,0:T(8,128)(2,1)S(1)}, u32[]{:S(2)}) copy-start(bf16[224,1920]{1,0:T(8,128)(2,1)S(1)} %collective-permute-done.4.refs_2_.refs_18_) | copy-start | bytes 2580484
  49.0 27.0 %copy-start.14 = (bf16[224,1920]{1,0:T(8,128)(2,1)}, bf16[224,1920]{1,0:T(8,128)(2,1)S(1)}, u32[]{:S(2)}) copy-start(bf16[224,1920]{1,0:T(8,128)(2,1)S(1)} %collective-permute-done.3.refs_1_.refs_17_) | copy-start | bytes 2580484
  56.7 19.3 %copy-start.6 = (f32[384,640]{1,0:T(8,128)}, f32[384,640]{1,0:T(8,128)S(1)}, u32[]{:S(2)}) copy-start(f32[384,640]{1,0:T(8,128)S(1)} %get-tuple-element.97.slope.refs_14_) | copy-start | bytes 2949124
  56.7 19.3 %copy-start.8 = (f32[384,640]{1,0:T(8,128)}, f32[384,640]{1,0:T(8,128)S(1)}, u32[]{:S(2)}) copy-start(f32[384,640]{1,0:T(8,128)S(1)} %get-tuple-element.98.activated.refs_15_) | copy-start | bytes 2949124
  56.7 11.5 %collective-permute-start.6 = (bf16[96,896]{1,0:T(8,128)(2,1)S(1)}, bf16[96,896]{1,0:T(8,128)(2,1)S(1)}, u32[]{:S(2)}, u32[]{:S(2)}) collective-permute-start(bf16[96,896]{1,0:T(8,128)(2,1)S(1)} %get-tuple-element.93), channel_id=1, source_target_pairs={{3,0},{0,1},{1,2},{2,3},{7,4},{4,5},{5,6},{6,7},{11,8},{8,9},{9,10... | collective-permute-start | bytes 516104 | tf_op jit(solution)/shard_map/ppermute | solution.py:40
  58.5 9.7 %collective-permute-start.7 = (bf16[96,896]{1,0:T(8,128)(2,1)S(1)}, bf16[96,896]{1,0:T(8,128)(2,1)S(1)}, u32[]{:S(2)}, u32[]{:S(2)}) collective-permute-start(bf16[96,896]{1,0:T(8,128)(2,1)S(1)} %get-tuple-element.94), channel_id=1, source_target_pairs={{2,0},{3,1},{0,2},{1,3},{6,4},{7,5},{4,6},{5,7},{10,8},{11,9},{8,1... | collective-permute-start | bytes 516104 | tf_op jit(solution)/shard_map/ppermute | solution.py:40
  62.2 6.0 %collective-permute-start.8 = (bf16[96,896]{1,0:T(8,128)(2,1)S(1)}, bf16[96,896]{1,0:T(8,128)(2,1)S(1)}, u32[]{:S(2)}, u32[]{:S(2)}) collective-permute-start(bf16[96,896]{1,0:T(8,128)(2,1)S(1)} %get-tuple-element.95), channel_id=1, source_target_pairs={{1,0},{2,1},{3,2},{0,3},{5,4},{6,5},{7,6},{4,7},{9,8},{10,9},{11,1... | collective-permute-start | bytes 516104 | tf_op jit(solution)/shard_map/ppermute | solution.py:40
  68.6 3.3 %collective-permute-start.12 = (bf16[96,896]{1,0:T(8,128)(2,1)S(1)}, bf16[96,896]{1,0:T(8,128)(2,1)S(1)}, u32[]{:S(2)}, u32[]{:S(2)}) collective-permute-start(bf16[96,896]{1,0:T(8,128)(2,1)S(1)} %mix.3.d), channel_id=1, source_target_pairs={{3,64},{0,65},{1,66},{2,67},{64,0},{65,1},{66,2},{67,3},{7,68},{4,... | collective-permute-start | bytes 516104 | tf_op jit(solution)/shard_map/ppermute | solution.py:46
  68.9 5.1 %collective-permute-start.11 = (bf16[96,896]{1,0:T(8,128)(2,1)S(1)}, bf16[96,896]{1,0:T(8,128)(2,1)S(1)}, u32[]{:S(2)}, u32[]{:S(2)}) collective-permute-start(bf16[96,896]{1,0:T(8,128)(2,1)S(1)} %mix.3.d), channel_id=1, source_target_pairs={{2,64},{3,65},{0,66},{1,67},{64,0},{65,1},{66,2},{67,3},{6,68},{7,... | collective-permute-start | bytes 516104 | tf_op jit(solution)/shard_map/ppermute | solution.py:46
  71.1 4.9 %collective-permute-start.10 = (bf16[96,896]{1,0:T(8,128)(2,1)S(1)}, bf16[96,896]{1,0:T(8,128)(2,1)S(1)}, u32[]{:S(2)}, u32[]{:S(2)}) collective-permute-start(bf16[96,896]{1,0:T(8,128)(2,1)S(1)} %mix.3.d), channel_id=1, source_target_pairs={{1,64},{2,65},{3,66},{0,67},{64,0},{65,1},{66,2},{67,3},{5,68},{6,... | collective-permute-start | bytes 516104 | tf_op jit(solution)/shard_map/ppermute | solution.py:46
  71.2 4.8 %collective-permute-start.9 = (bf16[96,896]{1,0:T(8,128)(2,1)S(1)}, bf16[96,896]{1,0:T(8,128)(2,1)S(1)}, u32[]{:S(2)}, u32[]{:S(2)}) collective-permute-start(bf16[96,896]{1,0:T(8,128)(2,1)S(1)} %mix.3.d), channel_id=1, source_target_pairs={{0,64},{1,65},{2,66},{3,67},{64,0},{65,1},{66,2},{67,3},{4,68},{5,... | collective-permute-start | bytes 516104 | tf_op jit(solution)/shard_map/ppermute | solution.py:46
  77.0 12.9 %collective-permute-start.14 = (bf16[96,896]{1,0:T(8,128)(2,1)}, bf16[96,896]{1,0:T(8,128)(2,1)}, u32[]{:S(2)}, u32[]{:S(2)}) collective-permute-start(bf16[96,896]{1,0:T(8,128)(2,1)} %get-tuple-element.102), channel_id=1, source_target_pairs={{67,0},{64,1},{65,2},{66,3},{0,64},{1,65},{2,66},{3,67},{71,4},{68... | collective-permute-start | bytes 516104 | tf_op jit(solution)/shard_map/ppermute | solution.py:46
  81.3 8.7 %collective-permute-start.15 = (bf16[96,896]{1,0:T(8,128)(2,1)}, bf16[96,896]{1,0:T(8,128)(2,1)}, u32[]{:S(2)}, u32[]{:S(2)}) collective-permute-start(bf16[96,896]{1,0:T(8,128)(2,1)} %get-tuple-element.103), channel_id=1, source_target_pairs={{66,0},{67,1},{64,2},{65,3},{0,64},{1,65},{2,66},{3,67},{70,4},{71... | collective-permute-start | bytes 516104 | tf_op jit(solution)/shard_map/ppermute | solution.py:46
  81.4 8.6 %collective-permute-start.16 = (bf16[96,896]{1,0:T(8,128)(2,1)}, bf16[96,896]{1,0:T(8,128)(2,1)}, u32[]{:S(2)}, u32[]{:S(2)}) collective-permute-start(bf16[96,896]{1,0:T(8,128)(2,1)} %get-tuple-element.104), channel_id=1, source_target_pairs={{65,0},{66,1},{67,2},{64,3},{0,64},{1,65},{2,66},{3,67},{69,4},{70... | collective-permute-start | bytes 516104 | tf_op jit(solution)/shard_map/ppermute | solution.py:46
  83.7 6.3 %collective-permute-start.13 = (bf16[96,896]{1,0:T(8,128)(2,1)}, bf16[96,896]{1,0:T(8,128)(2,1)}, u32[]{:S(2)}, u32[]{:S(2)}) collective-permute-start(bf16[96,896]{1,0:T(8,128)(2,1)} %get-tuple-element.99), channel_id=1, source_target_pairs={{64,0},{65,1},{66,2},{67,3},{0,64},{1,65},{2,66},{3,67},{68,4},{69... | collective-permute-start | bytes 516104 | tf_op jit(solution)/shard_map/ppermute | solution.py:46
  91.5 6.6 %collective-permute-start.20 = (bf16[96,896]{1,0:T(8,128)(2,1)S(1)}, bf16[96,896]{1,0:T(8,128)(2,1)S(1)}, u32[]{:S(2)}, u32[]{:S(2)}) collective-permute-start(bf16[96,896]{1,0:T(8,128)(2,1)S(1)} %mix.4.d), channel_id=1, source_target_pairs={{3,64},{0,65},{1,66},{2,67},{64,0},{65,1},{66,2},{67,3},{7,68},{4,... | collective-permute-start | bytes 516104 | tf_op jit(solution)/shard_map/ppermute | solution.py:46
  92.4 5.7 %collective-permute-start.19 = (bf16[96,896]{1,0:T(8,128)(2,1)S(1)}, bf16[96,896]{1,0:T(8,128)(2,1)S(1)}, u32[]{:S(2)}, u32[]{:S(2)}) collective-permute-start(bf16[96,896]{1,0:T(8,128)(2,1)S(1)} %mix.4.d), channel_id=1, source_target_pairs={{2,64},{3,65},{0,66},{1,67},{64,0},{65,1},{66,2},{67,3},{6,68},{7,... | collective-permute-start | bytes 516104 | tf_op jit(solution)/shard_map/ppermute | solution.py:46
  92.8 5.8 %collective-permute-start.18 = (bf16[96,896]{1,0:T(8,128)(2,1)S(1)}, bf16[96,896]{1,0:T(8,128)(2,1)S(1)}, u32[]{:S(2)}, u32[]{:S(2)}) collective-permute-start(bf16[96,896]{1,0:T(8,128)(2,1)S(1)} %mix.4.d), channel_id=1, source_target_pairs={{1,64},{2,65},{3,66},{0,67},{64,0},{65,1},{66,2},{67,3},{5,68},{6,... | collective-permute-start | bytes 516104 | tf_op jit(solution)/shard_map/ppermute | solution.py:46
  94.7 3.8 %collective-permute-start.17 = (bf16[96,896]{1,0:T(8,128)(2,1)S(1)}, bf16[96,896]{1,0:T(8,128)(2,1)S(1)}, u32[]{:S(2)}, u32[]{:S(2)}) collective-permute-start(bf16[96,896]{1,0:T(8,128)(2,1)S(1)} %mix.4.d), channel_id=1, source_target_pairs={{0,64},{1,65},{2,66},{3,67},{64,0},{65,1},{66,2},{67,3},{4,68},{5,... | collective-permute-start | bytes 516104 | tf_op jit(solution)/shard_map/ppermute | solution.py:46
  99.0 11.7 %collective-permute-start.21 = (bf16[96,896]{1,0:T(8,128)(2,1)S(1)}, bf16[96,896]{1,0:T(8,128)(2,1)S(1)}, u32[]{:S(2)}, u32[]{:S(2)}) collective-permute-start(bf16[96,896]{1,0:T(8,128)(2,1)S(1)} %get-tuple-element.109), channel_id=1, source_target_pairs={{64,0},{65,1},{66,2},{67,3},{0,64},{1,65},{2,66},{3,67},{68,4},{69... | collective-permute-start | bytes 516104 | tf_op jit(solution)/shard_map/ppermute | solution.py:46
  102.1 6.8 %collective-permute-start.22 = (bf16[96,896]{1,0:T(8,128)(2,1)S(1)}, bf16[96,896]{1,0:T(8,128)(2,1)S(1)}, u32[]{:S(2)}, u32[]{:S(2)}) collective-permute-start(bf16[96,896]{1,0:T(8,128)(2,1)S(1)} %get-tuple-element.118), channel_id=1, source_target_pairs={{67,0},{64,1},{65,2},{66,3},{0,64},{1,65},{2,66},{3,67},{71,4},{68... | collective-permute-start | bytes 516104 | tf_op jit(solution)/shard_map/ppermute | solution.py:46
  102.2 8.5 %collective-permute-start.23 = (bf16[96,896]{1,0:T(8,128)(2,1)S(1)}, bf16[96,896]{1,0:T(8,128)(2,1)S(1)}, u32[]{:S(2)}, u32[]{:S(2)}) collective-permute-start(bf16[96,896]{1,0:T(8,128)(2,1)S(1)} %get-tuple-element.119), channel_id=1, source_target_pairs={{66,0},{67,1},{64,2},{65,3},{0,64},{1,65},{2,66},{3,67},{70,4},{71... | collective-permute-start | bytes 516104 | tf_op jit(solution)/shard_map/ppermute | solution.py:46
  102.7 7.9 %collective-permute-start.24 = (bf16[96,896]{1,0:T(8,128)(2,1)S(1)}, bf16[96,896]{1,0:T(8,128)(2,1)S(1)}, u32[]{:S(2)}, u32[]{:S(2)}) collective-permute-start(bf16[96,896]{1,0:T(8,128)(2,1)S(1)} %get-tuple-element.120), channel_id=1, source_target_pairs={{65,0},{66,1},{67,2},{64,3},{0,64},{1,65},{2,66},{3,67},{69,4},{70... | collective-permute-start | bytes 516104 | tf_op jit(solution)/shard_map/ppermute | solution.py:46
  104.5 13.4 %copy-start.16 = (bf16[384,896]{1,0:T(8,128)(2,1)S(1)}, bf16[384,896]{1,0:T(8,128)(2,1)}, u32[]{:S(2)}) copy-start(bf16[384,896]{1,0:T(8,128)(2,1)} %get-tuple-element.169.d) | copy-start | bytes 2064388
  104.5 13.4 %copy-start.17 = (bf16[384,896]{1,0:T(8,128)(2,1)S(1)}, bf16[384,896]{1,0:T(8,128)(2,1)}, u32[]{:S(2)}) copy-start(bf16[384,896]{1,0:T(8,128)(2,1)} %get-tuple-element.121.x) | copy-start | bytes 2064388
  111.0 17.3 %collective-permute-start.28 = (bf16[224,1920]{1,0:T(8,128)(2,1)S(1)}, bf16[224,1920]{1,0:T(8,128)(2,1)S(1)}, u32[]{:S(2)}, u32[]{:S(2)}) collective-permute-start(bf16[224,1920]{1,0:T(8,128)(2,1)S(1)} %get-tuple-element.129), channel_id=1, source_target_pairs={{48,0},{52,4},{56,8},{60,12},{0,16},{4,20},{8,24},{12,28},{16,32},... | collective-permute-start | bytes 2580488 | tf_op jit(solution)/shard_map/ppermute | solution.py:35
  113.0 15.3 %collective-permute-start.29 = (bf16[224,1920]{1,0:T(8,128)(2,1)S(1)}, bf16[224,1920]{1,0:T(8,128)(2,1)S(1)}, u32[]{:S(2)}, u32[]{:S(2)}) collective-permute-start(bf16[224,1920]{1,0:T(8,128)(2,1)S(1)} %get-tuple-element.130), channel_id=1, source_target_pairs={{16,0},{20,4},{24,8},{28,12},{32,16},{36,20},{40,24},{44,28},{48,3... | collective-permute-start | bytes 2580488 | tf_op jit(solution)/shard_map/ppermute | solution.py:35
  114.3 10.2 %collective-permute-start.27 = (bf16[96,896]{1,0:T(8,128)(2,1)S(1)}, bf16[96,896]{1,0:T(8,128)(2,1)S(1)}, u32[]{:S(2)}, u32[]{:S(2)}) collective-permute-start(bf16[96,896]{1,0:T(8,128)(2,1)S(1)} %mix.5.refs_4_), channel_id=1, source_target_pairs={{3,0},{0,1},{1,2},{2,3},{7,4},{4,5},{5,6},{6,7},{11,8},{8,9},{9,10... | collective-permute-start | bytes 516104 | tf_op jit(solution)/shard_map/ppermute | solution.py:40
  114.6 10.0 %collective-permute-start.26 = (bf16[96,896]{1,0:T(8,128)(2,1)S(1)}, bf16[96,896]{1,0:T(8,128)(2,1)S(1)}, u32[]{:S(2)}, u32[]{:S(2)}) collective-permute-start(bf16[96,896]{1,0:T(8,128)(2,1)S(1)} %mix.5.refs_4_), channel_id=1, source_target_pairs={{2,0},{3,1},{0,2},{1,3},{6,4},{7,5},{4,6},{5,7},{10,8},{11,9},{8,1... | collective-permute-start | bytes 516104 | tf_op jit(solution)/shard_map/ppermute | solution.py:40
  117.9 7.3 %collective-permute-start.25 = (bf16[96,896]{1,0:T(8,128)(2,1)S(1)}, bf16[96,896]{1,0:T(8,128)(2,1)S(1)}, u32[]{:S(2)}, u32[]{:S(2)}) collective-permute-start(bf16[96,896]{1,0:T(8,128)(2,1)S(1)} %mix.5.refs_4_), channel_id=1, source_target_pairs={{1,0},{2,1},{3,2},{0,3},{5,4},{6,5},{7,6},{4,7},{9,8},{10,9},{11,1... | collective-permute-start | bytes 516104 | tf_op jit(solution)/shard_map/ppermute | solution.py:40
  125.2 14.6 %collective-permute-start.36 = (bf16[224,1920]{1,0:T(8,128)(2,1)S(1)}, bf16[224,1920]{1,0:T(8,128)(2,1)S(1)}, u32[]{:S(2)}, u32[]{:S(2)}) collective-permute-start(bf16[224,1920]{1,0:T(8,128)(2,1)S(1)} %get-tuple-element.147), channel_id=1, source_target_pairs={{32,0},{36,4},{40,8},{44,12},{48,16},{52,20},{56,24},{60,28},{0,32... | collective-permute-start | bytes 2580488 | tf_op jit(solution)/shard_map/ppermute | solution.py:35
  132.1 21.5 %collective-permute-start.30 = (bf16[224,1920]{1,0:T(8,128)(2,1)S(1)}, bf16[224,1920]{1,0:T(8,128)(2,1)S(1)}, u32[]{:S(2)}, u32[]{:S(2)}) collective-permute-start(bf16[224,1920]{1,0:T(8,128)(2,1)S(1)} %get-tuple-element.138), channel_id=1, source_target_pairs={{48,0},{52,4},{56,8},{60,12},{0,16},{4,20},{8,24},{12,28},{16,32},... | collective-permute-start | bytes 2580488 | tf_op jit(solution)/shard_map/ppermute | solution.py:35
  132.4 30.4 %collective-permute-start.31 = (bf16[224,1920]{1,0:T(8,128)(2,1)S(1)}, bf16[224,1920]{1,0:T(8,128)(2,1)S(1)}, u32[]{:S(2)}, u32[]{:S(2)}) collective-permute-start(bf16[224,1920]{1,0:T(8,128)(2,1)S(1)} %get-tuple-element.139), channel_id=1, source_target_pairs={{32,0},{36,4},{40,8},{44,12},{48,16},{52,20},{56,24},{60,28},{0,32... | collective-permute-start | bytes 2580488 | tf_op jit(solution)/shard_map/ppermute | solution.py:35
  135.6 27.2 %collective-permute-start.32 = (bf16[224,1920]{1,0:T(8,128)(2,1)S(1)}, bf16[224,1920]{1,0:T(8,128)(2,1)S(1)}, u32[]{:S(2)}, u32[]{:S(2)}) collective-permute-start(bf16[224,1920]{1,0:T(8,128)(2,1)S(1)} %get-tuple-element.140), channel_id=1, source_target_pairs={{16,0},{20,4},{24,8},{28,12},{32,16},{36,20},{40,24},{44,28},{48,3... | collective-permute-start | bytes 2580488 | tf_op jit(solution)/shard_map/ppermute | solution.py:35
  140.2 26.2 %collective-permute-start.37 = (bf16[56,1920]{1,0:T(8,128)(2,1)S(1)}, bf16[56,1920]{1,0:T(8,128)(2,1)S(1)}, u32[]{:S(2)}, u32[]{:S(2)}) collective-permute-start(bf16[56,1920]{1,0:T(8,128)(2,1)S(1)} %get-tuple-element.149), channel_id=1, source_target_pairs={{12,0},{0,4},{4,8},{8,12},{28,16},{16,20},{20,24},{24,28},{44,32},... | collective-permute-start | bytes 645128 | tf_op jit(solution)/shard_map/ppermute | solution.py:35
  141.1 26.7 %collective-permute-start.38 = (bf16[56,1920]{1,0:T(8,128)(2,1)S(1)}, bf16[56,1920]{1,0:T(8,128)(2,1)S(1)}, u32[]{:S(2)}, u32[]{:S(2)}) collective-permute-start(bf16[56,1920]{1,0:T(8,128)(2,1)S(1)} %get-tuple-element.150), channel_id=1, source_target_pairs={{8,0},{12,4},{0,8},{4,12},{24,16},{28,20},{16,24},{20,28},{40,32},... | collective-permute-start | bytes 645128 | tf_op jit(solution)/shard_map/ppermute | solution.py:35
  153.5 14.3 %collective-permute-start.39 = (bf16[56,1920]{1,0:T(8,128)(2,1)S(1)}, bf16[56,1920]{1,0:T(8,128)(2,1)S(1)}, u32[]{:S(2)}, u32[]{:S(2)}) collective-permute-start(bf16[56,1920]{1,0:T(8,128)(2,1)S(1)} %get-tuple-element.151), channel_id=1, source_target_pairs={{4,0},{8,4},{12,8},{0,12},{20,16},{24,20},{28,24},{16,28},{36,32},... | collective-permute-start | bytes 645128 | tf_op jit(solution)/shard_map/ppermute | solution.py:35
  163.3 9.5 %collective-permute-start.33 = (bf16[56,1920]{1,0:T(8,128)(2,1)S(1)}, bf16[56,1920]{1,0:T(8,128)(2,1)S(1)}, u32[]{:S(2)}, u32[]{:S(2)}) collective-permute-start(bf16[56,1920]{1,0:T(8,128)(2,1)S(1)} %get-tuple-element.142), channel_id=1, source_target_pairs={{12,0},{0,4},{4,8},{8,12},{28,16},{16,20},{20,24},{24,28},{44,32},... | collective-permute-start | bytes 645128 | tf_op jit(solution)/shard_map/ppermute | solution.py:35
  164.2 8.5 %collective-permute-start.34 = (bf16[56,1920]{1,0:T(8,128)(2,1)S(1)}, bf16[56,1920]{1,0:T(8,128)(2,1)S(1)}, u32[]{:S(2)}, u32[]{:S(2)}) collective-permute-start(bf16[56,1920]{1,0:T(8,128)(2,1)S(1)} %get-tuple-element.143), channel_id=1, source_target_pairs={{8,0},{12,4},{0,8},{4,12},{24,16},{28,20},{16,24},{20,28},{40,32},... | collective-permute-start | bytes 645128 | tf_op jit(solution)/shard_map/ppermute | solution.py:35
  166.4 7.2 %collective-permute-start.35 = (bf16[56,1920]{1,0:T(8,128)(2,1)S(1)}, bf16[56,1920]{1,0:T(8,128)(2,1)S(1)}, u32[]{:S(2)}, u32[]{:S(2)}) collective-permute-start(bf16[56,1920]{1,0:T(8,128)(2,1)S(1)} %get-tuple-element.144), channel_id=1, source_target_pairs={{4,0},{8,4},{12,8},{0,12},{20,16},{24,20},{28,24},{16,28},{36,32},... | collective-permute-start | bytes 645128 | tf_op jit(solution)/shard_map/ppermute | solution.py:35
  168.1 30.9 %copy-start.41 = (f32[1,56,2,3,640]{4,2,3,1,0:T(2,128)S(1)}, f32[1,56,2,3,640]{4,2,3,1,0:T(2,128)}, u32[]{:S(2)}) copy-start(f32[1,56,2,3,640]{4,2,3,1,0:T(2,128)} %param.11) | copy-start | bytes 2580484
  168.1 30.9 %copy-start.44 = (bf16[1,56,2,3,640]{4,2,3,1,0:T(2,128)(2,1)S(1)}, bf16[1,56,2,3,640]{4,2,3,1,0:T(2,128)(2,1)}, u32[]{:S(2)}) copy-start(bf16[1,56,2,3,640]{4,2,3,1,0:T(2,128)(2,1)} %param.13) | copy-start | bytes 1290244
  168.1 30.9 %copy-start.45 = (bf16[1,56,2,3,640]{4,2,3,1,0:T(2,128)(2,1)S(1)}, bf16[1,56,2,3,640]{4,2,3,1,0:T(2,128)(2,1)}, u32[]{:S(2)}) copy-start(bf16[1,56,2,3,640]{4,2,3,1,0:T(2,128)(2,1)} %param.12) | copy-start | bytes 1290244
  173.9 1.2 collective-permute-start.40
  175.0 4.8 %collective-permute-start.43 = (f32[8,128]{1,0:T(8,128)S(1)}, f32[8,128]{1,0:T(8,128)S(1)}, u32[]{:S(2)}, u32[]{:S(2)}) collective-permute-start(f32[8,128]{1,0:T(8,128)S(1)} %add.249), channel_id=1, source_target_pairs={{12,0},{0,4},{4,8},{8,12},{28,16},{16,20},{20,24},{24,28},{44,32},... | collective-permute-start | bytes 12296 | tf_op jit(solution)/shard_map/ppermute | solution.py:35
  176.3 5.1 %collective-permute-start.42 = (f32[8,128]{1,0:T(8,128)S(1)}, f32[8,128]{1,0:T(8,128)S(1)}, u32[]{:S(2)}, u32[]{:S(2)}) collective-permute-start(f32[8,128]{1,0:T(8,128)S(1)} %add.249), channel_id=1, source_target_pairs={{8,0},{12,4},{0,8},{4,12},{24,16},{28,20},{16,24},{20,28},{40,32},... | collective-permute-start | bytes 12296 | tf_op jit(solution)/shard_map/ppermute | solution.py:35
  179.2 3.6 %collective-permute-start.41 = (f32[8,128]{1,0:T(8,128)S(1)}, f32[8,128]{1,0:T(8,128)S(1)}, u32[]{:S(2)}, u32[]{:S(2)}) collective-permute-start(f32[8,128]{1,0:T(8,128)S(1)} %add.249), channel_id=1, source_target_pairs={{4,0},{8,4},{12,8},{0,12},{20,16},{24,20},{28,24},{16,28},{36,32},... | collective-permute-start | bytes 12296 | tf_op jit(solution)/shard_map/ppermute | solution.py:35
  182.8 5.8 %collective-permute-start.46 = (f32[8,128]{1,0:T(8,128)S(1)}, f32[8,128]{1,0:T(8,128)S(1)}, u32[]{:S(2)}, u32[]{:S(2)}) collective-permute-start(f32[8,128]{1,0:T(8,128)S(1)} %add_add_fusion.2), channel_id=1, source_target_pairs={{48,0},{52,4},{56,8},{60,12},{0,16},{4,20},{8,24},{12,28},{16,32},... | collective-permute-start | bytes 12296 | tf_op jit(solution)/shard_map/ppermute | solution.py:35
  185.8 5.1 %collective-permute-start.45 = (f32[8,128]{1,0:T(8,128)S(1)}, f32[8,128]{1,0:T(8,128)S(1)}, u32[]{:S(2)}, u32[]{:S(2)}) collective-permute-start(f32[8,128]{1,0:T(8,128)S(1)} %add_add_fusion.2), channel_id=1, source_target_pairs={{32,0},{36,4},{40,8},{44,12},{48,16},{52,20},{56,24},{60,28},{0,32... | collective-permute-start | bytes 12296 | tf_op jit(solution)/shard_map/ppermute | solution.py:35
  186.5 4.4 %collective-permute-start.44 = (f32[8,128]{1,0:T(8,128)S(1)}, f32[8,128]{1,0:T(8,128)S(1)}, u32[]{:S(2)}, u32[]{:S(2)}) collective-permute-start(f32[8,128]{1,0:T(8,128)S(1)} %add_add_fusion.2), channel_id=1, source_target_pairs={{16,0},{20,4},{24,8},{28,12},{32,16},{36,20},{40,24},{44,28},{48,3... | collective-permute-start | bytes 12296 | tf_op jit(solution)/shard_map/ppermute | solution.py:35
  190.9 4.9 %collective-permute-start.49 = (f32[8,128]{1,0:T(8,128)S(1)}, f32[8,128]{1,0:T(8,128)S(1)}, u32[]{:S(2)}, u32[]{:S(2)}) collective-permute-start(f32[8,128]{1,0:T(8,128)S(1)} %add_add_fusion.1), channel_id=1, source_target_pairs={{3,0},{0,1},{1,2},{2,3},{7,4},{4,5},{5,6},{6,7},{11,8},{8,9},{9,10... | collective-permute-start | bytes 12296 | tf_op jit(solution)/shard_map/ppermute | solution.py:40
  191.0 5.2 %collective-permute-start.48 = (f32[8,128]{1,0:T(8,128)S(1)}, f32[8,128]{1,0:T(8,128)S(1)}, u32[]{:S(2)}, u32[]{:S(2)}) collective-permute-start(f32[8,128]{1,0:T(8,128)S(1)} %add_add_fusion.1), channel_id=1, source_target_pairs={{2,0},{3,1},{0,2},{1,3},{6,4},{7,5},{4,6},{5,7},{10,8},{11,9},{8,1... | collective-permute-start | bytes 12296 | tf_op jit(solution)/shard_map/ppermute | solution.py:40
  193.9 3.9 %collective-permute-start.47 = (f32[8,128]{1,0:T(8,128)S(1)}, f32[8,128]{1,0:T(8,128)S(1)}, u32[]{:S(2)}, u32[]{:S(2)}) collective-permute-start(f32[8,128]{1,0:T(8,128)S(1)} %add_add_fusion.1), channel_id=1, source_target_pairs={{1,0},{2,1},{3,2},{0,3},{5,4},{6,5},{7,6},{4,7},{9,8},{10,9},{11,1... | collective-permute-start | bytes 12296 | tf_op jit(solution)/shard_map/ppermute | solution.py:40
  (36 other events, 198.1 us)
Sparse Core Ops, SparseCore 0:
  20.6 55.2 all-gather.1

commit v4 on v1

--- a/solution.py
+++ b/solution.py
@@ -540,9 +540,9 @@
     cot0 = shared_groups(mine0)
     upper_got = near_pieces(after(upper_terms, mine0))
     early_zero = early_parts(0, after(inputs[0, 0], mine0), [lower_ins, lower_down])
-    upper_got |= far_piece(after(upper_terms[2], cot0))
     early_zero = after(early_zero, [upper_got[by] for by in (1, 3)])
     lower_terms = terms(on_second, cot1, cot0, early_zero, lower_half, [lower_down])
+    upper_got |= far_piece(after(upper_terms[2], lower_terms[0]))
 
     lower_got = near_pieces(lower_terms) | far_piece(lower_terms[2])
     upper_sums = add_pieces(after(upper_terms[0], lower_terms[0]), upper_got)

time: 215 us -> 219 us (1.019)
  starting transfers between devices: 71.1 us -> 75.2 us
    ppermute x9, waiting for transfers between devices: 10.2 us -> 5.12 us  [from_z(): return lax.ppermute(value, 'tensor', pairs)]
    ppermute x24, waiting for transfers between devices: 46.9 us -> 51.8 us  [from_plane(): return lax.ppermute(value, ('pipe', 'dp'), pairs)]
    ppermute x24, starting transfers between devices: 37.6 us -> 42 us  [from_plane(): return lax.ppermute(value, ('pipe', 'dp'), pairs)]
  transfers between devices with their start and end apart: 51 -> 51, of which waited for: 23 -> 25; matrix products, arithmetic and copies ran while one was open for 8% -> 8% of each run, Pallas kernels for 14% -> 12%
where the time goes in v4:
time: 219 us; the launch traced here: 215 us
  starting transfers between devices  75.2 us (34%)
  waiting for transfers between devices  64 us (29%)
  Pallas kernels  31.6 us (14%)
  local copies, waits for them, and re-layouts  17.8 us (8%)
  between operations  16 us (7%)
  matrix products  7.74 us (4%)
  other arithmetic  3.23 us (1%)
    ppermute x24, waiting for transfers between devices, from_plane(): return lax.ppermute(value, ('pipe', 'dp'), pairs)  51.8 us
    ppermute x24, starting transfers between devices, from_plane(): return lax.ppermute(value, ('pipe', 'dp'), pairs)  42 us
    pallas_call x17, Pallas kernels, run(): pl.pallas_call(kernel, out_shape=[jax.ShapeDtypeStruct(o[0], o[1]) for o...  31.6 us
    ppermute x16, starting transfers between devices, across(): return lax.ppermute(value, ('pipe', 'tensor'), pairs)  18.9 us
    ppermute x9, starting transfers between devices, from_z(): return lax.ppermute(value, 'tensor', pairs)  14.2 us
    unnamed x101, local copies, waits for them, and re-layouts  11.2 us
    dot_general x3, matrix products, moved(): return jnp.dot(turned(rows), mover, preferred_element_type=F32).astype(BF16)  7.74 us
    ppermute x16, waiting for transfers between devices, across(): return lax.ppermute(value, ('pipe', 'tensor'), pairs)  5.86 us
  transfers between devices with their start and end apart: 51, of which 25 were waited for; matrix products, arithmetic and copies ran while one was open for 8% of the time, Pallas kernels for 12%

profile of v4, /device:TPU:0, one launch (start us, length us, event | category | flops | bytes accessed | tf_op | source)
XLA Modules:
  0.0 215.4 jit_solution(8175050440356511658)
XLA Ops:
  7.2 1.2 copy.43
  9.5 1.6 collective-permute-start.2
  11.1 2.7 %collective-permute-start.1 = (bf16[56,1920]{1,0:T(8,128)(2,1)S(1)}, bf16[56,1920]{1,0:T(8,128)(2,1)}, u32[]{:S(2)}, u32[]{:S(2)}) collective-permute-start(bf16[56,1920]{1,0:T(8,128)(2,1)S(1)} %bitcast.110), channel_id=1, source_target_pairs={{8,0},{12,4},{0,8},{4,12},{24,16},{28,20},{16,24},{20,28},{40,32},... | collective-permute-start | bytes 645128 | tf_op jit(solution)/shard_map/ppermute | solution.py:35
  13.9 1.4 collective-permute-start
  15.9 1.4 broadcast_compare_fusion
  18.0 2.0 collective-permute-done
  21.9 1.7 collective-permute-start.5
  23.6 2.9 %collective-permute-start.4 = (bf16[224,1920]{1,0:T(8,128)(2,1)S(1)}, bf16[224,1920]{1,0:T(8,128)(2,1)S(1)}, u32[]{:S(2)}, u32[]{:S(2)}) collective-permute-start(bf16[224,1920]{1,0:T(8,128)(2,1)S(1)} %constant_dynamic-update-slice_fusion.refs_0_.refs_16_), channel_id=1, source_target_pairs={{32,0},{36,4},{40,8},{44,12},{48,16},{52,20},{56,24},{60,28},{0,32... | collective-permute-start | bytes 2580488 | tf_op jit(solution)/shard_map/ppermute | solution.py:35
  26.5 1.6 collective-permute-start.3
  28.1 1.2 constant_dynamic-slice_fusion.3
  31.6 1.8 broadcast_select_fusion
  34.4 4.9 %fusion.16 = bf16[2,2,384,896]{3,2,1,0:T(8,128)(2,1)S(1)} fusion(bf16[2,2,96,896]{3,2,1,0:T(8,128)(2,1)S(1)} %get-tuple-element.164, bf16[2,2,96,896]{3,2,1,0:T(8,128)(2,1)S(1)} %get-tuple-element.165, bf16[2,2,96,896]{3,2,1,0:T(8,128)(2,1)S(1)} %get-tuple-element.166, bf16[2,2,96,896]{3,2,1,0:T(8,128)(2,1)S(1)} %get-tuple-element.163, s32[896]{0:T(1024)S(1)} %fusion.61), kind=kOutput, calls=%fused_computation.17 | convolution fusion | flops 2479439872 | bytes 5508608 | tf_op jit(solution)/shard_map/dot_general | solution.py:400
  39.3 1.3 slice_bitcast_fusion.1
  40.7 8.6 %collective-permute-done.4.refs_2_.refs_18_ = bf16[224,1920]{1,0:T(8,128)(2,1)S(1)} collective-permute-done((bf16[224,1920]{1,0:T(8,128)(2,1)S(1)}, bf16[224,1920]{1,0:T(8,128)(2,1)S(1)}, u32[]{:S(2)}, u32[]{:S(2)}) %collective-permute-start.4) | collective-permute-done | bytes 860192 | tf_op jit(solution)/shard_map/ppermute | solution.py:35
  49.3 6.0 %first.1 = (bf16[896,384]{1,0:T(8,128)(2,1)S(1)}, bf16[384,640]{1,0:T(8,128)(2,1)S(1)}, f32[384,640]{1,0:T(8,128)S(1)}, f32[384,640]{1,0:T(8,128)S(1)}, bf16[96,...) custom-call(bf16[384,896]{1,0:T(8,128)(2,1)S(1)} %get-tuple-element., ...), custom_call_target="tpu_custom_call" | custom-call | flops 2202009600 | bytes 8650752 | tf_op jit(solution)/shard_map/first/pallas_call | solution.py:68
  57.0 1.5 collective-permute-start.6
  58.6 3.4 %collective-permute-start.7 = (bf16[96,896]{1,0:T(8,128)(2,1)S(1)}, bf16[96,896]{1,0:T(8,128)(2,1)S(1)}, u32[]{:S(2)}, u32[]{:S(2)}) collective-permute-start(bf16[96,896]{1,0:T(8,128)(2,1)S(1)} %get-tuple-element.93), channel_id=1, source_target_pairs={{2,0},{3,1},{0,2},{1,3},{6,4},{7,5},{4,6},{5,7},{10,8},{11,9},{8,1... | collective-permute-start | bytes 516104 | tf_op jit(solution)/shard_map/ppermute | solution.py:40
  62.0 1.5 collective-permute-start.8
  63.5 3.2 %early.2 = (bf16[896,384]{1,0:T(8,128)(2,1)S(1)}, bf16[896,384]{1,0:T(8,128)(2,1)S(1)}, bf16[384,640]{1,0:T(8,128)(2,1)S(1)}, bf16[384,1280]{1,0:T(8,128)(2,1)S(1)}) custom-call(bf16[384,896]{1,0:T(8,128)(2,1)S(1)} %get-tuple-element.86.x, bf16[384,896]{1,0:T(8,128)(2,1)S(1)} %get-tuple-element.168.d, ...), custom_call_target="tpu_custom_call" | custom-call | flops 2202009600 | bytes 7667712 | tf_op jit(solution)/shard_map/early/pallas_call | solution.py:68
  66.7 2.1 collective-permute-done.7.refs_2_
  70.1 1.5 collective-permute-start.11
  73.1 1.8 collective-permute-done.11.refs_6_
  74.9 1.7 collective-permute-done.10.refs_5_
  77.7 4.3 %collective-permute-start.14 = (bf16[96,896]{1,0:T(8,128)(2,1)}, bf16[96,896]{1,0:T(8,128)(2,1)}, u32[]{:S(2)}, u32[]{:S(2)}) collective-permute-start(bf16[96,896]{1,0:T(8,128)(2,1)} %get-tuple-element.100), channel_id=1, source_target_pairs={{67,0},{64,1},{65,2},{66,3},{0,64},{1,65},{2,66},{3,67},{71,4},{68... | collective-permute-start | bytes 516104 | tf_op jit(solution)/shard_map/ppermute | solution.py:46
  82.0 2.6 %collective-permute-start.16 = (bf16[96,896]{1,0:T(8,128)(2,1)}, bf16[96,896]{1,0:T(8,128)(2,1)}, u32[]{:S(2)}, u32[]{:S(2)}) collective-permute-start(bf16[96,896]{1,0:T(8,128)(2,1)} %get-tuple-element.102), channel_id=1, source_target_pairs={{65,0},{66,1},{67,2},{64,3},{0,64},{1,65},{2,66},{3,67},{69,4},{70... | collective-permute-start | bytes 516104 | tf_op jit(solution)/shard_map/ppermute | solution.py:46
  84.7 2.0 copy-done
  86.7 4.0 %order.2.weights.ins.refs_0_ = bf16[896,1280]{1,0:T(8,128)(2,1)S(1)} custom-call(bf16[896,896]{1,0:T(8,128)(2,1)S(1)} %fusion.8.mover, bf16[896,1920]{1,0:T(8,128)(2,1)S(1)} %copy-done), custom_call_target="tpu_custom_call" | custom-call | flops 2055208960 | bytes 7340032 | tf_op jit(solution)/shard_map/order/pallas_call | solution.py:68
  90.7 1.4 mix.4.d
  93.4 2.3 %collective-permute-start.18 = (bf16[96,896]{1,0:T(8,128)(2,1)S(1)}, bf16[96,896]{1,0:T(8,128)(2,1)S(1)}, u32[]{:S(2)}, u32[]{:S(2)}) collective-permute-start(bf16[96,896]{1,0:T(8,128)(2,1)S(1)} %mix.4.d), channel_id=1, source_target_pairs={{1,64},{2,65},{3,66},{0,67},{64,0},{65,1},{66,2},{67,3},{5,68},{6,... | collective-permute-start | bytes 516104 | tf_op jit(solution)/shard_map/ppermute | solution.py:46
  95.9 1.5 gate.1
  97.5 1.8 order.3.down.refs_1_.refs_16_
  99.5 3.4 %collective-permute-start.21 = (bf16[96,896]{1,0:T(8,128)(2,1)S(1)}, bf16[96,896]{1,0:T(8,128)(2,1)S(1)}, u32[]{:S(2)}, u32[]{:S(2)}) collective-permute-start(bf16[96,896]{1,0:T(8,128)(2,1)S(1)} %get-tuple-element.107), channel_id=1, source_target_pairs={{64,0},{65,1},{66,2},{67,3},{0,64},{1,65},{2,66},{3,67},{68,4},{69... | collective-permute-start | bytes 516104 | tf_op jit(solution)/shard_map/ppermute | solution.py:46
  103.4 1.4 collective-permute-start.24
  105.0 4.4 %terms.2 = (bf16[224,1920]{1,0:T(8,128)(2,1)S(1)}, bf16[224,1920]{1,0:T(8,128)(2,1)S(1)}, bf16[224,1920]{1,0:T(8,128)(2,1)S(1)}, bf16[224,1920]{1,0:T(8,128)(2,1)S(1)}) custom-call(s32[1]{0:T(128)} %bitcast.4.use_first, bf16[96,896]{1,0:T(8,128)(2,1)S(1)} %get-tuple-element.91.d.refs_0_, bf16[96,896]{1,0:T(8,128)(2,1)S(1)} %copy-done.27, ...), custom_call_target="tpu_custom_call" | custom-call | flops 3082813440 | bytes 14254084 | tf_op jit(solution)/shard_map/terms/pallas_call | solution.py:68
  109.4 1.8 collective-permute-done.23.refs_2_
  111.6 1.6 collective-permute-start.28
  113.2 1.7 collective-permute-start.29
  115.1 3.4 %collective-permute-start.26 = (bf16[96,896]{1,0:T(8,128)(2,1)S(1)}, bf16[96,896]{1,0:T(8,128)(2,1)S(1)}, u32[]{:S(2)}, u32[]{:S(2)}) collective-permute-start(bf16[96,896]{1,0:T(8,128)(2,1)S(1)} %mix.5.refs_4_), channel_id=1, source_target_pairs={{2,0},{3,1},{0,2},{1,3},{6,4},{7,5},{4,6},{5,7},{10,8},{11,9},{8,1... | collective-permute-start | bytes 516104 | tf_op jit(solution)/shard_map/ppermute | solution.py:40
  118.9 2.2 early.3
  121.1 4.6 %collective-permute-done.28.refs_1_ = bf16[224,1920]{1,0:T(8,128)(2,1)S(1)} collective-permute-done((bf16[224,1920]{1,0:T(8,128)(2,1)S(1)}, bf16[224,1920]{1,0:T(8,128)(2,1)S(1)}, u32[]{:S(2)}, u32[]{:S(2)}) %collective-permute-start.28) | collective-permute-done | bytes 860192 | tf_op jit(solution)/shard_map/ppermute | solution.py:35
  126.1 3.8 %terms.3 = (bf16[224,1920]{1,0:T(8,128)(2,1)S(1)}, bf16[224,1920]{1,0:T(8,128)(2,1)S(1)}, bf16[224,1920]{1,0:T(8,128)(2,1)S(1)}, bf16[224,1920]{1,0:T(8,128)(2,1)S(1)}) custom-call(s32[1]{0:T(128)S(6)} %sub.36.active.use_first, bf16[96,896]{1,0:T(8,128)(2,1)S(1)} %collective-permute-done.17.refs_0_, bf16[96,896]{1,0:T(8,128)(2,1)S(1)} %collective-permute-done.18.refs_1_, ...), custom_call_target="tpu_custom_call" | custom-call | flops 3082813440 | bytes 11960324 | tf_op jit(solution)/shard_map/terms/pallas_call | solution.py:68
  129.9 3.0 %collective-permute-start.36 = (bf16[224,1920]{1,0:T(8,128)(2,1)S(1)}, bf16[224,1920]{1,0:T(8,128)(2,1)S(1)}, u32[]{:S(2)}, u32[]{:S(2)}) collective-permute-start(bf16[224,1920]{1,0:T(8,128)(2,1)S(1)} %get-tuple-element.145), channel_id=1, source_target_pairs={{32,0},{36,4},{40,8},{44,12},{48,16},{52,20},{56,24},{60,28},{0,32... | collective-permute-start | bytes 2580488 | tf_op jit(solution)/shard_map/ppermute | solution.py:35
  133.7 1.9 collective-permute-start.31
  136.4 7.9 %collective-permute-done.36.refs_2_ = bf16[224,1920]{1,0:T(8,128)(2,1)S(1)} collective-permute-done((bf16[224,1920]{1,0:T(8,128)(2,1)S(1)}, bf16[224,1920]{1,0:T(8,128)(2,1)S(1)}, u32[]{:S(2)}, u32[]{:S(2)}) %collective-permute-start.36) | collective-permute-done | bytes 860192 | tf_op jit(solution)/shard_map/ppermute | solution.py:35
  145.9 2.2 %collective-permute-start.38 = (bf16[56,1920]{1,0:T(8,128)(2,1)S(1)}, bf16[56,1920]{1,0:T(8,128)(2,1)S(1)}, u32[]{:S(2)}, u32[]{:S(2)}) collective-permute-start(bf16[56,1920]{1,0:T(8,128)(2,1)S(1)} %get-tuple-element.148), channel_id=1, source_target_pairs={{8,0},{12,4},{0,8},{4,12},{24,16},{28,20},{16,24},{20,28},{40,32},... | collective-permute-start | bytes 645128 | tf_op jit(solution)/shard_map/ppermute | solution.py:35
  148.0 10.0 %collective-permute-done.30.refs_1_ = bf16[224,1920]{1,0:T(8,128)(2,1)S(1)} collective-permute-done((bf16[224,1920]{1,0:T(8,128)(2,1)S(1)}, bf16[224,1920]{1,0:T(8,128)(2,1)S(1)}, u32[]{:S(2)}, u32[]{:S(2)}) %collective-permute-start.30) | collective-permute-done | bytes 860192 | tf_op jit(solution)/shard_map/ppermute | solution.py:35
  158.1 1.7 collective-permute-start.39
  159.8 7.5 %collective-permute-done.31.refs_2_ = bf16[224,1920]{1,0:T(8,128)(2,1)S(1)} collective-permute-done((bf16[224,1920]{1,0:T(8,128)(2,1)S(1)}, bf16[224,1920]{1,0:T(8,128)(2,1)S(1)}, u32[]{:S(2)}, u32[]{:S(2)}) %collective-permute-start.31) | collective-permute-done | bytes 860192 | tf_op jit(solution)/shard_map/ppermute | solution.py:35
  169.0 2.6 %collective-permute-start.34 = (bf16[56,1920]{1,0:T(8,128)(2,1)S(1)}, bf16[56,1920]{1,0:T(8,128)(2,1)S(1)}, u32[]{:S(2)}, u32[]{:S(2)}) collective-permute-start(bf16[56,1920]{1,0:T(8,128)(2,1)S(1)} %get-tuple-element.141), channel_id=1, source_target_pairs={{8,0},{12,4},{0,8},{4,12},{24,16},{28,20},{16,24},{20,28},{40,32},... | collective-permute-start | bytes 645128 | tf_op jit(solution)/shard_map/ppermute | solution.py:35
  171.6 1.2 collective-permute-start.35
  173.1 2.0 collective-permute-done.33.refs_1_
  175.1 2.6 %collective-permute-done.34.refs_2_ = bf16[56,1920]{1,0:T(8,128)(2,1)S(1)} collective-permute-done((bf16[56,1920]{1,0:T(8,128)(2,1)S(1)}, bf16[56,1920]{1,0:T(8,128)(2,1)S(1)}, u32[]{:S(2)}, u32[]{:S(2)}) %collective-permute-start.34) | collective-permute-done | bytes 215072 | tf_op jit(solution)/shard_map/ppermute | solution.py:35
  178.6 1.2 collective-permute-done.40
  179.8 1.5 collective-permute-start.43
  181.3 2.6 %collective-permute-start.42 = (f32[8,128]{1,0:T(8,128)S(1)}, f32[8,128]{1,0:T(8,128)S(1)}, u32[]{:S(2)}, u32[]{:S(2)}) collective-permute-start(f32[8,128]{1,0:T(8,128)S(1)} %add.249), channel_id=1, source_target_pairs={{8,0},{12,4},{0,8},{4,12},{24,16},{28,20},{16,24},{20,28},{40,32},... | collective-permute-start | bytes 12296 | tf_op jit(solution)/shard_map/ppermute | solution.py:35
  184.6 1.8 collective-permute-done.42
  186.4 1.1 collective-permute-done.41
  187.5 1.2 collective-permute-start.46
  188.7 2.9 %collective-permute-start.45 = (f32[8,128]{1,0:T(8,128)S(1)}, f32[8,128]{1,0:T(8,128)S(1)}, u32[]{:S(2)}, u32[]{:S(2)}) collective-permute-start(f32[8,128]{1,0:T(8,128)S(1)} %add_add_fusion.2), channel_id=1, source_target_pairs={{32,0},{36,4},{40,8},{44,12},{48,16},{52,20},{56,24},{60,28},{0,32... | collective-permute-start | bytes 12296 | tf_op jit(solution)/shard_map/ppermute | solution.py:35
  191.6 1.4 collective-permute-start.44
  193.9 1.6 collective-permute-done.44
  195.6 3.4 %collective-permute-start.48 = (f32[8,128]{1,0:T(8,128)S(1)}, f32[8,128]{1,0:T(8,128)S(1)}, u32[]{:S(2)}, u32[]{:S(2)}) collective-permute-start(f32[8,128]{1,0:T(8,128)S(1)} %add_add_fusion.1), channel_id=1, source_target_pairs={{2,0},{3,1},{0,2},{1,3},{6,4},{7,5},{4,6},{5,7},{10,8},{11,9},{8,1... | collective-permute-start | bytes 12296 | tf_op jit(solution)/shard_map/ppermute | solution.py:40
  200.7 1.9 collective-permute-done.47
  207.0 1.3 copy.25
  (189 shorter events, 29.2 us)
Async XLA Ops:
  7.2 77.5 %all-gather.2.cloned.1.call-start = ((), (), s32[]{:S(2)}) async-start(), calls=%async_computation | async-start | bytes 3655680 | tf_op jit(solution)/shard_map/all_gather | solution.py:376
  9.5 19.9 %copy-start.42 = (bf16[1,2,384,896]{3,2,1,0:T(8,128)(2,1)S(1)}, bf16[1,2,384,896]{3,2,1,0:T(8,128)(2,1)}, u32[]{:S(2)}) copy-start(bf16[1,2,384,896]{3,2,1,0:T(8,128)(2,1)} %param.8) | copy-start | bytes 4128772
  9.5 12.3 %collective-permute-start.2 = (bf16[56,1920]{1,0:T(8,128)(2,1)S(1)}, bf16[56,1920]{1,0:T(8,128)(2,1)S(1)}, u32[]{:S(2)}, u32[]{:S(2)}) collective-permute-start(bf16[56,1920]{1,0:T(8,128)(2,1)S(1)} %bitcast.109), channel_id=1, source_target_pairs={{12,0},{0,4},{4,8},{8,12},{28,16},{16,20},{20,24},{24,28},{44,32},... | collective-permute-start | bytes 645128 | tf_op jit(solution)/shard_map/ppermute | solution.py:35
  11.1 9.7 %collective-permute-start.1 = (bf16[56,1920]{1,0:T(8,128)(2,1)S(1)}, bf16[56,1920]{1,0:T(8,128)(2,1)}, u32[]{:S(2)}, u32[]{:S(2)}) collective-permute-start(bf16[56,1920]{1,0:T(8,128)(2,1)S(1)} %bitcast.110), channel_id=1, source_target_pairs={{8,0},{12,4},{0,8},{4,12},{24,16},{28,20},{16,24},{20,28},{40,32},... | collective-permute-start | bytes 645128 | tf_op jit(solution)/shard_map/ppermute | solution.py:35
  13.9 6.0 %collective-permute-start = (bf16[56,1920]{1,0:T(8,128)(2,1)S(1)}, bf16[56,1920]{1,0:T(8,128)(2,1)}, u32[]{:S(2)}, u32[]{:S(2)}) collective-permute-start(bf16[56,1920]{1,0:T(8,128)(2,1)S(1)} %bitcast.111), channel_id=1, source_target_pairs={{4,0},{8,4},{12,8},{0,12},{20,16},{24,20},{28,24},{16,28},{36,32},... | collective-permute-start | bytes 645128 | tf_op jit(solution)/shard_map/ppermute | solution.py:35
  17.9 11.6 %copy-start.41 = (bf16[1,2,2,384,896]{4,3,2,1,0:T(8,128)(2,1)S(1)}, bf16[1,2,2,384,896]{4,3,2,1,0:T(8,128)(2,1)}, u32[]{:S(2)}) copy-start(bf16[1,2,2,384,896]{4,3,2,1,0:T(8,128)(2,1)} %param.7) | copy-start | bytes 8257540
  21.9 54.7 %copy-start.3 = (bf16[224,1920]{1,0:T(8,128)(2,1)}, bf16[224,1920]{1,0:T(8,128)(2,1)S(1)}, u32[]{:S(2)}) copy-start(bf16[224,1920]{1,0:T(8,128)(2,1)S(1)} %constant_dynamic-update-slice_fusion.refs_0_.refs_16_) | copy-start | bytes 2580484
  21.9 18.8 %collective-permute-start.5 = (bf16[224,1920]{1,0:T(8,128)(2,1)S(1)}, bf16[224,1920]{1,0:T(8,128)(2,1)S(1)}, u32[]{:S(2)}, u32[]{:S(2)}) collective-permute-start(bf16[224,1920]{1,0:T(8,128)(2,1)S(1)} %constant_dynamic-update-slice_fusion.refs_0_.refs_16_), channel_id=1, source_target_pairs={{48,0},{52,4},{56,8},{60,12},{0,16},{4,20},{8,24},{12,28},{16,32},... | collective-permute-start | bytes 2580488 | tf_op jit(solution)/shard_map/ppermute | solution.py:35
  23.6 25.7 %collective-permute-start.4 = (bf16[224,1920]{1,0:T(8,128)(2,1)S(1)}, bf16[224,1920]{1,0:T(8,128)(2,1)S(1)}, u32[]{:S(2)}, u32[]{:S(2)}) collective-permute-start(bf16[224,1920]{1,0:T(8,128)(2,1)S(1)} %constant_dynamic-update-slice_fusion.refs_0_.refs_16_), channel_id=1, source_target_pairs={{32,0},{36,4},{40,8},{44,12},{48,16},{52,20},{56,24},{60,28},{0,32... | collective-permute-start | bytes 2580488 | tf_op jit(solution)/shard_map/ppermute | solution.py:35
  26.5 22.8 %collective-permute-start.3 = (bf16[224,1920]{1,0:T(8,128)(2,1)S(1)}, bf16[224,1920]{1,0:T(8,128)(2,1)S(1)}, u32[]{:S(2)}, u32[]{:S(2)}) collective-permute-start(bf16[224,1920]{1,0:T(8,128)(2,1)S(1)} %constant_dynamic-update-slice_fusion.refs_0_.refs_16_), channel_id=1, source_target_pairs={{16,0},{20,4},{24,8},{28,12},{32,16},{36,20},{40,24},{44,28},{48,3... | collective-permute-start | bytes 2580488 | tf_op jit(solution)/shard_map/ppermute | solution.py:35
  40.7 35.9 %copy-start.9 = (bf16[224,1920]{1,0:T(8,128)(2,1)}, bf16[224,1920]{1,0:T(8,128)(2,1)S(1)}, u32[]{:S(2)}) copy-start(bf16[224,1920]{1,0:T(8,128)(2,1)S(1)} %collective-permute-done.5.refs_3_.refs_19_) | copy-start | bytes 2580484
  49.3 27.3 %copy-start.11 = (bf16[224,1920]{1,0:T(8,128)(2,1)}, bf16[224,1920]{1,0:T(8,128)(2,1)S(1)}, u32[]{:S(2)}) copy-start(bf16[224,1920]{1,0:T(8,128)(2,1)S(1)} %collective-permute-done.4.refs_2_.refs_18_) | copy-start | bytes 2580484
  49.3 27.3 %copy-start.13 = (bf16[224,1920]{1,0:T(8,128)(2,1)}, bf16[224,1920]{1,0:T(8,128)(2,1)S(1)}, u32[]{:S(2)}) copy-start(bf16[224,1920]{1,0:T(8,128)(2,1)S(1)} %collective-permute-done.3.refs_1_.refs_17_) | copy-start | bytes 2580484
  57.0 19.6 %copy-start.5 = (f32[384,640]{1,0:T(8,128)}, f32[384,640]{1,0:T(8,128)S(1)}, u32[]{:S(2)}) copy-start(f32[384,640]{1,0:T(8,128)S(1)} %get-tuple-element.95.slope.refs_14_) | copy-start | bytes 2949124
  57.0 19.6 %copy-start.7 = (f32[384,640]{1,0:T(8,128)}, f32[384,640]{1,0:T(8,128)S(1)}, u32[]{:S(2)}) copy-start(f32[384,640]{1,0:T(8,128)S(1)} %get-tuple-element.96.activated.refs_15_) | copy-start | bytes 2949124
  57.0 9.7 %collective-permute-start.6 = (bf16[96,896]{1,0:T(8,128)(2,1)S(1)}, bf16[96,896]{1,0:T(8,128)(2,1)S(1)}, u32[]{:S(2)}, u32[]{:S(2)}) collective-permute-start(bf16[96,896]{1,0:T(8,128)(2,1)S(1)} %get-tuple-element.92), channel_id=1, source_target_pairs={{3,0},{0,1},{1,2},{2,3},{7,4},{4,5},{5,6},{6,7},{11,8},{8,9},{9,10... | collective-permute-start | bytes 516104 | tf_op jit(solution)/shard_map/ppermute | solution.py:40
  58.6 10.3 %collective-permute-start.7 = (bf16[96,896]{1,0:T(8,128)(2,1)S(1)}, bf16[96,896]{1,0:T(8,128)(2,1)S(1)}, u32[]{:S(2)}, u32[]{:S(2)}) collective-permute-start(bf16[96,896]{1,0:T(8,128)(2,1)S(1)} %get-tuple-element.93), channel_id=1, source_target_pairs={{2,0},{3,1},{0,2},{1,3},{6,4},{7,5},{4,6},{5,7},{10,8},{11,9},{8,1... | collective-permute-start | bytes 516104 | tf_op jit(solution)/shard_map/ppermute | solution.py:40
  62.0 6.8 %collective-permute-start.8 = (bf16[96,896]{1,0:T(8,128)(2,1)S(1)}, bf16[96,896]{1,0:T(8,128)(2,1)S(1)}, u32[]{:S(2)}, u32[]{:S(2)}) collective-permute-start(bf16[96,896]{1,0:T(8,128)(2,1)S(1)} %get-tuple-element.94), channel_id=1, source_target_pairs={{1,0},{2,1},{3,2},{0,3},{5,4},{6,5},{7,6},{4,7},{9,8},{10,9},{11,1... | collective-permute-start | bytes 516104 | tf_op jit(solution)/shard_map/ppermute | solution.py:40
  69.2 3.8 %collective-permute-start.12 = (bf16[96,896]{1,0:T(8,128)(2,1)S(1)}, bf16[96,896]{1,0:T(8,128)(2,1)S(1)}, u32[]{:S(2)}, u32[]{:S(2)}) collective-permute-start(bf16[96,896]{1,0:T(8,128)(2,1)S(1)} %mix.3.d), channel_id=1, source_target_pairs={{3,64},{0,65},{1,66},{2,67},{64,0},{65,1},{66,2},{67,3},{7,68},{4,... | collective-permute-start | bytes 516104 | tf_op jit(solution)/shard_map/ppermute | solution.py:46
  70.1 4.8 %collective-permute-start.11 = (bf16[96,896]{1,0:T(8,128)(2,1)S(1)}, bf16[96,896]{1,0:T(8,128)(2,1)S(1)}, u32[]{:S(2)}, u32[]{:S(2)}) collective-permute-start(bf16[96,896]{1,0:T(8,128)(2,1)S(1)} %mix.3.d), channel_id=1, source_target_pairs={{2,64},{3,65},{0,66},{1,67},{64,0},{65,1},{66,2},{67,3},{6,68},{7,... | collective-permute-start | bytes 516104 | tf_op jit(solution)/shard_map/ppermute | solution.py:46
  71.7 4.9 %collective-permute-start.10 = (bf16[96,896]{1,0:T(8,128)(2,1)S(1)}, bf16[96,896]{1,0:T(8,128)(2,1)S(1)}, u32[]{:S(2)}, u32[]{:S(2)}) collective-permute-start(bf16[96,896]{1,0:T(8,128)(2,1)S(1)} %mix.3.d), channel_id=1, source_target_pairs={{1,64},{2,65},{3,66},{0,67},{64,0},{65,1},{66,2},{67,3},{5,68},{6,... | collective-permute-start | bytes 516104 | tf_op jit(solution)/shard_map/ppermute | solution.py:46
  71.8 4.8 %collective-permute-start.9 = (bf16[96,896]{1,0:T(8,128)(2,1)S(1)}, bf16[96,896]{1,0:T(8,128)(2,1)S(1)}, u32[]{:S(2)}, u32[]{:S(2)}) collective-permute-start(bf16[96,896]{1,0:T(8,128)(2,1)S(1)} %mix.3.d), channel_id=1, source_target_pairs={{0,64},{1,65},{2,66},{3,67},{64,0},{65,1},{66,2},{67,3},{4,68},{5,... | collective-permute-start | bytes 516104 | tf_op jit(solution)/shard_map/ppermute | solution.py:46
  77.7 13.0 %collective-permute-start.14 = (bf16[96,896]{1,0:T(8,128)(2,1)}, bf16[96,896]{1,0:T(8,128)(2,1)}, u32[]{:S(2)}, u32[]{:S(2)}) collective-permute-start(bf16[96,896]{1,0:T(8,128)(2,1)} %get-tuple-element.100), channel_id=1, source_target_pairs={{67,0},{64,1},{65,2},{66,3},{0,64},{1,65},{2,66},{3,67},{71,4},{68... | collective-permute-start | bytes 516104 | tf_op jit(solution)/shard_map/ppermute | solution.py:46
  82.0 8.8 %collective-permute-start.15 = (bf16[96,896]{1,0:T(8,128)(2,1)}, bf16[96,896]{1,0:T(8,128)(2,1)}, u32[]{:S(2)}, u32[]{:S(2)}) collective-permute-start(bf16[96,896]{1,0:T(8,128)(2,1)} %get-tuple-element.101), channel_id=1, source_target_pairs={{66,0},{67,1},{64,2},{65,3},{0,64},{1,65},{2,66},{3,67},{70,4},{71... | collective-permute-start | bytes 516104 | tf_op jit(solution)/shard_map/ppermute | solution.py:46
  82.0 8.7 %collective-permute-start.16 = (bf16[96,896]{1,0:T(8,128)(2,1)}, bf16[96,896]{1,0:T(8,128)(2,1)}, u32[]{:S(2)}, u32[]{:S(2)}) collective-permute-start(bf16[96,896]{1,0:T(8,128)(2,1)} %get-tuple-element.102), channel_id=1, source_target_pairs={{65,0},{66,1},{67,2},{64,3},{0,64},{1,65},{2,66},{3,67},{69,4},{70... | collective-permute-start | bytes 516104 | tf_op jit(solution)/shard_map/ppermute | solution.py:46
  84.7 6.1 %collective-permute-start.13 = (bf16[96,896]{1,0:T(8,128)(2,1)}, bf16[96,896]{1,0:T(8,128)(2,1)}, u32[]{:S(2)}, u32[]{:S(2)}) collective-permute-start(bf16[96,896]{1,0:T(8,128)(2,1)} %get-tuple-element.97), channel_id=1, source_target_pairs={{64,0},{65,1},{66,2},{67,3},{0,64},{1,65},{2,66},{3,67},{68,4},{69... | collective-permute-start | bytes 516104 | tf_op jit(solution)/shard_map/ppermute | solution.py:46
  92.2 7.1 %collective-permute-start.20 = (bf16[96,896]{1,0:T(8,128)(2,1)S(1)}, bf16[96,896]{1,0:T(8,128)(2,1)S(1)}, u32[]{:S(2)}, u32[]{:S(2)}) collective-permute-start(bf16[96,896]{1,0:T(8,128)(2,1)S(1)} %mix.4.d), channel_id=1, source_target_pairs={{3,64},{0,65},{1,66},{2,67},{64,0},{65,1},{66,2},{67,3},{7,68},{4,... | collective-permute-start | bytes 516104 | tf_op jit(solution)/shard_map/ppermute | solution.py:46
  93.0 6.3 %collective-permute-start.19 = (bf16[96,896]{1,0:T(8,128)(2,1)S(1)}, bf16[96,896]{1,0:T(8,128)(2,1)S(1)}, u32[]{:S(2)}, u32[]{:S(2)}) collective-permute-start(bf16[96,896]{1,0:T(8,128)(2,1)S(1)} %mix.4.d), channel_id=1, source_target_pairs={{2,64},{3,65},{0,66},{1,67},{64,0},{65,1},{66,2},{67,3},{6,68},{7,... | collective-permute-start | bytes 516104 | tf_op jit(solution)/shard_map/ppermute | solution.py:46
  93.4 5.9 %collective-permute-start.18 = (bf16[96,896]{1,0:T(8,128)(2,1)S(1)}, bf16[96,896]{1,0:T(8,128)(2,1)S(1)}, u32[]{:S(2)}, u32[]{:S(2)}) collective-permute-start(bf16[96,896]{1,0:T(8,128)(2,1)S(1)} %mix.4.d), channel_id=1, source_target_pairs={{1,64},{2,65},{3,66},{0,67},{64,0},{65,1},{66,2},{67,3},{5,68},{6,... | collective-permute-start | bytes 516104 | tf_op jit(solution)/shard_map/ppermute | solution.py:46
  95.7 3.6 %collective-permute-start.17 = (bf16[96,896]{1,0:T(8,128)(2,1)S(1)}, bf16[96,896]{1,0:T(8,128)(2,1)S(1)}, u32[]{:S(2)}, u32[]{:S(2)}) collective-permute-start(bf16[96,896]{1,0:T(8,128)(2,1)S(1)} %mix.4.d), channel_id=1, source_target_pairs={{0,64},{1,65},{2,66},{3,67},{64,0},{65,1},{66,2},{67,3},{4,68},{5,... | collective-permute-start | bytes 516104 | tf_op jit(solution)/shard_map/ppermute | solution.py:46
  99.5 11.7 %collective-permute-start.21 = (bf16[96,896]{1,0:T(8,128)(2,1)S(1)}, bf16[96,896]{1,0:T(8,128)(2,1)S(1)}, u32[]{:S(2)}, u32[]{:S(2)}) collective-permute-start(bf16[96,896]{1,0:T(8,128)(2,1)S(1)} %get-tuple-element.107), channel_id=1, source_target_pairs={{64,0},{65,1},{66,2},{67,3},{0,64},{1,65},{2,66},{3,67},{68,4},{69... | collective-permute-start | bytes 516104 | tf_op jit(solution)/shard_map/ppermute | solution.py:46
  103.0 6.4 %collective-permute-start.22 = (bf16[96,896]{1,0:T(8,128)(2,1)S(1)}, bf16[96,896]{1,0:T(8,128)(2,1)S(1)}, u32[]{:S(2)}, u32[]{:S(2)}) collective-permute-start(bf16[96,896]{1,0:T(8,128)(2,1)S(1)} %get-tuple-element.116), channel_id=1, source_target_pairs={{67,0},{64,1},{65,2},{66,3},{0,64},{1,65},{2,66},{3,67},{71,4},{68... | collective-permute-start | bytes 516104 | tf_op jit(solution)/shard_map/ppermute | solution.py:46
  103.0 8.2 %collective-permute-start.23 = (bf16[96,896]{1,0:T(8,128)(2,1)S(1)}, bf16[96,896]{1,0:T(8,128)(2,1)S(1)}, u32[]{:S(2)}, u32[]{:S(2)}) collective-permute-start(bf16[96,896]{1,0:T(8,128)(2,1)S(1)} %get-tuple-element.117), channel_id=1, source_target_pairs={{66,0},{67,1},{64,2},{65,3},{0,64},{1,65},{2,66},{3,67},{70,4},{71... | collective-permute-start | bytes 516104 | tf_op jit(solution)/shard_map/ppermute | solution.py:46
  103.4 7.8 %collective-permute-start.24 = (bf16[96,896]{1,0:T(8,128)(2,1)S(1)}, bf16[96,896]{1,0:T(8,128)(2,1)S(1)}, u32[]{:S(2)}, u32[]{:S(2)}) collective-permute-start(bf16[96,896]{1,0:T(8,128)(2,1)S(1)} %get-tuple-element.118), channel_id=1, source_target_pairs={{65,0},{66,1},{67,2},{64,3},{0,64},{1,65},{2,66},{3,67},{69,4},{70... | collective-permute-start | bytes 516104 | tf_op jit(solution)/shard_map/ppermute | solution.py:46
  104.9 14.0 %copy-start.15 = (bf16[384,896]{1,0:T(8,128)(2,1)S(1)}, bf16[384,896]{1,0:T(8,128)(2,1)}, u32[]{:S(2)}) copy-start(bf16[384,896]{1,0:T(8,128)(2,1)} %get-tuple-element.167.d) | copy-start | bytes 2064388
  104.9 14.0 %copy-start.16 = (bf16[384,896]{1,0:T(8,128)(2,1)S(1)}, bf16[384,896]{1,0:T(8,128)(2,1)}, u32[]{:S(2)}) copy-start(bf16[384,896]{1,0:T(8,128)(2,1)} %get-tuple-element.119.x) | copy-start | bytes 2064388
  111.6 14.1 %collective-permute-start.28 = (bf16[224,1920]{1,0:T(8,128)(2,1)S(1)}, bf16[224,1920]{1,0:T(8,128)(2,1)S(1)}, u32[]{:S(2)}, u32[]{:S(2)}) collective-permute-start(bf16[224,1920]{1,0:T(8,128)(2,1)S(1)} %get-tuple-element.127), channel_id=1, source_target_pairs={{48,0},{52,4},{56,8},{60,12},{0,16},{4,20},{8,24},{12,28},{16,32},... | collective-permute-start | bytes 2580488 | tf_op jit(solution)/shard_map/ppermute | solution.py:35
  113.2 12.8 %collective-permute-start.29 = (bf16[224,1920]{1,0:T(8,128)(2,1)S(1)}, bf16[224,1920]{1,0:T(8,128)(2,1)S(1)}, u32[]{:S(2)}, u32[]{:S(2)}) collective-permute-start(bf16[224,1920]{1,0:T(8,128)(2,1)S(1)} %get-tuple-element.128), channel_id=1, source_target_pairs={{16,0},{20,4},{24,8},{28,12},{32,16},{36,20},{40,24},{44,28},{48,3... | collective-permute-start | bytes 2580488 | tf_op jit(solution)/shard_map/ppermute | solution.py:35
  114.9 11.1 %collective-permute-start.27 = (bf16[96,896]{1,0:T(8,128)(2,1)S(1)}, bf16[96,896]{1,0:T(8,128)(2,1)S(1)}, u32[]{:S(2)}, u32[]{:S(2)}) collective-permute-start(bf16[96,896]{1,0:T(8,128)(2,1)S(1)} %mix.5.refs_4_), channel_id=1, source_target_pairs={{3,0},{0,1},{1,2},{2,3},{7,4},{4,5},{5,6},{6,7},{11,8},{8,9},{9,10... | collective-permute-start | bytes 516104 | tf_op jit(solution)/shard_map/ppermute | solution.py:40
  115.1 10.9 %collective-permute-start.26 = (bf16[96,896]{1,0:T(8,128)(2,1)S(1)}, bf16[96,896]{1,0:T(8,128)(2,1)S(1)}, u32[]{:S(2)}, u32[]{:S(2)}) collective-permute-start(bf16[96,896]{1,0:T(8,128)(2,1)S(1)} %mix.5.refs_4_), channel_id=1, source_target_pairs={{2,0},{3,1},{0,2},{1,3},{6,4},{7,5},{4,6},{5,7},{10,8},{11,9},{8,1... | collective-permute-start | bytes 516104 | tf_op jit(solution)/shard_map/ppermute | solution.py:40
  118.5 7.6 %collective-permute-start.25 = (bf16[96,896]{1,0:T(8,128)(2,1)S(1)}, bf16[96,896]{1,0:T(8,128)(2,1)S(1)}, u32[]{:S(2)}, u32[]{:S(2)}) collective-permute-start(bf16[96,896]{1,0:T(8,128)(2,1)S(1)} %mix.5.refs_4_), channel_id=1, source_target_pairs={{1,0},{2,1},{3,2},{0,3},{5,4},{6,5},{7,6},{4,7},{9,8},{10,9},{11,1... | collective-permute-start | bytes 516104 | tf_op jit(solution)/shard_map/ppermute | solution.py:40
  129.9 14.5 %collective-permute-start.36 = (bf16[224,1920]{1,0:T(8,128)(2,1)S(1)}, bf16[224,1920]{1,0:T(8,128)(2,1)S(1)}, u32[]{:S(2)}, u32[]{:S(2)}) collective-permute-start(bf16[224,1920]{1,0:T(8,128)(2,1)S(1)} %get-tuple-element.145), channel_id=1, source_target_pairs={{32,0},{36,4},{40,8},{44,12},{48,16},{52,20},{56,24},{60,28},{0,32... | collective-permute-start | bytes 2580488 | tf_op jit(solution)/shard_map/ppermute | solution.py:35
  132.8 25.2 %collective-permute-start.30 = (bf16[224,1920]{1,0:T(8,128)(2,1)S(1)}, bf16[224,1920]{1,0:T(8,128)(2,1)S(1)}, u32[]{:S(2)}, u32[]{:S(2)}) collective-permute-start(bf16[224,1920]{1,0:T(8,128)(2,1)S(1)} %get-tuple-element.136), channel_id=1, source_target_pairs={{48,0},{52,4},{56,8},{60,12},{0,16},{4,20},{8,24},{12,28},{16,32},... | collective-permute-start | bytes 2580488 | tf_op jit(solution)/shard_map/ppermute | solution.py:35
  133.7 33.6 %collective-permute-start.31 = (bf16[224,1920]{1,0:T(8,128)(2,1)S(1)}, bf16[224,1920]{1,0:T(8,128)(2,1)S(1)}, u32[]{:S(2)}, u32[]{:S(2)}) collective-permute-start(bf16[224,1920]{1,0:T(8,128)(2,1)S(1)} %get-tuple-element.137), channel_id=1, source_target_pairs={{32,0},{36,4},{40,8},{44,12},{48,16},{52,20},{56,24},{60,28},{0,32... | collective-permute-start | bytes 2580488 | tf_op jit(solution)/shard_map/ppermute | solution.py:35
  135.6 32.0 %collective-permute-start.32 = (bf16[224,1920]{1,0:T(8,128)(2,1)S(1)}, bf16[224,1920]{1,0:T(8,128)(2,1)S(1)}, u32[]{:S(2)}, u32[]{:S(2)}) collective-permute-start(bf16[224,1920]{1,0:T(8,128)(2,1)S(1)} %get-tuple-element.138), channel_id=1, source_target_pairs={{16,0},{20,4},{24,8},{28,12},{32,16},{36,20},{40,24},{44,28},{48,3... | collective-permute-start | bytes 2580488 | tf_op jit(solution)/shard_map/ppermute | solution.py:35
  144.8 26.8 %collective-permute-start.37 = (bf16[56,1920]{1,0:T(8,128)(2,1)S(1)}, bf16[56,1920]{1,0:T(8,128)(2,1)S(1)}, u32[]{:S(2)}, u32[]{:S(2)}) collective-permute-start(bf16[56,1920]{1,0:T(8,128)(2,1)S(1)} %get-tuple-element.147), channel_id=1, source_target_pairs={{12,0},{0,4},{4,8},{8,12},{28,16},{16,20},{20,24},{24,28},{44,32},... | collective-permute-start | bytes 645128 | tf_op jit(solution)/shard_map/ppermute | solution.py:35
  145.9 27.0 %collective-permute-start.38 = (bf16[56,1920]{1,0:T(8,128)(2,1)S(1)}, bf16[56,1920]{1,0:T(8,128)(2,1)S(1)}, u32[]{:S(2)}, u32[]{:S(2)}) collective-permute-start(bf16[56,1920]{1,0:T(8,128)(2,1)S(1)} %get-tuple-element.148), channel_id=1, source_target_pairs={{8,0},{12,4},{0,8},{4,12},{24,16},{28,20},{16,24},{20,28},{40,32},... | collective-permute-start | bytes 645128 | tf_op jit(solution)/shard_map/ppermute | solution.py:35
  158.1 14.8 %collective-permute-start.39 = (bf16[56,1920]{1,0:T(8,128)(2,1)S(1)}, bf16[56,1920]{1,0:T(8,128)(2,1)S(1)}, u32[]{:S(2)}, u32[]{:S(2)}) collective-permute-start(bf16[56,1920]{1,0:T(8,128)(2,1)S(1)} %get-tuple-element.149), channel_id=1, source_target_pairs={{4,0},{8,4},{12,8},{0,12},{20,16},{24,20},{28,24},{16,28},{36,32},... | collective-permute-start | bytes 645128 | tf_op jit(solution)/shard_map/ppermute | solution.py:35
  168.0 7.1 %collective-permute-start.33 = (bf16[56,1920]{1,0:T(8,128)(2,1)S(1)}, bf16[56,1920]{1,0:T(8,128)(2,1)S(1)}, u32[]{:S(2)}, u32[]{:S(2)}) collective-permute-start(bf16[56,1920]{1,0:T(8,128)(2,1)S(1)} %get-tuple-element.140), channel_id=1, source_target_pairs={{12,0},{0,4},{4,8},{8,12},{28,16},{16,20},{20,24},{24,28},{44,32},... | collective-permute-start | bytes 645128 | tf_op jit(solution)/shard_map/ppermute | solution.py:35
  169.0 8.7 %collective-permute-start.34 = (bf16[56,1920]{1,0:T(8,128)(2,1)S(1)}, bf16[56,1920]{1,0:T(8,128)(2,1)S(1)}, u32[]{:S(2)}, u32[]{:S(2)}) collective-permute-start(bf16[56,1920]{1,0:T(8,128)(2,1)S(1)} %get-tuple-element.141), channel_id=1, source_target_pairs={{8,0},{12,4},{0,8},{4,12},{24,16},{28,20},{16,24},{20,28},{40,32},... | collective-permute-start | bytes 645128 | tf_op jit(solution)/shard_map/ppermute | solution.py:35
  171.6 6.7 %collective-permute-start.35 = (bf16[56,1920]{1,0:T(8,128)(2,1)S(1)}, bf16[56,1920]{1,0:T(8,128)(2,1)S(1)}, u32[]{:S(2)}, u32[]{:S(2)}) collective-permute-start(bf16[56,1920]{1,0:T(8,128)(2,1)S(1)} %get-tuple-element.142), channel_id=1, source_target_pairs={{4,0},{8,4},{12,8},{0,12},{20,16},{24,20},{28,24},{16,28},{36,32},... | collective-permute-start | bytes 645128 | tf_op jit(solution)/shard_map/ppermute | solution.py:35
  173.1 30.8 %copy-start.40 = (f32[1,56,2,3,640]{4,2,3,1,0:T(2,128)S(1)}, f32[1,56,2,3,640]{4,2,3,1,0:T(2,128)}, u32[]{:S(2)}) copy-start(f32[1,56,2,3,640]{4,2,3,1,0:T(2,128)} %param.11) | copy-start | bytes 2580484
  173.1 30.8 %copy-start.43 = (bf16[1,56,2,3,640]{4,2,3,1,0:T(2,128)(2,1)S(1)}, bf16[1,56,2,3,640]{4,2,3,1,0:T(2,128)(2,1)}, u32[]{:S(2)}) copy-start(bf16[1,56,2,3,640]{4,2,3,1,0:T(2,128)(2,1)} %param.13) | copy-start | bytes 1290244
  173.1 30.8 %copy-start.44 = (bf16[1,56,2,3,640]{4,2,3,1,0:T(2,128)(2,1)S(1)}, bf16[1,56,2,3,640]{4,2,3,1,0:T(2,128)(2,1)}, u32[]{:S(2)}) copy-start(bf16[1,56,2,3,640]{4,2,3,1,0:T(2,128)(2,1)} %param.12) | copy-start | bytes 1290244
  178.6 1.2 collective-permute-start.40
  179.8 4.8 %collective-permute-start.43 = (f32[8,128]{1,0:T(8,128)S(1)}, f32[8,128]{1,0:T(8,128)S(1)}, u32[]{:S(2)}, u32[]{:S(2)}) collective-permute-start(f32[8,128]{1,0:T(8,128)S(1)} %add.249), channel_id=1, source_target_pairs={{12,0},{0,4},{4,8},{8,12},{28,16},{16,20},{20,24},{24,28},{44,32},... | collective-permute-start | bytes 12296 | tf_op jit(solution)/shard_map/ppermute | solution.py:35
  181.3 5.1 %collective-permute-start.42 = (f32[8,128]{1,0:T(8,128)S(1)}, f32[8,128]{1,0:T(8,128)S(1)}, u32[]{:S(2)}, u32[]{:S(2)}) collective-permute-start(f32[8,128]{1,0:T(8,128)S(1)} %add.249), channel_id=1, source_target_pairs={{8,0},{12,4},{0,8},{4,12},{24,16},{28,20},{16,24},{20,28},{40,32},... | collective-permute-start | bytes 12296 | tf_op jit(solution)/shard_map/ppermute | solution.py:35
  183.9 3.6 %collective-permute-start.41 = (f32[8,128]{1,0:T(8,128)S(1)}, f32[8,128]{1,0:T(8,128)S(1)}, u32[]{:S(2)}, u32[]{:S(2)}) collective-permute-start(f32[8,128]{1,0:T(8,128)S(1)} %add.249), channel_id=1, source_target_pairs={{4,0},{8,4},{12,8},{0,12},{20,16},{24,20},{28,24},{16,28},{36,32},... | collective-permute-start | bytes 12296 | tf_op jit(solution)/shard_map/ppermute | solution.py:35
  187.5 5.5 %collective-permute-start.46 = (f32[8,128]{1,0:T(8,128)S(1)}, f32[8,128]{1,0:T(8,128)S(1)}, u32[]{:S(2)}, u32[]{:S(2)}) collective-permute-start(f32[8,128]{1,0:T(8,128)S(1)} %add_add_fusion.2), channel_id=1, source_target_pairs={{48,0},{52,4},{56,8},{60,12},{0,16},{4,20},{8,24},{12,28},{16,32},... | collective-permute-start | bytes 12296 | tf_op jit(solution)/shard_map/ppermute | solution.py:35
  188.7 5.1 %collective-permute-start.45 = (f32[8,128]{1,0:T(8,128)S(1)}, f32[8,128]{1,0:T(8,128)S(1)}, u32[]{:S(2)}, u32[]{:S(2)}) collective-permute-start(f32[8,128]{1,0:T(8,128)S(1)} %add_add_fusion.2), channel_id=1, source_target_pairs={{32,0},{36,4},{40,8},{44,12},{48,16},{52,20},{56,24},{60,28},{0,32... | collective-permute-start | bytes 12296 | tf_op jit(solution)/shard_map/ppermute | solution.py:35
  191.6 3.8 %collective-permute-start.44 = (f32[8,128]{1,0:T(8,128)S(1)}, f32[8,128]{1,0:T(8,128)S(1)}, u32[]{:S(2)}, u32[]{:S(2)}) collective-permute-start(f32[8,128]{1,0:T(8,128)S(1)} %add_add_fusion.2), channel_id=1, source_target_pairs={{16,0},{20,4},{24,8},{28,12},{32,16},{36,20},{40,24},{44,28},{48,3... | collective-permute-start | bytes 12296 | tf_op jit(solution)/shard_map/ppermute | solution.py:35
  195.4 4.8 %collective-permute-start.49 = (f32[8,128]{1,0:T(8,128)S(1)}, f32[8,128]{1,0:T(8,128)S(1)}, u32[]{:S(2)}, u32[]{:S(2)}) collective-permute-start(f32[8,128]{1,0:T(8,128)S(1)} %add_add_fusion.1), channel_id=1, source_target_pairs={{3,0},{0,1},{1,2},{2,3},{7,4},{4,5},{5,6},{6,7},{11,8},{8,9},{9,10... | collective-permute-start | bytes 12296 | tf_op jit(solution)/shard_map/ppermute | solution.py:40
  195.6 5.1 %collective-permute-start.48 = (f32[8,128]{1,0:T(8,128)S(1)}, f32[8,128]{1,0:T(8,128)S(1)}, u32[]{:S(2)}, u32[]{:S(2)}) collective-permute-start(f32[8,128]{1,0:T(8,128)S(1)} %add_add_fusion.1), channel_id=1, source_target_pairs={{2,0},{3,1},{0,2},{1,3},{6,4},{7,5},{4,6},{5,7},{10,8},{11,9},{8,1... | collective-permute-start | bytes 12296 | tf_op jit(solution)/shard_map/ppermute | solution.py:40
  199.1 3.6 %collective-permute-start.47 = (f32[8,128]{1,0:T(8,128)S(1)}, f32[8,128]{1,0:T(8,128)S(1)}, u32[]{:S(2)}, u32[]{:S(2)}) collective-permute-start(f32[8,128]{1,0:T(8,128)S(1)} %add_add_fusion.1), channel_id=1, source_target_pairs={{1,0},{2,1},{3,2},{0,3},{5,4},{6,5},{7,6},{4,7},{9,8},{10,9},{11,1... | collective-permute-start | bytes 12296 | tf_op jit(solution)/shard_map/ppermute | solution.py:40
  (33 other events, 181.9 us)
Sparse Core Ops, SparseCore 0:
  10.7 64.5 all-gather.1
